TPU v7x, 32 devices: a whole 2x2x4 slice. The times are simulated.
32 devices in a mesh: gx: 8 (over z, y), gy: 2 (over x), depth: 2 (over core).
Axes of the slice: x: 2, y: 2, z: 4, core: 2. Of those that a mesh axis runs over, the one named last changes fastest.
Arguments:
- adjoint: float32 [19, 24, 32, 1024], P(None, 'depth', 'gy', 'gx'), may hold values from -6 to 6
- momentum: float32 [3, 24, 32, 1024], P(None, 'depth', 'gy', 'gx'), may hold values from -4 to 4
- design: float32 [32, 1024], P('gy', 'gx'), may hold values from 0 to 1
- solid_mask: int32 [24, 32, 1024], P('depth', 'gy', 'gx'), may hold values 0 or 1
- port_label: int32 [24, 32, 1024], P('depth', 'gy', 'gx'), may hold values from 0 to 2, as said below
Outputs:
- new_adjoint: float32 [19, 24, 32, 1024], P(None, 'depth', 'gy', 'gx')
- sensitivity: float32 [32, 1024], P('gy', 'gx')
Inputs may be any that keep to these rules, and one draw needn't show every extreme that they name: `solid_mask`: 1 marks a solid cell, 0 a fluid one. `port_label`: 0 marks an ordinary cell, 1 an inlet cell, 2 an outlet cell.
All inputs are finite; a program needn't handle non-finite values. No bound on the sum of `solid_mask` on one device may be relied on, other than what follows from the above.
Results may differ from a plain program's by a relative error of at most 0.00012.
Values sent between devices are 32-bit elements; how exact they have to be, the bound alone decides.
No kernel may reach another device: no remote copies, remote signals or barrier semaphores. Data moves between devices by JAX's collectives and lax.ppermute only.
A program may use at most 128 MiB of HBM per device.

v0:
```python
import functools
import math

import jax
import jax.numpy as jnp
from jax import lax
from jax.experimental import pallas as pl
from jax.experimental.pallas import tpu as pltpu
from jax.sharding import PartitionSpec as P

velocities = (
    (0, 0, 0),
    (1, 0, 0),
    (-1, 0, 0),
    (0, 1, 0),
    (0, -1, 0),
    (0, 0, 1),
    (0, 0, -1),
    (1, 1, 0),
    (-1, -1, 0),
    (1, -1, 0),
    (-1, 1, 0),
    (1, 0, 1),
    (-1, 0, -1),
    (1, 0, -1),
    (-1, 0, 1),
    (0, 1, 1),
    (0, -1, -1),
    (0, 1, -1),
    (0, -1, 1),
)
lattice_weights = (1.0 / 3.0,) + (1.0 / 18.0,) * 6 + (1.0 / 36.0,) * 12
opposite = (0, 2, 1, 4, 3, 6, 5, 8, 7, 10, 9, 12, 11, 14, 13, 16, 15, 18, 17)
relax_rate = 1.25
damp_top = 0.5
cone_radius = 5.0
filter_reach = 4
wide = filter_reach + 1
tile = 8
level_group = 3
laterals = ((0, 0), (1, 0), (-1, 0), (0, 1), (0, -1))
lateral_weights = (1.0 / 18.0,) + (1.0 / 36.0,) * 4
kinds = len(laterals) + 3


def crossing(axis, sign):
    others = [other for other in range(3) if other != axis]
    return [
        next(
            number
            for number, vector in enumerate(velocities)
            if vector[axis] == sign and (vector[others[0]], vector[others[1]]) == lateral
        )
        for lateral in laterals
    ]


def cone(offset_y, offset_x):
    return max(0.0, cone_radius - math.sqrt(offset_y * offset_y + offset_x * offset_x))


def pairings(axis):
    return range(min(lax.axis_size(axis) - 1, 2))


def swap(array, axis, pairing):
    pairs = []
    for low in range(pairing, lax.axis_size(axis) - 1, 2):
        pairs += [(low, low + 1), (low + 1, low)]
    return lax.ppermute(array, axis, pairs)


def partner_after(axis, pairing):
    return lax.rem(lax.axis_index(axis) + pairing, 2) == 0


def pick(flag, yes, no):
    return lax.select(flag, yes, no)


def turn(array, shift, axis):
    shift = shift % array.shape[axis]
    return array if shift == 0 else pltpu.roll(array, shift, axis)


def lanes_of(shape):
    return lax.broadcasted_iota(jnp.int32, shape, len(shape) - 1)


def rows_of(shape):
    return lax.broadcasted_iota(jnp.int32, shape, len(shape) - 2)


def halves(axis, arrays):
    before, after = 0.0, 0.0
    for pairing, array in enumerate(arrays):
        flag = partner_after(axis, pairing)
        none = jnp.zeros_like(array)
        before = before + pick(flag, none, array)
        after = after + pick(flag, array, none)
    return (before, after)


def depth_plane(adjoint, halo, number, level):
    levels = adjoint.shape[1]
    if 0 <= level < levels:
        return adjoint[number, level]
    sign = 1 if level == levels else -1
    side = halo[1] if sign > 0 else halo[0]
    return side[crossing(2, sign).index(number)]


def gain_of(momentum, scale, solid, port, level):
    kept = (solid[level] == 0) & (port[level] != 1)
    factor = jnp.where(kept, scale, 0.0)
    return [factor * momentum[part, level] for part in range(3)]


def along_x(plane, step):
    lane = lanes_of(plane.shape)
    edge = plane.shape[-1] - 1 if step > 0 else 0
    return jnp.where(lane == edge, 0.0, turn(plane, -step, 1))


def along_y(plane, step):
    row = rows_of(plane.shape)
    edge = plane.shape[-2] - 1 if step > 0 else 0
    return jnp.where(row == edge, 0.0, turn(plane, -step, 0))


def own_moment(take):
    heavy, light = (1.0 / 18.0, 1.0 / 36.0)
    p = {
        number: take(number, vector[2]) for number, vector in enumerate(velocities) if number != 0
    }
    for number in (7, 8, 9, 10):
        p[number] = along_y(p[number], velocities[number][1])
    right_x = along_x(heavy * p[1] + light * ((p[7] + p[9]) + (p[11] + p[13])), 1)
    left_x = along_x(heavy * p[2] + light * ((p[8] + p[10]) + (p[12] + p[14])), -1)
    right_y = along_x(light * (p[7] - p[9]), 1)
    left_y = along_x(light * (p[10] - p[8]), -1)
    right_z = along_x(light * (p[11] - p[13]), 1)
    left_z = along_x(light * (p[14] - p[12]), -1)
    lower_y = along_y(heavy * p[3] + light * (p[15] + p[17]), 1)
    upper_y = along_y(heavy * p[4] + light * (p[16] + p[18]), -1)
    lower_z = along_y(light * (p[15] - p[17]), 1)
    upper_z = along_y(light * (p[18] - p[16]), -1)
    moment_x = right_x - left_x
    moment_y = (lower_y - upper_y) + (right_y + left_y)
    moment_z = heavy * (p[5] - p[6]) + ((right_z + left_z) + (lower_z + upper_z))
    return (moment_x, moment_y, moment_z)


def groups_of(levels):
    return [(low, min(low + level_group, levels)) for low in range(0, levels, level_group)]


def face_kernel(z_pairs, adjoint, *refs):
    outs, sems = (refs[:z_pairs], refs[z_pairs])
    levels = adjoint.shape[1]
    copies = []
    for pairing in range(z_pairs):
        after = partner_after("depth", pairing)
        level = jnp.where(after, levels - 1, 0)
        for kind, numbers in enumerate(zip(crossing(2, -1), crossing(2, 1))):
            number = jnp.where(after, numbers[0], numbers[1])
            copies.append(
                pltpu.make_async_copy(
                    adjoint.at[number, level],
                    outs[pairing].at[kind],
                    sems.at[pairing * len(laterals) + kind],
                )
            )
    for copy in copies:
        copy.start()
    for copy in copies:
        copy.wait()


def pack_kernel(counts, adjoint_far, momentum_far, design_far, solid_far, port_far, *refs):
    x_pairs, y_pairs = counts
    adjoint, design, solid, port, refs = (*refs[:4], refs[4:])
    x_out, refs = (refs[:x_pairs], refs[x_pairs:])
    y_out, refs = (refs[:y_pairs], refs[y_pairs:])
    own_out, edge_gain, momentum, sems = refs
    levels, rows, lanes = adjoint.shape[1:]
    slots = lanes // tile
    assert levels + 3 <= slots
    pairs = [(design_far, design), (solid_far, solid), (port_far, port), (momentum_far, momentum)]
    pairs += [
        (adjoint_far.at[:, low:high], adjoint.at[:, low:high]) for low, high in groups_of(levels)
    ]
    copies = [
        pltpu.make_async_copy(far, near, sems.at[place]) for place, (far, near) in enumerate(pairs)
    ]
    for copy in copies:
        copy.start()
    for copy in copies[:4]:
        copy.wait()
    loads = dict(zip([low for low, high in groups_of(levels)], copies[4:]))
    scale = 6.0 * damp_top / ((1.0 + design[...]) * (1.0 + design[...]))
    lane = lanes_of((rows, lanes))
    for pairing in range(y_pairs):
        y_out[pairing][...] = jnp.zeros(y_out[pairing].shape, jnp.float32)
    total = jnp.zeros((rows, lanes), jnp.float32)
    first_pack = jnp.zeros((rows, lanes), jnp.float32)
    last_pack = jnp.zeros((rows, lanes), jnp.float32)
    loads.pop(0).wait()
    for level in range(levels):
        if level + 1 in loads:
            loads.pop(level + 1).wait()
        gain = gain_of(momentum, scale, solid, port, level)
        moment = own_moment(
            lambda number, step: adjoint[number, level + step]
            if 0 <= level + step < levels
            else jnp.zeros((rows, lanes), jnp.float32)
        )
        total = total + (gain[0] * moment[0] + gain[1] * moment[1] + gain[2] * moment[2])
        for side, edge in enumerate((0, levels - 1)):
            if level == edge:
                for part in range(3):
                    edge_gain[side, part] = gain[part]
        for pairing in range(y_pairs):
            after = partner_after("gy", pairing)
            for part in range(3):
                place = (len(laterals) + part) * slots + level
                y_out[pairing][place : place + 1, :] = pick(
                    after, gain[part][rows - 1 : rows], gain[part][0:1]
                )
        for kind in range(kinds):
            if kind < len(laterals):
                first = adjoint[crossing(0, 1)[kind], level]
                last = adjoint[crossing(0, -1)[kind], level]
            else:
                first = last = gain[kind - len(laterals)]
            place = level * tile + kind
            first_pack = jnp.where(lane == place, turn(first, place, 1), first_pack)
            last_pack = jnp.where(lane == place, turn(last, place + 1, 1), last_pack)
    for pairing in range(y_pairs):
        after = partner_after("gy", pairing)
        for kind in range(len(laterals)):
            last, first = (crossing(1, -1)[kind], crossing(1, 1)[kind])
            y_out[pairing][kind * slots : kind * slots + levels, :] = pick(
                after, adjoint[last, :, rows - 1, :], adjoint[first, :, 0, :]
            )
    own_out[...] = total
    for pairing in range(x_pairs):
        x_out[pairing][...] = pick(partner_after("gx", pairing), last_pack, first_pack)


def depth_kernel(counts, levels, *refs):
    x_pairs, y_pairs, z_pairs = counts
    z_got, refs = (refs[:z_pairs], refs[z_pairs:])
    x_pack, refs = (refs[:x_pairs], refs[x_pairs:])
    y_pack, refs = (refs[:y_pairs], refs[y_pairs:])
    own, edge_gain, refs = (*refs[:2], refs[2:])
    x_out, refs = (refs[:x_pairs], refs[x_pairs:])
    y_out, own_out = (refs[:y_pairs], refs[y_pairs])
    rows, lanes = own.shape
    slots = lanes // tile
    halo = halves("depth", [got[...] for got in z_got])
    lane = lanes_of((rows, lanes))
    total = own[...]
    if z_pairs:
        for side, sign in enumerate((-1, 1)):
            gain = [edge_gain[side, part] for part in range(3)]
            for kind, (step_x_, step_y_) in enumerate(laterals):
                plane = halo[side][kind]
                pull = sign * gain[2]
                if step_x_ != 0:
                    plane = along_x(plane, step_x_)
                    pull = pull + step_x_ * gain[0]
                if step_y_ != 0:
                    plane = along_y(plane, step_y_)
                    pull = pull + step_y_ * gain[1]
                total = total + lateral_weights[kind] * plane * pull
    own_out[...] = total
    beyond = ((3, levels, 1), (4, -1, 0))
    for pairing in range(y_pairs):
        after = partner_after("gy", pairing)
        y_out[pairing][...] = y_pack[pairing][...]
        if z_pairs:
            for kind, level, side in beyond:
                planes = crossing(2, 1 if side else -1)
                last, first = (
                    halo[side][planes.index(crossing(1, sign)[kind])] for sign in (-1, 1)
                )
                place = kind * slots + level % slots
                y_out[pairing][place : place + 1, :] = pick(
                    after, last[rows - 1 : rows], first[0:1]
                )
    spare = (levels + 1) * tile
    chosen = (lane >= spare) & (lane < spare + filter_reach)
    packs = []
    for edge_shift, sign, sums in ((0, 1, 0), (1, -1, filter_reach)):
        pack = jnp.where(chosen, turn(total, spare + sums, 1), 0.0)
        if z_pairs:
            for kind, level, side in beyond:
                planes = crossing(2, 1 if side else -1)
                plane = halo[side][planes.index(crossing(0, sign)[kind])]
                place = (level % slots) * tile + kind
                pack = jnp.where(lane == place, turn(plane, place + edge_shift, 1), pack)
        packs.append(pack)
    ends = [jnp.zeros((slots, lanes), jnp.float32) for side in range(2)]
    lane = lanes_of((slots, lanes))
    for pairing in range(y_pairs):
        for kind in range(kinds):
            line = y_out[pairing][kind * slots : (kind + 1) * slots, :]
            place = (pairing * kinds + kind) * wide
            chosen = (lane >= place) & (lane < place + wide)
            ends[0] = jnp.where(chosen, turn(line, place, 1), ends[0])
            ends[1] = jnp.where(chosen, turn(line, place + wide, 1), ends[1])
    for pairing in range(x_pairs):
        after = partner_after("gx", pairing)
        x_out[pairing][0:rows, :] = x_pack[pairing][...] + pick(after, packs[1], packs[0])
        x_out[pairing][rows : rows + slots, :] = pick(after, ends[1], ends[0])


def cross_x(levels, faces, gains, sign):
    rows, lanes = faces.shape
    lane, row = (lanes_of(faces.shape), rows_of(faces.shape))
    gain = [turn(gains, -(len(laterals) + part), 1) for part in range(3)]
    total = jnp.zeros_like(faces)
    for kind, (step_y, step_z) in enumerate(laterals):
        source = turn(faces, -kind - tile * step_z, 1)
        pull = sign * gain[0]
        if step_y != 0:
            edge = rows - 1 if step_y > 0 else 0
            source = jnp.where(row == edge, 0.0, turn(source, -step_y, 0))
            pull = pull + step_y * gain[1]
        if step_z != 0:
            pull = pull + step_z * gain[2]
        total = total + lateral_weights[kind] * source * pull
    used = (lane % tile == 0) & (lane < tile * levels)
    return jnp.sum(jnp.where(used, total, 0.0), axis=1, keepdims=True)


def middle_kernel(counts, levels, *refs):
    x_pairs, y_pairs = counts
    x_got, refs = (refs[:x_pairs], refs[x_pairs:])
    x_sent, refs = (refs[:x_pairs], refs[x_pairs:])
    y_rows, refs = (refs[:y_pairs], refs[y_pairs:])
    own, refs = (refs[0], refs[1:])
    y_out, middle = (refs[:y_pairs], refs[y_pairs])
    rows, lanes = own.shape
    slots = lanes // tile
    lane = lanes_of((rows, lanes))
    main = own[...]
    side = jnp.zeros((rows, lanes), jnp.float32)
    spare = (levels + 1) * tile
    for pairing in range(x_pairs):
        after = partner_after("gx", pairing)
        sign = jnp.where(after, 1.0, -1.0)
        got, sent = (x_got[pairing][0:rows, :], x_sent[pairing][0:rows, :])
        there = cross_x(levels, sent, got, -sign)
        here = cross_x(levels, got, sent, sign)
        right = jnp.where(lane < filter_reach, turn(got, -spare, 1), 0.0)
        right = right + jnp.where(lane == 0, there, 0.0)
        left = jnp.where(lane >= lanes - filter_reach, turn(got, -spare - filter_reach, 1), 0.0)
        left = left + jnp.where(lane == lanes - 1, there, 0.0)
        side = side + pick(after, right, left)
        edge = jnp.where(after, lanes - 1, 0)
        main = main + jnp.where(lane == edge, here, 0.0)
    middle[0] = main
    middle[1] = side
    left_ends, right_ends = halves("gx", [got[rows : rows + slots, :] for got in x_got])
    lane = lanes_of((slots, lanes))
    size = kinds * wide
    for pairing in range(y_pairs):
        after = partner_after("gy", pairing)
        out = y_out[pairing]
        out[0 : kinds * slots, :] = y_rows[pairing][...]
        ends = jnp.zeros((slots, lanes), jnp.float32)
        if x_pairs:
            ends = jnp.where(lane < size, turn(left_ends, -pairing * size, 1), ends)
            ends = jnp.where(
                (lane >= size) & (lane < 2 * size), turn(right_ends, size - pairing * size, 1), ends
            )
        base = kinds * slots
        out[base : base + slots, :] = ends
        for number, part in enumerate((main, side)):
            place = base + slots + number * tile
            out[place : place + tile, :] = pick(after, part[rows - tile :], part[0:tile])


def spread_ends(ends, kind, lanes):
    lane = lanes_of(ends.shape)
    size = kinds * wide
    right = jnp.where(lane < wide, turn(ends, -size - kind * wide, 1), 0.0)
    return jnp.where(lane >= lanes - wide, turn(ends, -wide - kind * wide, 1), right)


def step_x(main, side, step):
    if step == 0:
        return (main, side)
    lane = lanes_of(main.shape)
    edge = lane == (main.shape[-1] - 1 if step > 0 else 0)
    main, side = (turn(main, -step, 1), turn(side, -step, 1))
    return (jnp.where(edge, side, main), jnp.where(edge, main, side))


def cross_y(faces, gains, sign):
    total_main, total_side = (0.0, 0.0)
    for kind, (lateral_x, lateral_z) in enumerate(laterals):
        main, side = step_x(*faces[kind], lateral_x)
        main, side = (turn(main, -lateral_z, 0), turn(side, -lateral_z, 0))
        pull_main, pull_side = (sign * gains[1][0], sign * gains[1][1])
        if lateral_x != 0:
            pull_main = pull_main + lateral_x * gains[0][0]
            pull_side = pull_side + lateral_x * gains[0][1]
        if lateral_z != 0:
            pull_main = pull_main + lateral_z * gains[2][0]
            pull_side = pull_side + lateral_z * gains[2][1]
        total_main = total_main + lateral_weights[kind] * main * pull_main
        total_side = total_side + lateral_weights[kind] * side * pull_side
    return (
        jnp.sum(total_main, axis=0, keepdims=True),
        jnp.sum(total_side, axis=0, keepdims=True),
    )


def face_lines(packed, slots, lanes):
    ends = packed[kinds * slots : (kinds + 1) * slots, :]
    return [
        (packed[kind * slots : (kind + 1) * slots, :], spread_ends(ends, kind, lanes))
        for kind in range(kinds)
    ]


def extend_kernel(y_pairs, *refs):
    y_got, refs = (refs[:y_pairs], refs[y_pairs:])
    y_sent, refs = (refs[:y_pairs], refs[y_pairs:])
    middle, out = refs
    rows, lanes = middle.shape[1:]
    slots = lanes // tile
    row, row_tile = (rows_of((rows, lanes)), rows_of((tile, lanes)))
    own = [middle[0], middle[1]]
    before = [jnp.zeros((tile, lanes), jnp.float32) for part in range(2)]
    after = [jnp.zeros((tile, lanes), jnp.float32) for part in range(2)]
    for pairing in range(y_pairs):
        flag = partner_after("gy", pairing)
        sign = jnp.where(flag, 1.0, -1.0)
        got = face_lines(y_got[pairing], slots, lanes)
        sent = face_lines(y_sent[pairing], slots, lanes)
        there = cross_y(sent[:5], got[5:], -sign)
        here = cross_y(got[:5], sent[5:], sign)
        edge_here = jnp.where(flag, rows - 1, 0)
        edge_there = jnp.where(flag, 0, tile - 1)
        for part in range(2):
            place = (kinds + 1) * slots + part * tile
            sums = y_got[pairing][place : place + tile, :]
            sums = sums + jnp.where(row_tile == edge_there, there[part], 0.0)
            none = jnp.zeros_like(sums)
            before[part] = before[part] + pick(flag, none, sums)
            after[part] = after[part] + pick(flag, sums, none)
            own[part] = own[part] + jnp.where(row == edge_here, here[part], 0.0)
    for part in range(2):
        out[part, 0:tile, :] = before[part]
        out[part, tile : tile + rows, :] = own[part]
        out[part, tile + rows :, :] = after[part]


def cone_sum(main, side, rows):
    lanes = main.shape[-1]
    lane = lanes_of(main.shape)
    pairs = [main]
    for offset in range(1, filter_reach + 1):
        up = jnp.where(lane < lanes - offset, turn(main, -offset, 1), turn(side, -offset, 1))
        down = jnp.where(lane >= offset, turn(main, offset, 1), turn(side, offset, 1))
        pairs.append(up + down)
    total = jnp.zeros((rows, lanes), jnp.float32)
    for offset in range(filter_reach + 1):
        weighted = jnp.zeros_like(main)
        for distance, pair in enumerate(pairs):
            weight = cone(offset, distance)
            if weight > 0.0:
                weighted = weighted + weight * pair
        for step in sorted({offset, -offset}):
            total = total + turn(weighted, -step, 0)[tile : tile + rows]
    return total


def filter_kernel(mine, other, norm, out):
    rows = out.shape[0]
    out[...] = cone_sum(mine[0] + other[0], mine[1] + other[1], rows) * norm[...]


def filter_norm(rows, lanes):
    shape = (rows + 2 * tile, lanes)
    row, lane = (rows_of(shape), lanes_of(shape))
    place = lax.axis_index("gy") * rows + row - tile
    inside = jnp.where((place >= 0) & (place < lax.axis_size("gy") * rows), 1.0, 0.0)
    left = (lax.axis_index("gx") > 0).astype(jnp.float32)
    right = (lax.axis_index("gx") < lax.axis_size("gx") - 1).astype(jnp.float32)
    beside = inside * jnp.where(lane < lanes // 2, right, left)
    return 1.0 / cone_sum(inside, beside, rows)


def collide_kernel(counts, adjoint, design, solid, port, *refs):
    x_pairs, y_pairs, z_pairs = counts
    x_got, refs = (refs[:x_pairs], refs[x_pairs:])
    z_got, refs = (refs[:z_pairs], refs[z_pairs:])
    far, edge_rows, norm, out, sems = refs
    levels, rows, lanes = adjoint.shape[1:]
    slots = lanes // tile
    halo_z = halves("depth", [got[...] for got in z_got])
    halo_x = halves("gx", [got[0:rows, :] for got in x_got])
    damping = damp_top * (1.0 - design[...]) / (1.0 + design[...])
    rate = 3.0 * (relax_rate - damping)
    lane = lanes_of((rows, lanes))
    copies = []
    for level in range(levels):
        pulled = []
        for number, (step_x_, step_y_, step_z_) in enumerate(velocities):
            source = level + step_z_
            if z_pairs or 0 <= source < levels:
                plane = depth_plane(adjoint, halo_z, number, source)
            else:
                plane = jnp.zeros((rows, lanes), jnp.float32)
            if step_x_ != 0:
                edge = lanes - 1 if step_x_ > 0 else 0
                column = 0.0
                if x_pairs:
                    kind = crossing(0, step_x_).index(number)
                    place = (source % slots) * tile + kind
                    column = turn(halo_x[1 if step_x_ > 0 else 0], edge - place, 1)
                plane = jnp.where(lane == edge, column, turn(plane, -step_x_, 1))
            if step_y_ != 0:
                plane = along_y(plane, step_y_)
            pulled.append(plane)
        zeroth, moment = sums_of(pulled)
        base = relax_rate * zeroth
        scaled = [rate * part for part in moment]
        fluid, inlet = (solid[level] == 0, port[level] == 1)
        outflow = jnp.where(port[level] == 2, 1.0, 0.0)
        for number, vector in enumerate(velocities):
            updated = base + (1.0 - relax_rate) * pulled[number]
            if number > 0:
                updated = updated + along(vector, scaled)
            updated = jnp.where(fluid, updated, pulled[opposite[number]])
            updated = jnp.where(inlet, 0.0, updated)
            if vector[0] != 0:
                updated = updated + vector[0] * outflow
            out[number, level] = updated
        for place, (low, high) in enumerate(groups_of(levels)):
            if level == high - 1:
                copy = pltpu.make_async_copy(
                    out.at[:, low:high], far.at[:, low:high], sems.at[place]
                )
                copy.start()
                copies.append(copy)
    for pairing in range(y_pairs):
        after = partner_after("gy", pairing)
        for number in range(len(velocities)):
            edge_rows[pairing, number] = pick(after, out[number, :, rows - 1, :], out[number, :, 0, :])
    norm[...] = filter_norm(rows, lanes)
    for copy in copies:
        copy.wait()


def along(vector, parts):
    total = 0.0
    for component, part in zip(vector, parts):
        if component > 0:
            total = total + part
        if component < 0:
            total = total - part
    return total


def sums_of(pulled):
    heavy, light = (lattice_weights[1], lattice_weights[7])
    both, gap = ({}, {})
    for number in range(1, len(velocities), 2):
        both[number] = pulled[number] + pulled[number + 1]
        gap[number] = pulled[number] - pulled[number + 1]
    zeroth = lattice_weights[0] * pulled[0] + heavy * ((both[1] + both[3]) + both[5])
    zeroth = zeroth + light * (((both[7] + both[9]) + (both[11] + both[13])) + (both[15] + both[17]))
    moment = (
        heavy * gap[1] + light * ((gap[7] + gap[9]) + (gap[11] + gap[13])),
        heavy * gap[3] + light * ((gap[7] - gap[9]) + (gap[15] + gap[17])),
        heavy * gap[5] + light * ((gap[11] - gap[13]) + (gap[15] - gap[17])),
    )
    return (zeroth, moment)


def row_kernel(y_pairs, new, edge_rows, design, solid, port, *refs):
    y_got, (far, out, sems) = (refs[:y_pairs], refs[y_pairs:])
    levels, rows, lanes = solid.shape
    slots = lanes // tile
    copies = []
    for pairing in range(y_pairs):
        after = partner_after("gy", pairing)
        sign = jnp.where(after, 1.0, -1.0)
        got = y_got[pairing]
        ends = got[kinds * slots : (kinds + 1) * slots, :]
        extra, moment = ({}, [0.0, 0.0, 0.0])
        zeroth = 0.0
        for kind, (lateral_x, lateral_z) in enumerate(laterals):
            line = got[kind * slots : (kind + 1) * slots, :]
            if lateral_x != 0:
                line = step_x(line, spread_ends(ends, kind, lanes), lateral_x)[0]
            line = turn(line, -lateral_z, 0)[0:levels]
            none = jnp.zeros_like(line)
            extra[crossing(1, 1)[kind]] = pick(after, line, none)
            extra[crossing(1, -1)[kind]] = pick(after, none, line)
            weighted = lateral_weights[kind] * line
            zeroth = zeroth + weighted
            moment[0] = moment[0] + lateral_x * weighted
            moment[2] = moment[2] + lateral_z * weighted
        moment[1] = sign * zeroth
        edge_design = pick(after, design[rows - 1 : rows, :], design[0:1, :])
        damping = damp_top * (1.0 - edge_design) / (1.0 + edge_design)
        rate = 3.0 * (relax_rate - damping)
        fluid = pick(after, solid[:, rows - 1, :], solid[:, 0, :]) == 0
        inlet = pick(after, port[:, rows - 1, :], port[:, 0, :]) == 1
        scaled = [rate * part for part in moment]
        base = relax_rate * zeroth
        for number, vector in enumerate(velocities):
            added = base
            if number > 0:
                added = added + along(vector, scaled)
            if number in extra:
                added = added + (1.0 - relax_rate) * extra[number]
            added = jnp.where(fluid, added, extra.get(opposite[number], 0.0))
            added = jnp.where(inlet, 0.0, added)
            out[pairing, number, :, 0, :] = edge_rows[pairing, number] + added
        place = jnp.where(after, rows - 1, 0)
        copies.append(
            pltpu.make_async_copy(
                out.at[pairing, :, :, 0:1, :], far.at[:, :, pl.ds(place, 1), :], sems.at[pairing]
            )
        )
        copies[-1].start()
    for copy in copies:
        copy.wait()


def local_call(body, name, operands, out_shapes, scratch=(), far=(), far_out=(), aliases=None):
    near_spec = pl.BlockSpec(memory_space=pltpu.VMEM)
    far_spec = pl.BlockSpec(memory_space=pltpu.HBM)
    shapes = [
        shape if isinstance(shape, jax.ShapeDtypeStruct) else jax.ShapeDtypeStruct(shape, jnp.float32)
        for shape in out_shapes
    ]
    return pl.pallas_call(
        body,
        out_shape=shapes,
        in_specs=[far_spec if place in far else near_spec for place in range(len(operands))],
        out_specs=[far_spec if place in far_out else near_spec for place in range(len(shapes))],
        scratch_shapes=list(scratch),
        input_output_aliases=aliases or {},
        compiler_params=pltpu.CompilerParams(vmem_limit_bytes=16 * 1024 * 1024),
        name=name,
    )(*operands)


def on_device(adjoint, momentum, design, solid_mask, port_label):
    levels, rows, lanes = adjoint.shape[1:]
    slots = lanes // tile
    groups = len(groups_of(levels))
    x_pairs, y_pairs, z_pairs = (len(pairings(axis)) for axis in ("gx", "gy", "depth"))
    z_got = []
    if z_pairs:
        faces = local_call(
            functools.partial(face_kernel, z_pairs),
            "depth_faces",
            [adjoint],
            [(len(laterals), rows, lanes)] * z_pairs,
            scratch=[pltpu.SemaphoreType.DMA((z_pairs * len(laterals),))],
            far=(0,),
        )
        z_got = [swap(face, "depth", pairing) for pairing, face in enumerate(faces)]
    packed = local_call(
        functools.partial(pack_kernel, (x_pairs, y_pairs)),
        "pack_faces",
        [adjoint, momentum, design, solid_mask, port_label],
        [adjoint.shape, (rows, lanes)]
        + [jax.ShapeDtypeStruct(solid_mask.shape, jnp.int32)] * 2
        + [(rows, lanes)] * x_pairs
        + [(kinds * slots, lanes)] * y_pairs
        + [(rows, lanes), (2, 3, rows, lanes)],
        scratch=[
            pltpu.VMEM(momentum.shape, jnp.float32),
            pltpu.SemaphoreType.DMA((4 + groups,)),
        ],
        far=range(5),
    )
    adjoint, design, solid_mask, port_label = packed[:4]
    packed = packed[4:]
    filled = local_call(
        functools.partial(depth_kernel, (x_pairs, y_pairs, z_pairs), levels),
        "add_z_faces",
        [*z_got, *packed],
        [(rows + slots, lanes)] * x_pairs + [(kinds * slots, lanes)] * y_pairs + [(rows, lanes)],
    )
    x_sent, y_rows, own = (
        filled[:x_pairs],
        filled[x_pairs : x_pairs + y_pairs],
        filled[x_pairs + y_pairs],
    )
    x_got = [swap(x_sent[pairing], "gx", pairing) for pairing in range(x_pairs)]
    merged = local_call(
        functools.partial(middle_kernel, (x_pairs, y_pairs), levels),
        "add_x_faces",
        [*x_got, *x_sent, *y_rows, own],
        [((kinds + 1) * slots + 2 * tile, lanes)] * y_pairs + [(2, rows, lanes)],
    )
    y_sent, middle = (merged[:y_pairs], merged[y_pairs])
    y_got = [swap(y_sent[pairing], "gy", pairing) for pairing in range(y_pairs)]
    (column,) = local_call(
        functools.partial(extend_kernel, y_pairs),
        "add_y_faces",
        [*y_got, *y_sent, middle],
        [(2, rows + 2 * tile, lanes)],
    )
    if z_pairs == 1:
        other = swap(column, "depth", 0)
    else:
        other = lax.psum(column, "depth") - column
    new_adjoint, edge_rows, norm = local_call(
        functools.partial(collide_kernel, (x_pairs, y_pairs, z_pairs)),
        "collide",
        [adjoint, design, solid_mask, port_label, *x_got, *z_got],
        [adjoint.shape, (max(y_pairs, 1), len(velocities), levels, lanes), (rows, lanes)],
        scratch=[pltpu.VMEM(adjoint.shape, jnp.float32), pltpu.SemaphoreType.DMA((groups,))],
        far_out=(0,),
    )
    if y_pairs:
        (new_adjoint,) = local_call(
            functools.partial(row_kernel, y_pairs),
            "add_y_rows",
            [new_adjoint, edge_rows, design, solid_mask, port_label, *y_got],
            [adjoint.shape],
            scratch=[
                pltpu.VMEM((y_pairs, len(velocities), levels, tile, lanes), jnp.float32),
                pltpu.SemaphoreType.DMA((y_pairs,)),
            ],
            far=(0,),
            far_out=(0,),
            aliases={0: 0},
        )
    (sensitivity,) = local_call(
        filter_kernel, "cone_filter", [column, other, norm], [(rows, lanes)]
    )
    return (new_adjoint, sensitivity)


def solution(mesh):
    in_specs = (
        P(None, "depth", "gy", "gx"),
        P(None, "depth", "gy", "gx"),
        P("gy", "gx"),
        P("depth", "gy", "gx"),
        P("depth", "gy", "gx"),
    )
    out_specs = (P(None, "depth", "gy", "gx"), P("gy", "gx"))
    return jax.shard_map(
        on_device, mesh=mesh, in_specs=in_specs, out_specs=out_specs, check_vma=False
    )
```

profile of v0, /device:TPU:9, one launch (start us, length us, event | category | flops | bytes accessed | tf_op | source)
XLA Modules:
  0.0 22.0 jit_solution(9725498542447985483)
XLA Ops:
  0.6 0.0 copy-start
  0.6 1.5 %copy-done = f32[19,12,16,128]{3,2,1,0:T(8,128)S(1)} copy-done((f32[19,12,16,128]{3,2,1,0:T(8,128)S(1)}, f32[19,12,16,128]{3,2,1,0:T(8,128)}, u32[]{:S(2)}) %copy-start) | copy-done | bytes 1867800
  2.1 0.0 copy-start.1
  2.1 0.0 copy-start.2
  2.1 0.0 copy-start.3
  2.1 0.0 copy-start.4
  2.2 0.1 depth_faces.1
  2.3 0.7 %collective-permute-start = (f32[5,16,128]{2,1,0:T(8,128)S(1)}, f32[5,16,128]{2,1,0:T(8,128)S(1)}, u32[]{:S(2)}, u32[]{:S(2)}) collective-permute-start(f32[5,16,128]{2,1,0:T(8,128)S(1)} %depth_faces.1), channel_id=1, source_target_pairs={{0,1},{1,0},{2,3},{3,2},{4,5},{5,4},{6,7},{7,6},{8,9},{9,8},{10,11... | collective-permute-start | bytes 122888 | tf_op jit(solution)/shard_map/ppermute | solution.py:70
  3.0 0.1 copy-done.1
  3.1 0.0 copy-done.2
  3.1 0.0 copy-done.3
  3.2 0.0 copy-done.4
  3.2 1.4 %pack_faces.1 = (f32[19,12,16,128]{3,2,1,0:T(8,128)S(1)}, f32[16,128]{1,0:T(8,128)S(1)}, s32[12,16,128]{2,1,0:T(8,128)S(1)}, s32[12,16,128]{2,1,0:T(8,128)S(1)},...) custom-call(f32[19,12,16,128]{3,2,1,0:T(8,128)S(1)} %copy-done, ...), custom_call_target="tpu_custom_call" | custom-call | tf_op jit(solution)/shard_map/pack_faces/pallas_call | solution.py:646
  4.6 0.0 collective-permute-done.refs_0_.refs_2_
  4.6 0.2 add_z_faces.1
  4.8 1.3 %collective-permute-start.1 = (f32[32,128]{1,0:T(8,128)S(1)}, f32[32,128]{1,0:T(8,128)S(1)}, u32[]{:S(2)}, u32[]{:S(2)}) collective-permute-start(f32[32,128]{1,0:T(8,128)S(1)} %get-tuple-element.29.refs_2_), channel_id=1, source_target_pairs={{0,4},{4,0},{8,12},{12,8},{16,20},{20,16},{24,28},{28,24},{1,5},{5... | collective-permute-start | bytes 49160 | tf_op jit(solution)/shard_map/ppermute | solution.py:70
  6.1 1.9 %collective-permute-start.2 = (f32[32,128]{1,0:T(8,128)S(1)}, f32[32,128]{1,0:T(8,128)S(1)}, u32[]{:S(2)}, u32[]{:S(2)}) collective-permute-start(f32[32,128]{1,0:T(8,128)S(1)} %get-tuple-element.30.refs_3_), channel_id=1, source_target_pairs={{4,8},{8,4},{12,16},{16,12},{20,24},{24,20},{5,9},{9,5},{13,17},{1... | collective-permute-start | bytes 49160 | tf_op jit(solution)/shard_map/ppermute | solution.py:70
  8.0 0.0 collective-permute-done.1.refs_0_
  8.0 3.4 %collective-permute-done.2.refs_1_ = f32[32,128]{1,0:T(8,128)S(1)} collective-permute-done((f32[32,128]{1,0:T(8,128)S(1)}, f32[32,128]{1,0:T(8,128)S(1)}, u32[]{:S(2)}, u32[]{:S(2)}) %collective-permute-start.2) | collective-permute-done | bytes 16416 | tf_op jit(solution)/shard_map/ppermute | solution.py:70
  11.4 0.3 %add_x_faces.1 = (f32[160,128]{1,0:T(8,128)S(1)}, f32[2,16,128]{2,1,0:T(8,128)S(1)}) custom-call(f32[32,128]{1,0:T(8,128)S(1)} %collective-permute-done.1.refs_0_, f32[32,128]{1,0:T(8,128)S(1)} %collective-permute-done.2.refs_1_, f32[32,128]{1,0:T(8,128)S(1)} %get-tuple-element.29.refs_2_, f32[32,128]{1,0:T(8,128)S(1)} %get-tuple-element.30.refs_3_, ...), custom_call_target="tpu_custom_call" | custom-call | tf_op jit(solution)/shard_map/add_x_faces/pallas_call | solution.py:646
  11.7 1.3 %collective-permute-start.3 = (f32[160,128]{1,0:T(8,128)S(1)}, f32[160,128]{1,0:T(8,128)S(1)}, u32[]{:S(2)}, u32[]{:S(2)}) collective-permute-start(f32[160,128]{1,0:T(8,128)S(1)} %get-tuple-element.35.refs_1_), channel_id=1, source_target_pairs={{0,2},{2,0},{1,3},{3,1},{4,6},{6,4},{5,7},{7,5},{8,10},{10,8},{9,1... | collective-permute-start | bytes 245768 | tf_op jit(solution)/shard_map/ppermute | solution.py:70
  13.0 2.1 %collective-permute-done.3.refs_0_ = f32[160,128]{1,0:T(8,128)S(1)} collective-permute-done((f32[160,128]{1,0:T(8,128)S(1)}, f32[160,128]{1,0:T(8,128)S(1)}, u32[]{:S(2)}, u32[]{:S(2)}) %collective-permute-start.3) | collective-permute-done | bytes 81952 | tf_op jit(solution)/shard_map/ppermute | solution.py:70
  15.1 0.2 add_y_faces.1.mine
  15.2 3.3 %collective-permute-start.4 = (f32[2,32,128]{2,1,0:T(8,128)S(1)}, f32[2,32,128]{2,1,0:T(8,128)S(1)}, u32[]{:S(2)}, u32[]{:S(2)}) collective-permute-start(f32[2,32,128]{2,1,0:T(8,128)S(1)} %add_y_faces.1.mine), channel_id=1, source_target_pairs={{0,1},{1,0},{2,3},{3,2},{4,5},{5,4},{6,7},{7,6},{8,9},{9,8},{10,11... | collective-permute-start | bytes 98312 | tf_op jit(solution)/shard_map/ppermute | solution.py:70
  18.5 1.8 %collide.1 = (f32[19,12,16,128]{3,2,1,0:T(8,128)}, f32[1,19,12,128]{3,2,1,0:T(8,128)S(1)}, f32[16,128]{1,0:T(8,128)S(1)}) custom-call(f32[19,12,16,128]{3,2,1,0:T(8,128)S(1)} %get-tuple-element.20.adjoint, f32[16,128]{1,0:T(8,128)S(1)} %get-tuple-element.21.design, s32[12,16,128]{2,1,0:T(8,128)S(1)} %get-tuple-element.22.solid, ...), custom_call_target="tpu_custom_call" | custom-call | tf_op jit(solution)/shard_map/collide/pallas_call | solution.py:646
  20.4 0.9 %add_y_rows.1 = f32[19,12,16,128]{3,2,1,0:T(8,128)} custom-call(f32[19,12,16,128]{3,2,1,0:T(8,128)} %get-tuple-element.31.new, f32[1,19,12,128]{3,2,1,0:T(8,128)S(1)} %get-tuple-element.32.edge_rows, f32[16,128]{1,0:T(8,128)S(1)} %get-tuple-element.21.design, s32[12,16,128]{2,1,0:T(8,128)S(1)} %get-tuple-element.22.solid, ...), custom_call_target="tpu_custom_call", output_to_operand_aliasing={{}: (0, {})} | custom-call | tf_op jit(solution)/shard_map/add_y_rows/pallas_call | solution.py:646
  21.3 0.0 collective-permute-done.4.other
  21.3 0.7 %cone_filter.1 = f32[16,128]{1,0:T(8,128)} custom-call(f32[2,32,128]{2,1,0:T(8,128)S(1)} %add_y_faces.1.mine, f32[2,32,128]{2,1,0:T(8,128)S(1)} %collective-permute-done.4.other, f32[16,128]{1,0:T(8,128)S(1)} %get-tuple-element.37.norm), custom_call_target="tpu_custom_call" | custom-call | tf_op jit(solution)/shard_map/cone_filter/pallas_call | solution.py:646
Async XLA Ops:
  0.6 1.5 %copy-start = (f32[19,12,16,128]{3,2,1,0:T(8,128)S(1)}, f32[19,12,16,128]{3,2,1,0:T(8,128)}, u32[]{:S(2)}) copy-start(f32[19,12,16,128]{3,2,1,0:T(8,128)} %adjoint.1) | copy-start | bytes 5603332
  2.1 1.0 %copy-start.1 = (f32[3,12,16,128]{3,2,1,0:T(8,128)S(1)}, f32[3,12,16,128]{3,2,1,0:T(8,128)}, u32[]{:S(2)}) copy-start(f32[3,12,16,128]{3,2,1,0:T(8,128)} %momentum_far.1) | copy-start | bytes 884740
  2.1 1.0 %copy-start.2 = (s32[12,16,128]{2,1,0:T(8,128)S(1)}, s32[12,16,128]{2,1,0:T(8,128)}, u32[]{:S(2)}) copy-start(s32[12,16,128]{2,1,0:T(8,128)} %solid_far.1) | copy-start | bytes 294916
  2.1 1.0 %copy-start.3 = (s32[12,16,128]{2,1,0:T(8,128)S(1)}, s32[12,16,128]{2,1,0:T(8,128)}, u32[]{:S(2)}) copy-start(s32[12,16,128]{2,1,0:T(8,128)} %port_far.1) | copy-start | bytes 294916
  2.1 1.0 %copy-start.4 = (f32[16,128]{1,0:T(8,128)S(1)}, f32[16,128]{1,0:T(8,128)}, u32[]{:S(2)}) copy-start(f32[16,128]{1,0:T(8,128)} %design_far.1) | copy-start | bytes 24580
  2.3 2.3 %collective-permute-start = (f32[5,16,128]{2,1,0:T(8,128)S(1)}, f32[5,16,128]{2,1,0:T(8,128)S(1)}, u32[]{:S(2)}, u32[]{:S(2)}) collective-permute-start(f32[5,16,128]{2,1,0:T(8,128)S(1)} %depth_faces.1), channel_id=1, source_target_pairs={{0,1},{1,0},{2,3},{3,2},{4,5},{5,4},{6,7},{7,6},{8,9},{9,8},{10,11... | collective-permute-start | bytes 122888 | tf_op jit(solution)/shard_map/ppermute | solution.py:70
  4.8 3.2 %collective-permute-start.1 = (f32[32,128]{1,0:T(8,128)S(1)}, f32[32,128]{1,0:T(8,128)S(1)}, u32[]{:S(2)}, u32[]{:S(2)}) collective-permute-start(f32[32,128]{1,0:T(8,128)S(1)} %get-tuple-element.29.refs_2_), channel_id=1, source_target_pairs={{0,4},{4,0},{8,12},{12,8},{16,20},{20,16},{24,28},{28,24},{1,5},{5... | collective-permute-start | bytes 49160 | tf_op jit(solution)/shard_map/ppermute | solution.py:70
  6.1 5.4 %collective-permute-start.2 = (f32[32,128]{1,0:T(8,128)S(1)}, f32[32,128]{1,0:T(8,128)S(1)}, u32[]{:S(2)}, u32[]{:S(2)}) collective-permute-start(f32[32,128]{1,0:T(8,128)S(1)} %get-tuple-element.30.refs_3_), channel_id=1, source_target_pairs={{4,8},{8,4},{12,16},{16,12},{20,24},{24,20},{5,9},{9,5},{13,17},{1... | collective-permute-start | bytes 49160 | tf_op jit(solution)/shard_map/ppermute | solution.py:70
  11.7 3.4 %collective-permute-start.3 = (f32[160,128]{1,0:T(8,128)S(1)}, f32[160,128]{1,0:T(8,128)S(1)}, u32[]{:S(2)}, u32[]{:S(2)}) collective-permute-start(f32[160,128]{1,0:T(8,128)S(1)} %get-tuple-element.35.refs_1_), channel_id=1, source_target_pairs={{0,2},{2,0},{1,3},{3,1},{4,6},{6,4},{5,7},{7,5},{8,10},{10,8},{9,1... | collective-permute-start | bytes 245768 | tf_op jit(solution)/shard_map/ppermute | solution.py:70
  15.2 6.0 %collective-permute-start.4 = (f32[2,32,128]{2,1,0:T(8,128)S(1)}, f32[2,32,128]{2,1,0:T(8,128)S(1)}, u32[]{:S(2)}, u32[]{:S(2)}) collective-permute-start(f32[2,32,128]{2,1,0:T(8,128)S(1)} %add_y_faces.1.mine), channel_id=1, source_target_pairs={{0,1},{1,0},{2,3},{3,2},{4,5},{5,4},{6,7},{7,6},{8,9},{9,8},{10,11... | collective-permute-start | bytes 98312 | tf_op jit(solution)/shard_map/ppermute | solution.py:70
where the time goes:
time: 22.2 us; the launch traced here: 22 us
  starting transfers between devices  8.52 us (38%)
  Pallas kernels  5.6 us (25%)
  waiting for transfers between devices  5.53 us (25%)
  local copies, waits for them, and re-layouts  1.65 us (7%)
  between operations  0.72 us (3%)
    ppermute x5, starting transfers between devices, swap(): return lax.ppermute(array, axis, pairs)  8.52 us
    pallas_call x8, Pallas kernels, local_call(): pl.pallas_call(body, out_shape=shapes, in_specs=[far_spec if place in far...  5.6 us
    ppermute x5, waiting for transfers between devices, swap(): return lax.ppermute(array, axis, pairs)  5.53 us
    unnamed x10, local copies, waits for them, and re-layouts  1.65 us
  transfers between devices with their start and end apart: 5, of which 2 were waited for; matrix products, arithmetic and copies ran while one was open for 0% of the time, Pallas kernels for 19%

commit v1 on v0

--- a/solution.py
+++ b/solution.py
@@ -64,14 +64,35 @@
 
 
 def swap(array, axis, pairing):
+    size, cores = (lax.axis_size(axis), lax.axis_size("depth"))
     pairs = []
-    for low in range(pairing, lax.axis_size(axis) - 1, 2):
+    for low in range(pairing, size - 1, 2):
         pairs += [(low, low + 1), (low + 1, low)]
-    return lax.ppermute(array, axis, pairs)
+    alone = [place for place in range(size) if place not in dict(pairs)]
+    if axis == "depth" or cores % 2 != 0 or not alone:
+        return lax.ppermute(array, axis, pairs)
+    full = [(a * cores + core, b * cores + core) for a, b in pairs for core in range(cores)]
+    for place in alone:
+        full += [(place * cores + core, place * cores + (core ^ 1)) for core in range(cores)]
+    return lax.ppermute(array, (axis, "depth"), full)
 
 
 def partner_after(axis, pairing):
     return lax.rem(lax.axis_index(axis) + pairing, 2) == 0
+
+
+def partners(axis, pairing):
+    place, after = (lax.axis_index(axis), partner_after(axis, pairing))
+    none_before, none_after = (place == 0, place == lax.axis_size(axis) - 1)
+    return (
+        jnp.logical_not(jnp.logical_or(after, none_before)),
+        jnp.logical_and(after, jnp.logical_not(none_after)),
+    )
+
+
+def present(axis, pairing, array):
+    before, after = partners(axis, pairing)
+    return pick(jnp.logical_or(before, after), array, jnp.zeros_like(array))
 
 
 def pick(flag, yes, no):
@@ -94,10 +115,10 @@
 def halves(axis, arrays):
     before, after = 0.0, 0.0
     for pairing, array in enumerate(arrays):
-        flag = partner_after(axis, pairing)
+        is_before, is_after = partners(axis, pairing)
         none = jnp.zeros_like(array)
-        before = before + pick(flag, none, array)
-        after = after + pick(flag, array, none)
+        before = before + pick(is_before, array, none)
+        after = after + pick(is_after, array, none)
     return (before, after)
 
 
@@ -155,49 +176,35 @@
     return [(low, min(low + level_group, levels)) for low in range(0, levels, level_group)]
 
 
-def face_kernel(z_pairs, adjoint, *refs):
-    outs, sems = (refs[:z_pairs], refs[z_pairs])
+def load_kernel(z_pairs, adjoint, momentum, design, solid, port, *refs):
+    near, outs, sems = (refs[:4], refs[4 : 4 + z_pairs], refs[4 + z_pairs])
     levels = adjoint.shape[1]
-    copies = []
+    pairs = []
     for pairing in range(z_pairs):
         after = partner_after("depth", pairing)
         level = jnp.where(after, levels - 1, 0)
         for kind, numbers in enumerate(zip(crossing(2, -1), crossing(2, 1))):
             number = jnp.where(after, numbers[0], numbers[1])
-            copies.append(
-                pltpu.make_async_copy(
-                    adjoint.at[number, level],
-                    outs[pairing].at[kind],
-                    sems.at[pairing * len(laterals) + kind],
-                )
-            )
+            pairs.append((adjoint.at[number, level], outs[pairing].at[kind]))
+    pairs += zip((momentum, design, solid, port), near)
+    copies = [
+        pltpu.make_async_copy(source, target, sems.at[place])
+        for place, (source, target) in enumerate(pairs)
+    ]
     for copy in copies:
         copy.start()
     for copy in copies:
         copy.wait()
 
 
-def pack_kernel(counts, adjoint_far, momentum_far, design_far, solid_far, port_far, *refs):
+def pack_kernel(counts, adjoint, momentum, design, solid, port, *refs):
     x_pairs, y_pairs = counts
-    adjoint, design, solid, port, refs = (*refs[:4], refs[4:])
     x_out, refs = (refs[:x_pairs], refs[x_pairs:])
     y_out, refs = (refs[:y_pairs], refs[y_pairs:])
-    own_out, edge_gain, momentum, sems = refs
+    own_out, edge_gain = refs
     levels, rows, lanes = adjoint.shape[1:]
     slots = lanes // tile
     assert levels + 3 <= slots
-    pairs = [(design_far, design), (solid_far, solid), (port_far, port), (momentum_far, momentum)]
-    pairs += [
-        (adjoint_far.at[:, low:high], adjoint.at[:, low:high]) for low, high in groups_of(levels)
-    ]
-    copies = [
-        pltpu.make_async_copy(far, near, sems.at[place]) for place, (far, near) in enumerate(pairs)
-    ]
-    for copy in copies:
-        copy.start()
-    for copy in copies[:4]:
-        copy.wait()
-    loads = dict(zip([low for low, high in groups_of(levels)], copies[4:]))
     scale = 6.0 * damp_top / ((1.0 + design[...]) * (1.0 + design[...]))
     lane = lanes_of((rows, lanes))
     for pairing in range(y_pairs):
@@ -205,10 +212,7 @@
     total = jnp.zeros((rows, lanes), jnp.float32)
     first_pack = jnp.zeros((rows, lanes), jnp.float32)
     last_pack = jnp.zeros((rows, lanes), jnp.float32)
-    loads.pop(0).wait()
     for level in range(levels):
-        if level + 1 in loads:
-            loads.pop(level + 1).wait()
         gain = gain_of(momentum, scale, solid, port, level)
         moment = own_moment(
             lambda number, step: adjoint[number, level + step]
@@ -337,9 +341,8 @@
 
 def middle_kernel(counts, levels, *refs):
     x_pairs, y_pairs = counts
-    x_got, refs = (refs[:x_pairs], refs[x_pairs:])
+    x_got, refs = (refs[:x_pairs][::-1], refs[x_pairs:])
     x_sent, refs = (refs[:x_pairs], refs[x_pairs:])
-    y_rows, refs = (refs[:y_pairs], refs[y_pairs:])
     own, refs = (refs[0], refs[1:])
     y_out, middle = (refs[:y_pairs], refs[y_pairs])
     rows, lanes = own.shape
@@ -351,7 +354,8 @@
     for pairing in range(x_pairs):
         after = partner_after("gx", pairing)
         sign = jnp.where(after, 1.0, -1.0)
-        got, sent = (x_got[pairing][0:rows, :], x_sent[pairing][0:rows, :])
+        got = present("gx", pairing, x_got[pairing][0:rows, :])
+        sent = x_sent[pairing][0:rows, :]
         there = cross_x(levels, sent, got, -sign)
         here = cross_x(levels, got, sent, sign)
         right = jnp.where(lane < filter_reach, turn(got, -spare, 1), 0.0)
@@ -369,17 +373,15 @@
     for pairing in range(y_pairs):
         after = partner_after("gy", pairing)
         out = y_out[pairing]
-        out[0 : kinds * slots, :] = y_rows[pairing][...]
         ends = jnp.zeros((slots, lanes), jnp.float32)
         if x_pairs:
             ends = jnp.where(lane < size, turn(left_ends, -pairing * size, 1), ends)
             ends = jnp.where(
                 (lane >= size) & (lane < 2 * size), turn(right_ends, size - pairing * size, 1), ends
             )
-        base = kinds * slots
-        out[base : base + slots, :] = ends
+        out[0:slots, :] = ends
         for number, part in enumerate((main, side)):
-            place = base + slots + number * tile
+            place = slots + number * tile
             out[place : place + tile, :] = pick(after, part[rows - tile :], part[0:tile])
 
 
@@ -419,10 +421,9 @@
     )
 
 
-def face_lines(packed, slots, lanes):
-    ends = packed[kinds * slots : (kinds + 1) * slots, :]
+def face_lines(lines, ends, slots, lanes):
     return [
-        (packed[kind * slots : (kind + 1) * slots, :], spread_ends(ends, kind, lanes))
+        (lines[kind * slots : (kind + 1) * slots], spread_ends(ends[0:slots], kind, lanes))
         for kind in range(kinds)
     ]
 
@@ -430,7 +431,9 @@
 def extend_kernel(y_pairs, *refs):
     y_got, refs = (refs[:y_pairs], refs[y_pairs:])
     y_sent, refs = (refs[:y_pairs], refs[y_pairs:])
-    middle, out = refs
+    ends_got, refs = (refs[:y_pairs], refs[y_pairs:])
+    ends_sent, refs = (refs[:y_pairs], refs[y_pairs:])
+    middle, norm, out = refs
     rows, lanes = middle.shape[1:]
     slots = lanes // tile
     row, row_tile = (rows_of((rows, lanes)), rows_of((tile, lanes)))
@@ -440,15 +443,17 @@
     for pairing in range(y_pairs):
         flag = partner_after("gy", pairing)
         sign = jnp.where(flag, 1.0, -1.0)
-        got = face_lines(y_got[pairing], slots, lanes)
-        sent = face_lines(y_sent[pairing], slots, lanes)
+        got_lines = present("gy", pairing, y_got[pairing][...])
+        got_ends = present("gy", pairing, ends_got[pairing][...])
+        got = face_lines(got_lines, got_ends, slots, lanes)
+        sent = face_lines(y_sent[pairing][...], ends_sent[pairing][...], slots, lanes)
         there = cross_y(sent[:5], got[5:], -sign)
         here = cross_y(got[:5], sent[5:], sign)
         edge_here = jnp.where(flag, rows - 1, 0)
         edge_there = jnp.where(flag, 0, tile - 1)
         for part in range(2):
-            place = (kinds + 1) * slots + part * tile
-            sums = y_got[pairing][place : place + tile, :]
+            place = slots + part * tile
+            sums = got_ends[place : place + tile]
             sums = sums + jnp.where(row_tile == edge_there, there[part], 0.0)
             none = jnp.zeros_like(sums)
             before[part] = before[part] + pick(flag, none, sums)
@@ -498,7 +503,7 @@
 
 def collide_kernel(counts, adjoint, design, solid, port, *refs):
     x_pairs, y_pairs, z_pairs = counts
-    x_got, refs = (refs[:x_pairs], refs[x_pairs:])
+    x_got, refs = (refs[:x_pairs][::-1], refs[x_pairs:])
     z_got, refs = (refs[:z_pairs], refs[z_pairs:])
     far, edge_rows, norm, out, sems = refs
     levels, rows, lanes = adjoint.shape[1:]
@@ -585,19 +590,20 @@
 
 
 def row_kernel(y_pairs, new, edge_rows, design, solid, port, *refs):
-    y_got, (far, out, sems) = (refs[:y_pairs], refs[y_pairs:])
+    y_got, refs = (refs[:y_pairs], refs[y_pairs:])
+    ends_got, (far, out, sems) = (refs[:y_pairs], refs[y_pairs:])
     levels, rows, lanes = solid.shape
     slots = lanes // tile
     copies = []
     for pairing in range(y_pairs):
         after = partner_after("gy", pairing)
         sign = jnp.where(after, 1.0, -1.0)
-        got = y_got[pairing]
-        ends = got[kinds * slots : (kinds + 1) * slots, :]
+        got = present("gy", pairing, y_got[pairing][...])
+        ends = present("gy", pairing, ends_got[pairing][0:slots, :])
         extra, moment = ({}, [0.0, 0.0, 0.0])
         zeroth = 0.0
         for kind, (lateral_x, lateral_z) in enumerate(laterals):
-            line = got[kind * slots : (kind + 1) * slots, :]
+            line = got[kind * slots : (kind + 1) * slots]
             if lateral_x != 0:
                 line = step_x(line, spread_ends(ends, kind, lanes), lateral_x)[0]
             line = turn(line, -lateral_z, 0)[0:levels]
@@ -636,11 +642,11 @@
         copy.wait()
 
 
-def local_call(body, name, operands, out_shapes, scratch=(), far=(), far_out=(), aliases=None):
+def local_call(body, name, operands, out_shapes, scratch=(), far=(), far_out=(), aliases=None, room=16):
     near_spec = pl.BlockSpec(memory_space=pltpu.VMEM)
     far_spec = pl.BlockSpec(memory_space=pltpu.HBM)
     shapes = [
-        shape if isinstance(shape, jax.ShapeDtypeStruct) else jax.ShapeDtypeStruct(shape, jnp.float32)
+        jax.ShapeDtypeStruct(shape, jnp.float32) if isinstance(shape, tuple) else shape
         for shape in out_shapes
     ]
     return pl.pallas_call(
@@ -650,7 +656,7 @@
         out_specs=[far_spec if place in far_out else near_spec for place in range(len(shapes))],
         scratch_shapes=list(scratch),
         input_output_aliases=aliases or {},
-        compiler_params=pltpu.CompilerParams(vmem_limit_bytes=16 * 1024 * 1024),
+        compiler_params=pltpu.CompilerParams(vmem_limit_bytes=room * 1024 * 1024),
         name=name,
     )(*operands)
 
@@ -660,77 +666,79 @@
     slots = lanes // tile
     groups = len(groups_of(levels))
     x_pairs, y_pairs, z_pairs = (len(pairings(axis)) for axis in ("gx", "gy", "depth"))
-    z_got = []
-    if z_pairs:
-        faces = local_call(
-            functools.partial(face_kernel, z_pairs),
-            "depth_faces",
-            [adjoint],
-            [(len(laterals), rows, lanes)] * z_pairs,
-            scratch=[pltpu.SemaphoreType.DMA((z_pairs * len(laterals),))],
-            far=(0,),
-        )
-        z_got = [swap(face, "depth", pairing) for pairing, face in enumerate(faces)]
+    loaded = local_call(
+        functools.partial(load_kernel, z_pairs),
+        "load",
+        [
+            pltpu.with_memory_space_constraint(array, pltpu.HBM)
+            for array in (adjoint, momentum, design, solid_mask, port_label)
+        ],
+        [
+            pltpu.VMEM(momentum.shape, jnp.float32),
+            pltpu.VMEM(design.shape, jnp.float32),
+            pltpu.VMEM(solid_mask.shape, jnp.int32),
+            pltpu.VMEM(port_label.shape, jnp.int32),
+        ]
+        + [pltpu.VMEM((len(laterals), rows, lanes), jnp.float32)] * z_pairs,
+        scratch=[pltpu.SemaphoreType.DMA((z_pairs * len(laterals) + 4,))],
+        far=range(5),
+    )
+    momentum, design, solid_mask, port_label = loaded[:4]
+    z_got = [swap(face, "depth", pairing) for pairing, face in enumerate(loaded[4:])]
     packed = local_call(
         functools.partial(pack_kernel, (x_pairs, y_pairs)),
         "pack_faces",
         [adjoint, momentum, design, solid_mask, port_label],
-        [adjoint.shape, (rows, lanes)]
-        + [jax.ShapeDtypeStruct(solid_mask.shape, jnp.int32)] * 2
-        + [(rows, lanes)] * x_pairs
+        [(rows, lanes)] * x_pairs
         + [(kinds * slots, lanes)] * y_pairs
         + [(rows, lanes), (2, 3, rows, lanes)],
-        scratch=[
-            pltpu.VMEM(momentum.shape, jnp.float32),
-            pltpu.SemaphoreType.DMA((4 + groups,)),
-        ],
-        far=range(5),
-    )
-    adjoint, design, solid_mask, port_label = packed[:4]
-    packed = packed[4:]
+    )
     filled = local_call(
         functools.partial(depth_kernel, (x_pairs, y_pairs, z_pairs), levels),
         "add_z_faces",
         [*z_got, *packed],
         [(rows + slots, lanes)] * x_pairs + [(kinds * slots, lanes)] * y_pairs + [(rows, lanes)],
     )
-    x_sent, y_rows, own = (
+    x_sent, y_sent, own = (
         filled[:x_pairs],
         filled[x_pairs : x_pairs + y_pairs],
         filled[x_pairs + y_pairs],
     )
-    x_got = [swap(x_sent[pairing], "gx", pairing) for pairing in range(x_pairs)]
+    y_got = [swap(y_sent[pairing], "gy", pairing) for pairing in range(y_pairs)]
+    x_got = [None] * x_pairs
+    for pairing in reversed(range(x_pairs)):
+        x_got[pairing] = swap(x_sent[pairing], "gx", pairing)
     merged = local_call(
         functools.partial(middle_kernel, (x_pairs, y_pairs), levels),
         "add_x_faces",
-        [*x_got, *x_sent, *y_rows, own],
-        [((kinds + 1) * slots + 2 * tile, lanes)] * y_pairs + [(2, rows, lanes)],
-    )
-    y_sent, middle = (merged[:y_pairs], merged[y_pairs])
-    y_got = [swap(y_sent[pairing], "gy", pairing) for pairing in range(y_pairs)]
+        [*x_got[::-1], *x_sent, own],
+        [(slots + 2 * tile, lanes)] * y_pairs + [(2, rows, lanes)],
+    )
+    ends_sent, middle = (merged[:y_pairs], merged[y_pairs])
+    ends_got = [swap(ends_sent[pairing], "gy", pairing) for pairing in range(y_pairs)]
+    new_adjoint, edge_rows, norm = local_call(
+        functools.partial(collide_kernel, (x_pairs, y_pairs, z_pairs)),
+        "collide",
+        [adjoint, design, solid_mask, port_label, *x_got[::-1], *z_got],
+        [adjoint.shape, (max(y_pairs, 1), len(velocities), levels, lanes), (rows, lanes)],
+        scratch=[pltpu.VMEM(adjoint.shape, jnp.float32), pltpu.SemaphoreType.DMA((groups,))],
+        far_out=(0,),
+    )
     (column,) = local_call(
         functools.partial(extend_kernel, y_pairs),
         "add_y_faces",
-        [*y_got, *y_sent, middle],
+        [*y_got, *y_sent, *ends_got, *ends_sent, middle, norm],
         [(2, rows + 2 * tile, lanes)],
     )
     if z_pairs == 1:
         other = swap(column, "depth", 0)
     else:
         other = lax.psum(column, "depth") - column
-    new_adjoint, edge_rows, norm = local_call(
-        functools.partial(collide_kernel, (x_pairs, y_pairs, z_pairs)),
-        "collide",
-        [adjoint, design, solid_mask, port_label, *x_got, *z_got],
-        [adjoint.shape, (max(y_pairs, 1), len(velocities), levels, lanes), (rows, lanes)],
-        scratch=[pltpu.VMEM(adjoint.shape, jnp.float32), pltpu.SemaphoreType.DMA((groups,))],
-        far_out=(0,),
-    )
     if y_pairs:
         (new_adjoint,) = local_call(
             functools.partial(row_kernel, y_pairs),
             "add_y_rows",
-            [new_adjoint, edge_rows, design, solid_mask, port_label, *y_got],
+            [new_adjoint, edge_rows, design, solid_mask, port_label, *y_got, *ends_got],
             [adjoint.shape],
             scratch=[
                 pltpu.VMEM((y_pairs, len(velocities), levels, tile, lanes), jnp.float32),

time: 22.2 us -> 17.6 us (0.79)
  the two profiles are of different devices: /device:TPU:9 before, /device:TPU:0 now
where the time goes in v1:
time: 17.6 us; the launch traced here: 17.4 us
  starting transfers between devices  7.11 us (40%)
  Pallas kernels  5.98 us (34%)
  waiting for transfers between devices  3.63 us (21%)
  between operations  0.69 us (4%)
    ppermute x5, starting transfers between devices, swap(): return lax.ppermute(array, axis, pairs)  7.1 us
    pallas_call x8, Pallas kernels, local_call(): pl.pallas_call(body, out_shape=shapes, in_specs=[far_spec if place in far...  5.98 us
    ppermute x5, waiting for transfers between devices, swap(): return lax.ppermute(array, axis, pairs)  3.63 us
  transfers between devices with their start and end apart: 6, of which 4 were waited for; matrix products, arithmetic and copies ran while one was open for 0% of the time, Pallas kernels for 20%

profile of v1, /device:TPU:0, one launch (start us, length us, event | category | flops | bytes accessed | tf_op | source)
XLA Modules:
  0.0 17.4 jit_solution(15578281035087103921)
XLA Ops:
  0.6 0.0 copy-start
  0.6 1.4 %load.1 = (f32[3,12,16,128]{3,2,1,0:T(8,128)S(1)}, f32[16,128]{1,0:T(8,128)S(1)}, s32[12,16,128]{2,1,0:T(8,128)S(1)}, s32[12,16,128]{2,1,0:T(8,128)S(1)}, f32[5,16,128]{2,1,0:T(8,128)S(1)}) custom-call(f32[19,12,16,128]{3,2,1,0:T(8,128)} %adjoint.5, f32[3,12,16,128]{3,2,1,0:T(8,128)} %momentum.1, f32[16,128]{1,0:T(8,128)} %design.1, s32[12,16,128]{2,1,0:T(8,128)} %solid.1, ...), custom_call_target="tpu_custom_call" | custom-call | tf_op jit(solution)/shard_map/load/pallas_call | solution.py:652
  2.0 0.5 %collective-permute-start = (f32[5,16,128]{2,1,0:T(8,128)S(1)}, f32[5,16,128]{2,1,0:T(8,128)S(1)}, u32[]{:S(2)}, u32[]{:S(2)}) collective-permute-start(f32[5,16,128]{2,1,0:T(8,128)S(1)} %get-tuple-element.24), channel_id=1, source_target_pairs={{0,1},{1,0},{2,3},{3,2},{4,5},{5,4},{6,7},{7,6},{8,9},{9,8},{10,11... | collective-permute-start | bytes 122888 | tf_op jit(solution)/shard_map/ppermute | solution.py:73
  2.5 0.0 copy-done
  2.5 0.6 %pack_faces.1 = (f32[16,128]{1,0:T(8,128)S(1)}, f32[16,128]{1,0:T(8,128)S(1)}, f32[128,128]{1,0:T(8,128)S(1)}, f32[16,128]{1,0:T(8,128)S(1)}, f32[2,3,16,128]{3,2,1,0:T(8,128)S(1)}) custom-call(f32[19,12,16,128]{3,2,1,0:T(8,128)S(1)} %copy-done, f32[3,12,16,128]{3,2,1,0:T(8,128)S(1)} %get-tuple-element.25.momentum, f32[16,128]{1,0:T(8,128)S(1)} %get-tuple-element.21.design, ...), custom_call_target="tpu_custom_call" | custom-call | tf_op jit(solution)/shard_map/pack_faces/pallas_call | solution.py:652
  3.2 0.2 %collective-permute-done.refs_0_.refs_2_ = f32[5,16,128]{2,1,0:T(8,128)S(1)} collective-permute-done((f32[5,16,128]{2,1,0:T(8,128)S(1)}, f32[5,16,128]{2,1,0:T(8,128)S(1)}, u32[]{:S(2)}, u32[]{:S(2)}) %collective-permute-start) | collective-permute-done | bytes 40992 | tf_op jit(solution)/shard_map/ppermute | solution.py:73
  3.4 0.2 add_z_faces.1
  3.5 2.9 %collective-permute-start.3 = (f32[128,128]{1,0:T(8,128)S(1)}, f32[128,128]{1,0:T(8,128)S(1)}, u32[]{:S(2)}, u32[]{:S(2)}) collective-permute-start(f32[128,128]{1,0:T(8,128)S(1)} %get-tuple-element.35.refs_1_), channel_id=1, source_target_pairs={{0,2},{2,0},{1,3},{3,1},{4,6},{6,4},{5,7},{7,5},{8,10},{10,8},{9,1... | collective-permute-start | bytes 196616 | tf_op jit(solution)/shard_map/ppermute | solution.py:73
  6.4 0.0 collective-permute-start.1
  6.4 3.0 %collective-permute-start.2 = (f32[32,128]{1,0:T(8,128)S(1)}, f32[32,128]{1,0:T(8,128)S(1)}, u32[]{:S(2)}, u32[]{:S(2)}) collective-permute-start(f32[32,128]{1,0:T(8,128)S(1)} %get-tuple-element.32.refs_2_), channel_id=1, source_target_pairs={{0,4},{4,0},{8,12},{12,8},{16,20},{20,16},{24,28},{28,24},{1,5},{5... | collective-permute-start | bytes 49160 | tf_op jit(solution)/shard_map/ppermute | solution.py:73
  9.5 0.0 collective-permute-done.1.refs_0_
  9.5 1.7 %collective-permute-done.2.refs_1_ = f32[32,128]{1,0:T(8,128)S(1)} collective-permute-done((f32[32,128]{1,0:T(8,128)S(1)}, f32[32,128]{1,0:T(8,128)S(1)}, u32[]{:S(2)}, u32[]{:S(2)}) %collective-permute-start.2) | collective-permute-done | bytes 16416 | tf_op jit(solution)/shard_map/ppermute | solution.py:73
  11.2 0.2 %add_x_faces.1 = (f32[32,128]{1,0:T(8,128)S(1)}, f32[2,16,128]{2,1,0:T(8,128)S(1)}) custom-call(f32[32,128]{1,0:T(8,128)S(1)} %collective-permute-done.1.refs_0_, f32[32,128]{1,0:T(8,128)S(1)} %collective-permute-done.2.refs_1_, f32[32,128]{1,0:T(8,128)S(1)} %get-tuple-element.32.refs_2_, f32[32,128]{1,0:T(8,128)S(1)} %get-tuple-element.31.refs_3_, ...), custom_call_target="tpu_custom_call" | custom-call | tf_op jit(solution)/shard_map/add_x_faces/pallas_call | solution.py:652
  11.4 0.6 %collective-permute-start.4 = (f32[32,128]{1,0:T(8,128)S(1)}, f32[32,128]{1,0:T(8,128)S(1)}, u32[]{:S(2)}, u32[]{:S(2)}) collective-permute-start(f32[32,128]{1,0:T(8,128)S(1)} %get-tuple-element.37.refs_3_), channel_id=1, source_target_pairs={{0,2},{2,0},{1,3},{3,1},{4,6},{6,4},{5,7},{7,5},{8,10},{10,8},{9,1... | collective-permute-start | bytes 49160 | tf_op jit(solution)/shard_map/ppermute | solution.py:73
  12.0 1.8 %collide.1 = (f32[19,12,16,128]{3,2,1,0:T(8,128)}, f32[1,19,12,128]{3,2,1,0:T(8,128)S(1)}, f32[16,128]{1,0:T(8,128)S(1)}) custom-call(f32[19,12,16,128]{3,2,1,0:T(8,128)S(1)} %copy-done, f32[16,128]{1,0:T(8,128)S(1)} %get-tuple-element.21.design, s32[12,16,128]{2,1,0:T(8,128)S(1)} %get-tuple-element.22.solid, s32[12,16,128]{2,1,0:T(8,128)S(1)} %get-tuple-element.23.port, ...), custom_call_target="tpu_custom_call" | custom-call | tf_op jit(solution)/shard_map/collide/pallas_call | solution.py:652
  13.8 1.4 %collective-permute-done.4.refs_1_.refs_2_ = f32[32,128]{1,0:T(8,128)S(1)} collective-permute-done((f32[32,128]{1,0:T(8,128)S(1)}, f32[32,128]{1,0:T(8,128)S(1)}, u32[]{:S(2)}, u32[]{:S(2)}) %collective-permute-start.4) | collective-permute-done | bytes 16416 | tf_op jit(solution)/shard_map/ppermute | solution.py:73
  15.2 0.0 collective-permute-done.3.refs_0_
  15.2 0.2 %add_y_faces.1.mine = f32[2,32,128]{2,1,0:T(8,128)S(1)} custom-call(f32[128,128]{1,0:T(8,128)S(1)} %collective-permute-done.3.refs_0_, f32[128,128]{1,0:T(8,128)S(1)} %get-tuple-element.35.refs_1_, f32[32,128]{1,0:T(8,128)S(1)} %collective-permute-done.4.refs_1_.refs_2_, f32[32,128]{1,0:T(8,128)S(1)} %get-tuple-element.37.refs_3_, ...), custom_call_target="tpu_custom_call" | custom-call | tf_op jit(solution)/shard_map/add_y_faces/pallas_call | solution.py:652
  15.4 0.1 collective-permute-start.5
  15.5 0.9 %add_y_rows.1 = f32[19,12,16,128]{3,2,1,0:T(8,128)} custom-call(f32[19,12,16,128]{3,2,1,0:T(8,128)} %get-tuple-element.33.new, f32[1,19,12,128]{3,2,1,0:T(8,128)S(1)} %get-tuple-element.34.edge_rows, f32[16,128]{1,0:T(8,128)S(1)} %get-tuple-element.21.design, s32[12,16,128]{2,1,0:T(8,128)S(1)} %get-tuple-element.22.solid, ...), custom_call_target="tpu_custom_call", output_to_operand_aliasing={{}: (0, {})} | custom-call | tf_op jit(solution)/shard_map/add_y_rows/pallas_call | solution.py:652
  16.4 0.3 %collective-permute-done.5.other = f32[2,32,128]{2,1,0:T(8,128)S(1)} collective-permute-done((f32[2,32,128]{2,1,0:T(8,128)S(1)}, f32[2,32,128]{2,1,0:T(8,128)S(1)}, u32[]{:S(2)}, u32[]{:S(2)}) %collective-permute-start.5) | collective-permute-done | bytes 32800 | tf_op jit(solution)/shard_map/ppermute | solution.py:73
  16.7 0.7 %cone_filter.1 = f32[16,128]{1,0:T(8,128)} custom-call(f32[2,32,128]{2,1,0:T(8,128)S(1)} %add_y_faces.1.mine, f32[2,32,128]{2,1,0:T(8,128)S(1)} %collective-permute-done.5.other, f32[16,128]{1,0:T(8,128)S(1)} %get-tuple-element.39.refs_5_.norm), custom_call_target="tpu_custom_call" | custom-call | tf_op jit(solution)/shard_map/cone_filter/pallas_call | solution.py:652
Async XLA Ops:
  0.6 1.9 %copy-start = (f32[19,12,16,128]{3,2,1,0:T(8,128)S(1)}, f32[19,12,16,128]{3,2,1,0:T(8,128)}, u32[]{:S(2)}) copy-start(f32[19,12,16,128]{3,2,1,0:T(8,128)} %adjoint.5) | copy-start | bytes 5603332
  2.0 1.4 %collective-permute-start = (f32[5,16,128]{2,1,0:T(8,128)S(1)}, f32[5,16,128]{2,1,0:T(8,128)S(1)}, u32[]{:S(2)}, u32[]{:S(2)}) collective-permute-start(f32[5,16,128]{2,1,0:T(8,128)S(1)} %get-tuple-element.24), channel_id=1, source_target_pairs={{0,1},{1,0},{2,3},{3,2},{4,5},{5,4},{6,7},{7,6},{8,9},{9,8},{10,11... | collective-permute-start | bytes 122888 | tf_op jit(solution)/shard_map/ppermute | solution.py:73
  3.5 11.7 %collective-permute-start.3 = (f32[128,128]{1,0:T(8,128)S(1)}, f32[128,128]{1,0:T(8,128)S(1)}, u32[]{:S(2)}, u32[]{:S(2)}) collective-permute-start(f32[128,128]{1,0:T(8,128)S(1)} %get-tuple-element.35.refs_1_), channel_id=1, source_target_pairs={{0,2},{2,0},{1,3},{3,1},{4,6},{6,4},{5,7},{7,5},{8,10},{10,8},{9,1... | collective-permute-start | bytes 196616 | tf_op jit(solution)/shard_map/ppermute | solution.py:73
  6.4 3.0 %collective-permute-start.1 = (f32[32,128]{1,0:T(8,128)S(1)}, f32[32,128]{1,0:T(8,128)S(1)}, u32[]{:S(2)}, u32[]{:S(2)}) collective-permute-start(f32[32,128]{1,0:T(8,128)S(1)} %get-tuple-element.31.refs_3_), channel_id=1, source_target_pairs={{4,8},{5,9},{8,4},{9,5},{12,16},{13,17},{16,12},{17,13},{20,24},{2... | collective-permute-start | bytes 49160 | tf_op jit(solution)/shard_map/ppermute | solution.py:77
  6.4 4.8 %collective-permute-start.2 = (f32[32,128]{1,0:T(8,128)S(1)}, f32[32,128]{1,0:T(8,128)S(1)}, u32[]{:S(2)}, u32[]{:S(2)}) collective-permute-start(f32[32,128]{1,0:T(8,128)S(1)} %get-tuple-element.32.refs_2_), channel_id=1, source_target_pairs={{0,4},{4,0},{8,12},{12,8},{16,20},{20,16},{24,28},{28,24},{1,5},{5... | collective-permute-start | bytes 49160 | tf_op jit(solution)/shard_map/ppermute | solution.py:73
  11.4 3.8 %collective-permute-start.4 = (f32[32,128]{1,0:T(8,128)S(1)}, f32[32,128]{1,0:T(8,128)S(1)}, u32[]{:S(2)}, u32[]{:S(2)}) collective-permute-start(f32[32,128]{1,0:T(8,128)S(1)} %get-tuple-element.37.refs_3_), channel_id=1, source_target_pairs={{0,2},{2,0},{1,3},{3,1},{4,6},{6,4},{5,7},{7,5},{8,10},{10,8},{9,1... | collective-permute-start | bytes 49160 | tf_op jit(solution)/shard_map/ppermute | solution.py:73
  15.4 1.3 %collective-permute-start.5 = (f32[2,32,128]{2,1,0:T(8,128)S(1)}, f32[2,32,128]{2,1,0:T(8,128)S(1)}, u32[]{:S(2)}, u32[]{:S(2)}) collective-permute-start(f32[2,32,128]{2,1,0:T(8,128)S(1)} %add_y_faces.1.mine), channel_id=1, source_target_pairs={{0,1},{1,0},{2,3},{3,2},{4,5},{5,4},{6,7},{7,6},{8,9},{9,8},{10,11... | collective-permute-start | bytes 98312 | tf_op jit(solution)/shard_map/ppermute | solution.py:73

commit v2 on v1

--- a/solution.py
+++ b/solution.py
@@ -642,7 +642,7 @@
         copy.wait()
 
 
-def local_call(body, name, operands, out_shapes, scratch=(), far=(), far_out=(), aliases=None, room=16):
+def local_call(body, name, operands, out_shapes, scratch=(), far=(), far_out=(), aliases=None, room=16, cost=None):
     near_spec = pl.BlockSpec(memory_space=pltpu.VMEM)
     far_spec = pl.BlockSpec(memory_space=pltpu.HBM)
     shapes = [
@@ -658,6 +658,7 @@
         input_output_aliases=aliases or {},
         compiler_params=pltpu.CompilerParams(vmem_limit_bytes=room * 1024 * 1024),
         name=name,
+        cost_estimate=cost,
     )(*operands)
 
 
@@ -723,6 +724,9 @@
         [adjoint.shape, (max(y_pairs, 1), len(velocities), levels, lanes), (rows, lanes)],
         scratch=[pltpu.VMEM(adjoint.shape, jnp.float32), pltpu.SemaphoreType.DMA((groups,))],
         far_out=(0,),
+        cost=pl.CostEstimate(
+            flops=8000 * math.prod(adjoint.shape), bytes_accessed=4000000, transcendentals=0
+        ),
     )
     (column,) = local_call(
         functools.partial(extend_kernel, y_pairs),

time: 17.6 us -> 16.1 us (0.915)
  waiting for transfers between devices: 3.63 us -> 1.18 us
  starting transfers between devices: 7.11 us -> 8.06 us
    ppermute x5, waiting for transfers between devices: 3.63 us -> 1.18 us  [swap(): return lax.ppermute(array, axis, pairs)]
    ppermute x5, starting transfers between devices: 7.1 us -> 7.67 us  [swap(): return lax.ppermute(array, axis, pairs)]
    ppermute x1, starting transfers between devices: 0.01 us -> 0.39 us  [swap(): return lax.ppermute(array, (axis, 'depth'), full)]
  transfers between devices with their start and end apart: 6 -> 6, of which waited for: 4 -> 4; matrix products, arithmetic and copies ran while one was open for 0% -> 0% of each run, Pallas kernels for 20% -> 22%
where the time goes in v2:
time: 16.1 us; the launch traced here: 15.9 us
  starting transfers between devices  8.06 us (50%)
  Pallas kernels  5.98 us (37%)
  waiting for transfers between devices  1.18 us (7%)
  between operations  0.69 us (4%)
    ppermute x5, starting transfers between devices, swap(): return lax.ppermute(array, axis, pairs)  7.67 us
    pallas_call x8, Pallas kernels, local_call(): pl.pallas_call(body, out_shape=shapes, in_specs=[far_spec if place in far...  5.98 us
    ppermute x5, waiting for transfers between devices, swap(): return lax.ppermute(array, axis, pairs)  1.18 us
    ppermute x1, starting transfers between devices, swap(): return lax.ppermute(array, (axis, 'depth'), full)  0.39 us
  transfers between devices with their start and end apart: 6, of which 4 were waited for; matrix products, arithmetic and copies ran while one was open for 0% of the time, Pallas kernels for 22%

profile of v2, /device:TPU:0, one launch (start us, length us, event | category | flops | bytes accessed | tf_op | source)
XLA Modules:
  0.0 15.9 jit_solution(17260848455209379856)
XLA Ops:
  0.6 0.0 copy-start
  0.6 1.4 %load.1 = (f32[3,12,16,128]{3,2,1,0:T(8,128)S(1)}, f32[16,128]{1,0:T(8,128)S(1)}, s32[12,16,128]{2,1,0:T(8,128)S(1)}, s32[12,16,128]{2,1,0:T(8,128)S(1)}, f32[5,16,128]{2,1,0:T(8,128)S(1)}) custom-call(f32[19,12,16,128]{3,2,1,0:T(8,128)} %adjoint.5, f32[3,12,16,128]{3,2,1,0:T(8,128)} %momentum.1, f32[16,128]{1,0:T(8,128)} %design.1, s32[12,16,128]{2,1,0:T(8,128)} %solid.1, ...), custom_call_target="tpu_custom_call" | custom-call | tf_op jit(solution)/shard_map/load/pallas_call | solution.py:652
  2.0 0.5 %collective-permute-start = (f32[5,16,128]{2,1,0:T(8,128)S(1)}, f32[5,16,128]{2,1,0:T(8,128)S(1)}, u32[]{:S(2)}, u32[]{:S(2)}) collective-permute-start(f32[5,16,128]{2,1,0:T(8,128)S(1)} %get-tuple-element.24), channel_id=1, source_target_pairs={{0,1},{1,0},{2,3},{3,2},{4,5},{5,4},{6,7},{7,6},{8,9},{9,8},{10,11... | collective-permute-start | bytes 122888 | tf_op jit(solution)/shard_map/ppermute | solution.py:73
  2.5 0.0 copy-done
  2.5 0.6 %pack_faces.1 = (f32[16,128]{1,0:T(8,128)S(1)}, f32[16,128]{1,0:T(8,128)S(1)}, f32[128,128]{1,0:T(8,128)S(1)}, f32[16,128]{1,0:T(8,128)S(1)}, f32[2,3,16,128]{3,2,1,0:T(8,128)S(1)}) custom-call(f32[19,12,16,128]{3,2,1,0:T(8,128)S(1)} %copy-done, f32[3,12,16,128]{3,2,1,0:T(8,128)S(1)} %get-tuple-element.25.momentum, f32[16,128]{1,0:T(8,128)S(1)} %get-tuple-element.21.design, ...), custom_call_target="tpu_custom_call" | custom-call | tf_op jit(solution)/shard_map/pack_faces/pallas_call | solution.py:652
  3.2 0.2 %collective-permute-done.refs_0_.refs_2_ = f32[5,16,128]{2,1,0:T(8,128)S(1)} collective-permute-done((f32[5,16,128]{2,1,0:T(8,128)S(1)}, f32[5,16,128]{2,1,0:T(8,128)S(1)}, u32[]{:S(2)}, u32[]{:S(2)}) %collective-permute-start) | collective-permute-done | bytes 40992 | tf_op jit(solution)/shard_map/ppermute | solution.py:73
  3.4 0.2 %add_z_faces.1 = (f32[32,128]{1,0:T(8,128)S(1)}, f32[32,128]{1,0:T(8,128)S(1)}, f32[128,128]{1,0:T(8,128)S(1)}, f32[16,128]{1,0:T(8,128)S(1)}) custom-call(f32[5,16,128]{2,1,0:T(8,128)S(1)} %collective-permute-done.refs_0_.refs_2_, f32[16,128]{1,0:T(8,128)S(1)} %get-tuple-element.26.refs_1_, f32[16,128]{1,0:T(8,128)S(1)} %get-tuple-element.27.refs_2_, ...), custom_call_target="tpu_custom_call" | custom-call | tf_op jit(solution)/shard_map/add_z_faces/pallas_call | solution.py:652
  3.5 0.4 %collective-permute-start.1 = (f32[32,128]{1,0:T(8,128)S(1)}, f32[32,128]{1,0:T(8,128)S(1)}, u32[]{:S(2)}, u32[]{:S(2)}) collective-permute-start(f32[32,128]{1,0:T(8,128)S(1)} %get-tuple-element.31.refs_3_), channel_id=1, source_target_pairs={{4,8},{5,9},{8,4},{9,5},{12,16},{13,17},{16,12},{17,13},{20,24},{2... | collective-permute-start | bytes 49160 | tf_op jit(solution)/shard_map/ppermute | solution.py:77
  3.9 4.0 %collective-permute-start.2 = (f32[32,128]{1,0:T(8,128)S(1)}, f32[32,128]{1,0:T(8,128)S(1)}, u32[]{:S(2)}, u32[]{:S(2)}) collective-permute-start(f32[32,128]{1,0:T(8,128)S(1)} %get-tuple-element.32.refs_2_), channel_id=1, source_target_pairs={{0,4},{4,0},{8,12},{12,8},{16,20},{20,16},{24,28},{28,24},{1,5},{5... | collective-permute-start | bytes 49160 | tf_op jit(solution)/shard_map/ppermute | solution.py:73
  8.0 1.5 %collective-permute-start.3 = (f32[128,128]{1,0:T(8,128)S(1)}, f32[128,128]{1,0:T(8,128)S(1)}, u32[]{:S(2)}, u32[]{:S(2)}) collective-permute-start(f32[128,128]{1,0:T(8,128)S(1)} %get-tuple-element.35.refs_1_), channel_id=1, source_target_pairs={{0,2},{2,0},{1,3},{3,1},{4,6},{6,4},{5,7},{7,5},{8,10},{10,8},{9,1... | collective-permute-start | bytes 196616 | tf_op jit(solution)/shard_map/ppermute | solution.py:73
  9.5 0.0 collective-permute-done.1.refs_0_
  9.5 0.2 %collective-permute-done.2.refs_1_ = f32[32,128]{1,0:T(8,128)S(1)} collective-permute-done((f32[32,128]{1,0:T(8,128)S(1)}, f32[32,128]{1,0:T(8,128)S(1)}, u32[]{:S(2)}, u32[]{:S(2)}) %collective-permute-start.2) | collective-permute-done | bytes 16416 | tf_op jit(solution)/shard_map/ppermute | solution.py:73
  9.7 0.2 %add_x_faces.1 = (f32[32,128]{1,0:T(8,128)S(1)}, f32[2,16,128]{2,1,0:T(8,128)S(1)}) custom-call(f32[32,128]{1,0:T(8,128)S(1)} %collective-permute-done.1.refs_0_, f32[32,128]{1,0:T(8,128)S(1)} %collective-permute-done.2.refs_1_, f32[32,128]{1,0:T(8,128)S(1)} %get-tuple-element.32.refs_2_, f32[32,128]{1,0:T(8,128)S(1)} %get-tuple-element.31.refs_3_, ...), custom_call_target="tpu_custom_call" | custom-call | tf_op jit(solution)/shard_map/add_x_faces/pallas_call | solution.py:652
  9.9 1.6 %collective-permute-start.4 = (f32[32,128]{1,0:T(8,128)S(1)}, f32[32,128]{1,0:T(8,128)S(1)}, u32[]{:S(2)}, u32[]{:S(2)}) collective-permute-start(f32[32,128]{1,0:T(8,128)S(1)} %get-tuple-element.37.refs_3_), channel_id=1, source_target_pairs={{0,2},{2,0},{1,3},{3,1},{4,6},{6,4},{5,7},{7,5},{8,10},{10,8},{9,1... | collective-permute-start | bytes 49160 | tf_op jit(solution)/shard_map/ppermute | solution.py:73
  11.5 1.8 %collide.1 = (f32[19,12,16,128]{3,2,1,0:T(8,128)}, f32[1,19,12,128]{3,2,1,0:T(8,128)S(1)}, f32[16,128]{1,0:T(8,128)S(1)}) custom-call(f32[19,12,16,128]{3,2,1,0:T(8,128)S(1)} %copy-done, f32[16,128]{1,0:T(8,128)S(1)} %get-tuple-element.21.design, s32[12,16,128]{2,1,0:T(8,128)S(1)} %get-tuple-element.22.solid, s32[12,16,128]{2,1,0:T(8,128)S(1)} %get-tuple-element.23.port, ...), custom_call_target="tpu_custom_call" | custom-call | flops 3735552000 | bytes 4000000 | tf_op jit(solution)/shard_map/collide/pallas_call | solution.py:652
  13.3 0.5 %collective-permute-done.4.refs_1_.refs_2_ = f32[32,128]{1,0:T(8,128)S(1)} collective-permute-done((f32[32,128]{1,0:T(8,128)S(1)}, f32[32,128]{1,0:T(8,128)S(1)}, u32[]{:S(2)}, u32[]{:S(2)}) %collective-permute-start.4) | collective-permute-done | bytes 16416 | tf_op jit(solution)/shard_map/ppermute | solution.py:73
  13.7 0.0 collective-permute-done.3.refs_0_
  13.7 0.2 %add_y_faces.1.mine = f32[2,32,128]{2,1,0:T(8,128)S(1)} custom-call(f32[128,128]{1,0:T(8,128)S(1)} %collective-permute-done.3.refs_0_, f32[128,128]{1,0:T(8,128)S(1)} %get-tuple-element.35.refs_1_, f32[32,128]{1,0:T(8,128)S(1)} %collective-permute-done.4.refs_1_.refs_2_, f32[32,128]{1,0:T(8,128)S(1)} %get-tuple-element.37.refs_3_, ...), custom_call_target="tpu_custom_call" | custom-call | tf_op jit(solution)/shard_map/add_y_faces/pallas_call | solution.py:652
  13.9 0.1 collective-permute-start.5
  14.0 0.9 %add_y_rows.1 = f32[19,12,16,128]{3,2,1,0:T(8,128)} custom-call(f32[19,12,16,128]{3,2,1,0:T(8,128)} %get-tuple-element.33.new, f32[1,19,12,128]{3,2,1,0:T(8,128)S(1)} %get-tuple-element.34.edge_rows, f32[16,128]{1,0:T(8,128)S(1)} %get-tuple-element.21.design, s32[12,16,128]{2,1,0:T(8,128)S(1)} %get-tuple-element.22.solid, ...), custom_call_target="tpu_custom_call", output_to_operand_aliasing={{}: (0, {})} | custom-call | tf_op jit(solution)/shard_map/add_y_rows/pallas_call | solution.py:652
  14.9 0.3 %collective-permute-done.5.other = f32[2,32,128]{2,1,0:T(8,128)S(1)} collective-permute-done((f32[2,32,128]{2,1,0:T(8,128)S(1)}, f32[2,32,128]{2,1,0:T(8,128)S(1)}, u32[]{:S(2)}, u32[]{:S(2)}) %collective-permute-start.5) | collective-permute-done | bytes 32800 | tf_op jit(solution)/shard_map/ppermute | solution.py:73
  15.2 0.7 %cone_filter.1 = f32[16,128]{1,0:T(8,128)} custom-call(f32[2,32,128]{2,1,0:T(8,128)S(1)} %add_y_faces.1.mine, f32[2,32,128]{2,1,0:T(8,128)S(1)} %collective-permute-done.5.other, f32[16,128]{1,0:T(8,128)S(1)} %get-tuple-element.39.refs_5_.norm), custom_call_target="tpu_custom_call" | custom-call | tf_op jit(solution)/shard_map/cone_filter/pallas_call | solution.py:652
Async XLA Ops:
  0.6 1.9 %copy-start = (f32[19,12,16,128]{3,2,1,0:T(8,128)S(1)}, f32[19,12,16,128]{3,2,1,0:T(8,128)}, u32[]{:S(2)}) copy-start(f32[19,12,16,128]{3,2,1,0:T(8,128)} %adjoint.5) | copy-start | bytes 5603332
  2.0 1.4 %collective-permute-start = (f32[5,16,128]{2,1,0:T(8,128)S(1)}, f32[5,16,128]{2,1,0:T(8,128)S(1)}, u32[]{:S(2)}, u32[]{:S(2)}) collective-permute-start(f32[5,16,128]{2,1,0:T(8,128)S(1)} %get-tuple-element.24), channel_id=1, source_target_pairs={{0,1},{1,0},{2,3},{3,2},{4,5},{5,4},{6,7},{7,6},{8,9},{9,8},{10,11... | collective-permute-start | bytes 122888 | tf_op jit(solution)/shard_map/ppermute | solution.py:73
  3.5 5.9 %collective-permute-start.1 = (f32[32,128]{1,0:T(8,128)S(1)}, f32[32,128]{1,0:T(8,128)S(1)}, u32[]{:S(2)}, u32[]{:S(2)}) collective-permute-start(f32[32,128]{1,0:T(8,128)S(1)} %get-tuple-element.31.refs_3_), channel_id=1, source_target_pairs={{4,8},{5,9},{8,4},{9,5},{12,16},{13,17},{16,12},{17,13},{20,24},{2... | collective-permute-start | bytes 49160 | tf_op jit(solution)/shard_map/ppermute | solution.py:77
  3.9 5.7 %collective-permute-start.2 = (f32[32,128]{1,0:T(8,128)S(1)}, f32[32,128]{1,0:T(8,128)S(1)}, u32[]{:S(2)}, u32[]{:S(2)}) collective-permute-start(f32[32,128]{1,0:T(8,128)S(1)} %get-tuple-element.32.refs_2_), channel_id=1, source_target_pairs={{0,4},{4,0},{8,12},{12,8},{16,20},{20,16},{24,28},{28,24},{1,5},{5... | collective-permute-start | bytes 49160 | tf_op jit(solution)/shard_map/ppermute | solution.py:73
  8.0 5.7 %collective-permute-start.3 = (f32[128,128]{1,0:T(8,128)S(1)}, f32[128,128]{1,0:T(8,128)S(1)}, u32[]{:S(2)}, u32[]{:S(2)}) collective-permute-start(f32[128,128]{1,0:T(8,128)S(1)} %get-tuple-element.35.refs_1_), channel_id=1, source_target_pairs={{0,2},{2,0},{1,3},{3,1},{4,6},{6,4},{5,7},{7,5},{8,10},{10,8},{9,1... | collective-permute-start | bytes 196616 | tf_op jit(solution)/shard_map/ppermute | solution.py:73
  9.9 3.8 %collective-permute-start.4 = (f32[32,128]{1,0:T(8,128)S(1)}, f32[32,128]{1,0:T(8,128)S(1)}, u32[]{:S(2)}, u32[]{:S(2)}) collective-permute-start(f32[32,128]{1,0:T(8,128)S(1)} %get-tuple-element.37.refs_3_), channel_id=1, source_target_pairs={{0,2},{2,0},{1,3},{3,1},{4,6},{6,4},{5,7},{7,5},{8,10},{10,8},{9,1... | collective-permute-start | bytes 49160 | tf_op jit(solution)/shard_map/ppermute | solution.py:73
  13.9 1.3 %collective-permute-start.5 = (f32[2,32,128]{2,1,0:T(8,128)S(1)}, f32[2,32,128]{2,1,0:T(8,128)S(1)}, u32[]{:S(2)}, u32[]{:S(2)}) collective-permute-start(f32[2,32,128]{2,1,0:T(8,128)S(1)} %add_y_faces.1.mine), channel_id=1, source_target_pairs={{0,1},{1,0},{2,3},{3,2},{4,5},{5,4},{6,7},{7,6},{8,9},{9,8},{10,11... | collective-permute-start | bytes 98312 | tf_op jit(solution)/shard_map/ppermute | solution.py:73

commit v3 on v2

--- a/solution.py
+++ b/solution.py
@@ -176,25 +176,24 @@
     return [(low, min(low + level_group, levels)) for low in range(0, levels, level_group)]
 
 
-def load_kernel(z_pairs, adjoint, momentum, design, solid, port, *refs):
-    near, outs, sems = (refs[:4], refs[4 : 4 + z_pairs], refs[4 + z_pairs])
-    levels = adjoint.shape[1]
-    pairs = []
-    for pairing in range(z_pairs):
-        after = partner_after("depth", pairing)
-        level = jnp.where(after, levels - 1, 0)
-        for kind, numbers in enumerate(zip(crossing(2, -1), crossing(2, 1))):
-            number = jnp.where(after, numbers[0], numbers[1])
-            pairs.append((adjoint.at[number, level], outs[pairing].at[kind]))
-    pairs += zip((momentum, design, solid, port), near)
-    copies = [
-        pltpu.make_async_copy(source, target, sems.at[place])
-        for place, (source, target) in enumerate(pairs)
-    ]
+def run_all(copies):
     for copy in copies:
         copy.start()
     for copy in copies:
         copy.wait()
+
+
+def face_kernel(z_pairs, adjoint, *refs):
+    outs, sems = (refs[:z_pairs], refs[z_pairs])
+    copies = []
+    for pairing in range(z_pairs):
+        after = partner_after("depth", pairing)
+        level = jnp.where(after, adjoint.shape[1] - 1, 0)
+        for kind, numbers in enumerate(zip(crossing(2, -1), crossing(2, 1))):
+            number = jnp.where(after, numbers[0], numbers[1])
+            source, target = (adjoint.at[number, level], outs[pairing].at[kind])
+            copies.append(pltpu.make_async_copy(source, target, sems.at[len(copies)]))
+    run_all(copies)
 
 
 def pack_kernel(counts, adjoint, momentum, design, solid, port, *refs):
@@ -459,10 +458,10 @@
             before[part] = before[part] + pick(flag, none, sums)
             after[part] = after[part] + pick(flag, sums, none)
             own[part] = own[part] + jnp.where(row == edge_here, here[part], 0.0)
-    for part in range(2):
-        out[part, 0:tile, :] = before[part]
-        out[part, tile : tile + rows, :] = own[part]
-        out[part, tile + rows :, :] = after[part]
+    main, side = (
+        jnp.concatenate([before[part], own[part], after[part]], axis=0) for part in range(2)
+    )
+    out[...] = cone_sum(main, side, rows) * norm[...]
 
 
 def cone_sum(main, side, rows):
@@ -485,9 +484,8 @@
     return total
 
 
-def filter_kernel(mine, other, norm, out):
-    rows = out.shape[0]
-    out[...] = cone_sum(mine[0] + other[0], mine[1] + other[1], rows) * norm[...]
+def filter_kernel(mine, other, out):
+    out[...] = mine[...] + other[...]
 
 
 def filter_norm(rows, lanes):
@@ -667,25 +665,18 @@
     slots = lanes // tile
     groups = len(groups_of(levels))
     x_pairs, y_pairs, z_pairs = (len(pairings(axis)) for axis in ("gx", "gy", "depth"))
-    loaded = local_call(
-        functools.partial(load_kernel, z_pairs),
-        "load",
-        [
-            pltpu.with_memory_space_constraint(array, pltpu.HBM)
-            for array in (adjoint, momentum, design, solid_mask, port_label)
-        ],
-        [
-            pltpu.VMEM(momentum.shape, jnp.float32),
-            pltpu.VMEM(design.shape, jnp.float32),
-            pltpu.VMEM(solid_mask.shape, jnp.int32),
-            pltpu.VMEM(port_label.shape, jnp.int32),
-        ]
-        + [pltpu.VMEM((len(laterals), rows, lanes), jnp.float32)] * z_pairs,
-        scratch=[pltpu.SemaphoreType.DMA((z_pairs * len(laterals) + 4,))],
-        far=range(5),
-    )
-    momentum, design, solid_mask, port_label = loaded[:4]
-    z_got = [swap(face, "depth", pairing) for pairing, face in enumerate(loaded[4:])]
+    z_got = []
+    if z_pairs:
+        faces = local_call(
+            functools.partial(face_kernel, z_pairs),
+            "depth_faces",
+            [pltpu.with_memory_space_constraint(adjoint, pltpu.HBM)],
+            [pltpu.VMEM((len(laterals), rows, lanes), jnp.float32)] * z_pairs,
+            scratch=[pltpu.SemaphoreType.DMA((z_pairs * len(laterals),))],
+            far=(0,),
+            cost=pl.CostEstimate(flops=2000 * math.prod(adjoint.shape), bytes_accessed=100000, transcendentals=0),
+        )
+        z_got = [swap(face, "depth", pairing) for pairing, face in enumerate(faces)]
     packed = local_call(
         functools.partial(pack_kernel, (x_pairs, y_pairs)),
         "pack_faces",
@@ -732,7 +723,7 @@
         functools.partial(extend_kernel, y_pairs),
         "add_y_faces",
         [*y_got, *y_sent, *ends_got, *ends_sent, middle, norm],
-        [(2, rows + 2 * tile, lanes)],
+        [(rows, lanes)],
     )
     if z_pairs == 1:
         other = swap(column, "depth", 0)
@@ -753,7 +744,7 @@
             aliases={0: 0},
         )
     (sensitivity,) = local_call(
-        filter_kernel, "cone_filter", [column, other, norm], [(rows, lanes)]
+        filter_kernel, "add_depth", [column, other], [(rows, lanes)]
     )
     return (new_adjoint, sensitivity)
 

time: 16.1 us -> 15.7 us (0.975)
  Pallas kernels: 5.98 us -> 5.58 us
    pallas_call x8, Pallas kernels: 5.98 us -> 5.58 us  [local_call(): pl.pallas_call(body, out_shape=shapes, in_specs=[far_spec if place in far...]
  transfers between devices with their start and end apart: 6 -> 6, of which waited for: 4 -> 4; matrix products, arithmetic and copies ran while one was open for 0% -> 0% of each run, Pallas kernels for 22% -> 23%
where the time goes in v3:
time: 15.7 us; the launch traced here: 15.5 us
  starting transfers between devices  8.08 us (51%)
  Pallas kernels  5.58 us (36%)
  waiting for transfers between devices  1.02 us (6%)
  between operations  0.73 us (5%)
    ppermute x5, starting transfers between devices, swap(): return lax.ppermute(array, axis, pairs)  7.67 us
    pallas_call x8, Pallas kernels, local_call(): pl.pallas_call(body, out_shape=shapes, in_specs=[far_spec if place in far...  5.58 us
    ppermute x5, waiting for transfers between devices, swap(): return lax.ppermute(array, axis, pairs)  1.02 us
    ppermute x1, starting transfers between devices, swap(): return lax.ppermute(array, (axis, 'depth'), full)  0.41 us
  transfers between devices with their start and end apart: 6, of which 4 were waited for; matrix products, arithmetic and copies ran while one was open for 0% of the time, Pallas kernels for 23%

profile of v3, /device:TPU:0, one launch (start us, length us, event | category | flops | bytes accessed | tf_op | source)
XLA Modules:
  0.0 15.5 jit_solution(2498263953541954218)
XLA Ops:
  0.6 0.0 copy-start
  0.6 0.0 copy-start.2
  0.7 0.0 copy-start.1
  0.7 0.0 copy-start.4
  0.7 0.0 copy-start.3
  0.7 1.0 %depth_faces.1 = f32[5,16,128]{2,1,0:T(8,128)S(1)} custom-call(f32[19,12,16,128]{3,2,1,0:T(8,128)} %adjoint.5), custom_call_target="tpu_custom_call" | custom-call | flops 933888000 | bytes 100000 | tf_op jit(solution)/shard_map/depth_faces/pallas_call | solution.py:650
  1.6 0.5 %collective-permute-start = (f32[5,16,128]{2,1,0:T(8,128)S(1)}, f32[5,16,128]{2,1,0:T(8,128)S(1)}, u32[]{:S(2)}, u32[]{:S(2)}) collective-permute-start(f32[5,16,128]{2,1,0:T(8,128)S(1)} %depth_faces.1), channel_id=1, source_target_pairs={{0,1},{1,0},{2,3},{3,2},{4,5},{5,4},{6,7},{7,6},{8,9},{9,8},{10,11... | collective-permute-start | bytes 122888 | tf_op jit(solution)/shard_map/ppermute | solution.py:73
  2.2 0.0 copy-done
  2.2 0.0 copy-done.2
  2.2 0.0 copy-done.1
  2.2 0.0 copy-done.4
  2.2 0.1 copy-done.3
  2.3 0.6 %pack_faces.1 = (f32[16,128]{1,0:T(8,128)S(1)}, f32[16,128]{1,0:T(8,128)S(1)}, f32[128,128]{1,0:T(8,128)S(1)}, f32[16,128]{1,0:T(8,128)S(1)}, f32[2,3,16,128]{3,2,1,0:T(8,128)S(1)}) custom-call(f32[19,12,16,128]{3,2,1,0:T(8,128)S(1)} %copy-done, f32[3,12,16,128]{3,2,1,0:T(8,128)S(1)} %copy-done.3, f32[16,128]{1,0:T(8,128)S(1)} %copy-done.4, ...), custom_call_target="tpu_custom_call" | custom-call | tf_op jit(solution)/shard_map/pack_faces/pallas_call | solution.py:650
  2.9 0.1 collective-permute-done.refs_0_.refs_2_
  3.0 0.2 %add_z_faces.1 = (f32[32,128]{1,0:T(8,128)S(1)}, f32[32,128]{1,0:T(8,128)S(1)}, f32[128,128]{1,0:T(8,128)S(1)}, f32[16,128]{1,0:T(8,128)S(1)}) custom-call(f32[5,16,128]{2,1,0:T(8,128)S(1)} %collective-permute-done.refs_0_.refs_2_, f32[16,128]{1,0:T(8,128)S(1)} %get-tuple-element.16.refs_1_, f32[16,128]{1,0:T(8,128)S(1)} %get-tuple-element.17.refs_2_, ...), custom_call_target="tpu_custom_call" | custom-call | tf_op jit(solution)/shard_map/add_z_faces/pallas_call | solution.py:650
  3.2 0.4 %collective-permute-start.1 = (f32[32,128]{1,0:T(8,128)S(1)}, f32[32,128]{1,0:T(8,128)S(1)}, u32[]{:S(2)}, u32[]{:S(2)}) collective-permute-start(f32[32,128]{1,0:T(8,128)S(1)} %get-tuple-element.21.refs_3_), channel_id=1, source_target_pairs={{4,8},{5,9},{8,4},{9,5},{12,16},{13,17},{16,12},{17,13},{20,24},{2... | collective-permute-start | bytes 49160 | tf_op jit(solution)/shard_map/ppermute | solution.py:77
  3.6 4.0 %collective-permute-start.2 = (f32[32,128]{1,0:T(8,128)S(1)}, f32[32,128]{1,0:T(8,128)S(1)}, u32[]{:S(2)}, u32[]{:S(2)}) collective-permute-start(f32[32,128]{1,0:T(8,128)S(1)} %get-tuple-element.22.refs_2_), channel_id=1, source_target_pairs={{0,4},{4,0},{8,12},{12,8},{16,20},{20,16},{24,28},{28,24},{1,5},{5... | collective-permute-start | bytes 49160 | tf_op jit(solution)/shard_map/ppermute | solution.py:73
  7.6 1.5 %collective-permute-start.3 = (f32[128,128]{1,0:T(8,128)S(1)}, f32[128,128]{1,0:T(8,128)S(1)}, u32[]{:S(2)}, u32[]{:S(2)}) collective-permute-start(f32[128,128]{1,0:T(8,128)S(1)} %get-tuple-element.25.refs_1_), channel_id=1, source_target_pairs={{0,2},{2,0},{1,3},{3,1},{4,6},{6,4},{5,7},{7,5},{8,10},{10,8},{9,1... | collective-permute-start | bytes 196616 | tf_op jit(solution)/shard_map/ppermute | solution.py:73
  9.1 0.0 collective-permute-done.1.refs_0_
  9.1 0.2 %collective-permute-done.2.refs_1_ = f32[32,128]{1,0:T(8,128)S(1)} collective-permute-done((f32[32,128]{1,0:T(8,128)S(1)}, f32[32,128]{1,0:T(8,128)S(1)}, u32[]{:S(2)}, u32[]{:S(2)}) %collective-permute-start.2) | collective-permute-done | bytes 16416 | tf_op jit(solution)/shard_map/ppermute | solution.py:73
  9.4 0.2 %add_x_faces.1 = (f32[32,128]{1,0:T(8,128)S(1)}, f32[2,16,128]{2,1,0:T(8,128)S(1)}) custom-call(f32[32,128]{1,0:T(8,128)S(1)} %collective-permute-done.1.refs_0_, f32[32,128]{1,0:T(8,128)S(1)} %collective-permute-done.2.refs_1_, f32[32,128]{1,0:T(8,128)S(1)} %get-tuple-element.22.refs_2_, f32[32,128]{1,0:T(8,128)S(1)} %get-tuple-element.21.refs_3_, ...), custom_call_target="tpu_custom_call" | custom-call | tf_op jit(solution)/shard_map/add_x_faces/pallas_call | solution.py:650
  9.6 1.6 %collective-permute-start.4 = (f32[32,128]{1,0:T(8,128)S(1)}, f32[32,128]{1,0:T(8,128)S(1)}, u32[]{:S(2)}, u32[]{:S(2)}) collective-permute-start(f32[32,128]{1,0:T(8,128)S(1)} %get-tuple-element.27.refs_3_), channel_id=1, source_target_pairs={{0,2},{2,0},{1,3},{3,1},{4,6},{6,4},{5,7},{7,5},{8,10},{10,8},{9,1... | collective-permute-start | bytes 49160 | tf_op jit(solution)/shard_map/ppermute | solution.py:73
  11.1 1.8 %collide.1 = (f32[19,12,16,128]{3,2,1,0:T(8,128)}, f32[1,19,12,128]{3,2,1,0:T(8,128)S(1)}, f32[16,128]{1,0:T(8,128)S(1)}) custom-call(f32[19,12,16,128]{3,2,1,0:T(8,128)S(1)} %copy-done, f32[16,128]{1,0:T(8,128)S(1)} %copy-done.4, s32[12,16,128]{2,1,0:T(8,128)S(1)} %copy-done.1, s32[12,16,128]{2,1,0:T(8,128)S(1)} %copy-done.2, ...), custom_call_target="tpu_custom_call" | custom-call | flops 3735552000 | bytes 4000000 | tf_op jit(solution)/shard_map/collide/pallas_call | solution.py:650
  12.9 0.5 %collective-permute-done.4.refs_1_.refs_2_ = f32[32,128]{1,0:T(8,128)S(1)} collective-permute-done((f32[32,128]{1,0:T(8,128)S(1)}, f32[32,128]{1,0:T(8,128)S(1)}, u32[]{:S(2)}, u32[]{:S(2)}) %collective-permute-start.4) | collective-permute-done | bytes 16416 | tf_op jit(solution)/shard_map/ppermute | solution.py:73
  13.4 0.0 collective-permute-done.3.refs_0_
  13.4 0.3 %add_y_faces.1.mine = f32[16,128]{1,0:T(8,128)S(1)} custom-call(f32[128,128]{1,0:T(8,128)S(1)} %collective-permute-done.3.refs_0_, f32[128,128]{1,0:T(8,128)S(1)} %get-tuple-element.25.refs_1_, f32[32,128]{1,0:T(8,128)S(1)} %collective-permute-done.4.refs_1_.refs_2_, f32[32,128]{1,0:T(8,128)S(1)} %get-tuple-element.27.refs_3_, ...), custom_call_target="tpu_custom_call" | custom-call | tf_op jit(solution)/shard_map/add_y_faces/pallas_call | solution.py:650
  13.7 0.1 collective-permute-start.5
  13.8 0.9 %add_y_rows.1 = f32[19,12,16,128]{3,2,1,0:T(8,128)} custom-call(f32[19,12,16,128]{3,2,1,0:T(8,128)} %get-tuple-element.23.new, f32[1,19,12,128]{3,2,1,0:T(8,128)S(1)} %get-tuple-element.24.edge_rows, f32[16,128]{1,0:T(8,128)S(1)} %copy-done.4, s32[12,16,128]{2,1,0:T(8,128)S(1)} %copy-done.1, ...), custom_call_target="tpu_custom_call", output_to_operand_aliasing={{}: (0, {})} | custom-call | tf_op jit(solution)/shard_map/add_y_rows/pallas_call | solution.py:650
  14.7 0.2 %collective-permute-done.5.other = f32[16,128]{1,0:T(8,128)S(1)} collective-permute-done((f32[16,128]{1,0:T(8,128)S(1)}, f32[16,128]{1,0:T(8,128)S(1)}, u32[]{:S(2)}, u32[]{:S(2)}) %collective-permute-start.5) | collective-permute-done | bytes 8224 | tf_op jit(solution)/shard_map/ppermute | solution.py:73
  14.9 0.6 %add_depth.1 = f32[16,128]{1,0:T(8,128)} custom-call(f32[16,128]{1,0:T(8,128)S(1)} %add_y_faces.1.mine, f32[16,128]{1,0:T(8,128)S(1)} %collective-permute-done.5.other), custom_call_target="tpu_custom_call" | custom-call | tf_op jit(solution)/shard_map/add_depth/pallas_call | solution.py:650
Async XLA Ops:
  0.6 1.6 %copy-start = (f32[19,12,16,128]{3,2,1,0:T(8,128)S(1)}, f32[19,12,16,128]{3,2,1,0:T(8,128)}, u32[]{:S(2)}) copy-start(f32[19,12,16,128]{3,2,1,0:T(8,128)} %adjoint.5) | copy-start | bytes 5603332
  0.6 1.6 %copy-start.2 = (s32[12,16,128]{2,1,0:T(8,128)S(1)}, s32[12,16,128]{2,1,0:T(8,128)}, u32[]{:S(2)}) copy-start(s32[12,16,128]{2,1,0:T(8,128)} %port.5) | copy-start | bytes 294916
  0.7 1.5 %copy-start.1 = (s32[12,16,128]{2,1,0:T(8,128)S(1)}, s32[12,16,128]{2,1,0:T(8,128)}, u32[]{:S(2)}) copy-start(s32[12,16,128]{2,1,0:T(8,128)} %solid.5) | copy-start | bytes 294916
  0.7 1.5 %copy-start.4 = (f32[16,128]{1,0:T(8,128)S(1)}, f32[16,128]{1,0:T(8,128)}, u32[]{:S(2)}) copy-start(f32[16,128]{1,0:T(8,128)} %design.5) | copy-start | bytes 24580
  0.7 1.6 %copy-start.3 = (f32[3,12,16,128]{3,2,1,0:T(8,128)S(1)}, f32[3,12,16,128]{3,2,1,0:T(8,128)}, u32[]{:S(2)}) copy-start(f32[3,12,16,128]{3,2,1,0:T(8,128)} %momentum.1) | copy-start | bytes 884740
  1.6 1.4 %collective-permute-start = (f32[5,16,128]{2,1,0:T(8,128)S(1)}, f32[5,16,128]{2,1,0:T(8,128)S(1)}, u32[]{:S(2)}, u32[]{:S(2)}) collective-permute-start(f32[5,16,128]{2,1,0:T(8,128)S(1)} %depth_faces.1), channel_id=1, source_target_pairs={{0,1},{1,0},{2,3},{3,2},{4,5},{5,4},{6,7},{7,6},{8,9},{9,8},{10,11... | collective-permute-start | bytes 122888 | tf_op jit(solution)/shard_map/ppermute | solution.py:73
  3.2 5.9 %collective-permute-start.1 = (f32[32,128]{1,0:T(8,128)S(1)}, f32[32,128]{1,0:T(8,128)S(1)}, u32[]{:S(2)}, u32[]{:S(2)}) collective-permute-start(f32[32,128]{1,0:T(8,128)S(1)} %get-tuple-element.21.refs_3_), channel_id=1, source_target_pairs={{4,8},{5,9},{8,4},{9,5},{12,16},{13,17},{16,12},{17,13},{20,24},{2... | collective-permute-start | bytes 49160 | tf_op jit(solution)/shard_map/ppermute | solution.py:77
  3.6 5.7 %collective-permute-start.2 = (f32[32,128]{1,0:T(8,128)S(1)}, f32[32,128]{1,0:T(8,128)S(1)}, u32[]{:S(2)}, u32[]{:S(2)}) collective-permute-start(f32[32,128]{1,0:T(8,128)S(1)} %get-tuple-element.22.refs_2_), channel_id=1, source_target_pairs={{0,4},{4,0},{8,12},{12,8},{16,20},{20,16},{24,28},{28,24},{1,5},{5... | collective-permute-start | bytes 49160 | tf_op jit(solution)/shard_map/ppermute | solution.py:73
  7.6 5.7 %collective-permute-start.3 = (f32[128,128]{1,0:T(8,128)S(1)}, f32[128,128]{1,0:T(8,128)S(1)}, u32[]{:S(2)}, u32[]{:S(2)}) collective-permute-start(f32[128,128]{1,0:T(8,128)S(1)} %get-tuple-element.25.refs_1_), channel_id=1, source_target_pairs={{0,2},{2,0},{1,3},{3,1},{4,6},{6,4},{5,7},{7,5},{8,10},{10,8},{9,1... | collective-permute-start | bytes 196616 | tf_op jit(solution)/shard_map/ppermute | solution.py:73
  9.6 3.8 %collective-permute-start.4 = (f32[32,128]{1,0:T(8,128)S(1)}, f32[32,128]{1,0:T(8,128)S(1)}, u32[]{:S(2)}, u32[]{:S(2)}) collective-permute-start(f32[32,128]{1,0:T(8,128)S(1)} %get-tuple-element.27.refs_3_), channel_id=1, source_target_pairs={{0,2},{2,0},{1,3},{3,1},{4,6},{6,4},{5,7},{7,5},{8,10},{10,8},{9,1... | collective-permute-start | bytes 49160 | tf_op jit(solution)/shard_map/ppermute | solution.py:73
  13.7 1.2 %collective-permute-start.5 = (f32[16,128]{1,0:T(8,128)S(1)}, f32[16,128]{1,0:T(8,128)S(1)}, u32[]{:S(2)}, u32[]{:S(2)}) collective-permute-start(f32[16,128]{1,0:T(8,128)S(1)} %add_y_faces.1.mine), channel_id=1, source_target_pairs={{0,1},{1,0},{2,3},{3,2},{4,5},{5,4},{6,7},{7,6},{8,9},{9,8},{10,11... | collective-permute-start | bytes 24584 | tf_op jit(solution)/shard_map/ppermute | solution.py:73

commit v4 on v3

--- a/solution.py
+++ b/solution.py
@@ -41,6 +41,11 @@
 laterals = ((0, 0), (1, 0), (-1, 0), (0, 1), (0, -1))
 lateral_weights = (1.0 / 18.0,) + (1.0 / 36.0,) * 4
 kinds = len(laterals) + 3
+both_ends = 2 * wide
+
+
+def spot(kind):
+    return 2 * kind + 1 if kind < kinds // 2 else 2 * kind - kinds
 
 
 def crossing(axis, sign):
@@ -209,8 +214,7 @@
     for pairing in range(y_pairs):
         y_out[pairing][...] = jnp.zeros(y_out[pairing].shape, jnp.float32)
     total = jnp.zeros((rows, lanes), jnp.float32)
-    first_pack = jnp.zeros((rows, lanes), jnp.float32)
-    last_pack = jnp.zeros((rows, lanes), jnp.float32)
+    joint = [jnp.zeros((rows, lanes), jnp.float32) for half in range(2)]
     for level in range(levels):
         gain = gain_of(momentum, scale, solid, port, level)
         moment = own_moment(
@@ -234,11 +238,12 @@
             if kind < len(laterals):
                 first = adjoint[crossing(0, 1)[kind], level]
                 last = adjoint[crossing(0, -1)[kind], level]
+                plane = jnp.where(lane == lanes - 1, last, first)
             else:
-                first = last = gain[kind - len(laterals)]
-            place = level * tile + kind
-            first_pack = jnp.where(lane == place, turn(first, place, 1), first_pack)
-            last_pack = jnp.where(lane == place, turn(last, place + 1, 1), last_pack)
+                plane = gain[kind - len(laterals)]
+            half, place = (kind // (kinds // 2), level * tile + 2 * (kind % (kinds // 2)))
+            chosen = lane // 2 == place // 2
+            joint[half] = jnp.where(chosen, turn(plane, place + 1, 1), joint[half])
     for pairing in range(y_pairs):
         after = partner_after("gy", pairing)
         for kind in range(len(laterals)):
@@ -247,6 +252,9 @@
                 after, adjoint[last, :, rows - 1, :], adjoint[first, :, 0, :]
             )
     own_out[...] = total
+    odd = lane % 2 == 1
+    first_pack = jnp.where(odd, joint[0], turn(joint[1], -1, 1))
+    last_pack = jnp.where(odd, turn(joint[0], 1, 1), joint[1])
     for pairing in range(x_pairs):
         x_out[pairing][...] = pick(partner_after("gx", pairing), last_pack, first_pack)
 
@@ -293,39 +301,41 @@
                     after, last[rows - 1 : rows], first[0:1]
                 )
     spare = (levels + 1) * tile
-    chosen = (lane >= spare) & (lane < spare + filter_reach)
+    chosen = (lane >= spare) & (lane < spare + 2 * filter_reach)
+    sums = jnp.where(chosen, turn(total, spare + filter_reach, 1), 0.0)
     packs = []
-    for edge_shift, sign, sums in ((0, 1, 0), (1, -1, filter_reach)):
-        pack = jnp.where(chosen, turn(total, spare + sums, 1), 0.0)
+    for edge_shift, sign in ((0, 1), (1, -1)):
+        pack = sums
         if z_pairs:
             for kind, level, side in beyond:
                 planes = crossing(2, 1 if side else -1)
                 plane = halo[side][planes.index(crossing(0, sign)[kind])]
-                place = (level % slots) * tile + kind
+                place = (level % slots) * tile + spot(kind)
                 pack = jnp.where(lane == place, turn(plane, place + edge_shift, 1), pack)
         packs.append(pack)
-    ends = [jnp.zeros((slots, lanes), jnp.float32) for side in range(2)]
-    lane = lanes_of((slots, lanes))
-    for pairing in range(y_pairs):
-        for kind in range(kinds):
-            line = y_out[pairing][kind * slots : (kind + 1) * slots, :]
-            place = (pairing * kinds + kind) * wide
-            chosen = (lane >= place) & (lane < place + wide)
-            ends[0] = jnp.where(chosen, turn(line, place, 1), ends[0])
-            ends[1] = jnp.where(chosen, turn(line, place + wide, 1), ends[1])
     for pairing in range(x_pairs):
         after = partner_after("gx", pairing)
         x_out[pairing][0:rows, :] = x_pack[pairing][...] + pick(after, packs[1], packs[0])
-        x_out[pairing][rows : rows + slots, :] = pick(after, ends[1], ends[0])
+    lane = lanes_of((slots, lanes))
+    for y_pairing in range(y_pairs):
+        ends = jnp.zeros((slots, lanes), jnp.float32)
+        for kind in range(kinds):
+            line = y_out[y_pairing][kind * slots : (kind + 1) * slots, :]
+            place = kind * both_ends
+            chosen = (lane >= place) & (lane < place + both_ends)
+            ends = jnp.where(chosen, turn(line, place + wide, 1), ends)
+        for pairing in range(x_pairs):
+            base = rows + y_pairing * slots
+            x_out[pairing][base : base + slots, :] = ends
 
 
 def cross_x(levels, faces, gains, sign):
     rows, lanes = faces.shape
     lane, row = (lanes_of(faces.shape), rows_of(faces.shape))
-    gain = [turn(gains, -(len(laterals) + part), 1) for part in range(3)]
+    gain = [turn(gains, -spot(len(laterals) + part), 1) for part in range(3)]
     total = jnp.zeros_like(faces)
     for kind, (step_y, step_z) in enumerate(laterals):
-        source = turn(faces, -kind - tile * step_z, 1)
+        source = turn(faces, -spot(kind) - tile * step_z, 1)
         pull = sign * gain[0]
         if step_y != 0:
             edge = rows - 1 if step_y > 0 else 0
@@ -357,38 +367,37 @@
         sent = x_sent[pairing][0:rows, :]
         there = cross_x(levels, sent, got, -sign)
         here = cross_x(levels, got, sent, sign)
-        right = jnp.where(lane < filter_reach, turn(got, -spare, 1), 0.0)
-        right = right + jnp.where(lane == 0, there, 0.0)
-        left = jnp.where(lane >= lanes - filter_reach, turn(got, -spare - filter_reach, 1), 0.0)
-        left = left + jnp.where(lane == lanes - 1, there, 0.0)
-        side = side + pick(after, right, left)
+        beyond = jnp.where(after, 0, lanes - filter_reach)
+        chosen = (lane >= beyond) & (lane < beyond + filter_reach)
+        side = side + jnp.where(chosen, turn(got, -spare - filter_reach, 1), 0.0)
+        side = side + jnp.where(lane == jnp.where(after, 0, lanes - 1), there, 0.0)
         edge = jnp.where(after, lanes - 1, 0)
         main = main + jnp.where(lane == edge, here, 0.0)
     middle[0] = main
     middle[1] = side
-    left_ends, right_ends = halves("gx", [got[rows : rows + slots, :] for got in x_got])
     lane = lanes_of((slots, lanes))
-    size = kinds * wide
     for pairing in range(y_pairs):
         after = partner_after("gy", pairing)
         out = y_out[pairing]
         ends = jnp.zeros((slots, lanes), jnp.float32)
         if x_pairs:
-            ends = jnp.where(lane < size, turn(left_ends, -pairing * size, 1), ends)
-            ends = jnp.where(
-                (lane >= size) & (lane < 2 * size), turn(right_ends, size - pairing * size, 1), ends
-            )
-        out[0:slots, :] = ends
-        for number, part in enumerate((main, side)):
-            place = slots + number * tile
-            out[place : place + tile, :] = pick(after, part[rows - tile :], part[0:tile])
+            base = rows + pairing * slots
+            left, right = halves("gx", [got[base : base + slots, :] for got in x_got])
+            ends = jnp.where(lane % both_ends < wide, left, right)
+        beside = turn(pick(after, side[rows - tile :], side[0:tile]), spare_lanes(lanes), 1)
+        used = lane < kinds * both_ends
+        out[0:slots, :] = jnp.where(used, ends, 0.0)
+        out[0:tile, :] = jnp.where(used[0:tile], ends[0:tile], beside)
+        out[slots : slots + tile, :] = pick(after, main[rows - tile :], main[0:tile])
+
+
+def spare_lanes(lanes):
+    assert kinds * both_ends + 2 * filter_reach <= lanes
+    return kinds * both_ends + filter_reach
 
 
 def spread_ends(ends, kind, lanes):
-    lane = lanes_of(ends.shape)
-    size = kinds * wide
-    right = jnp.where(lane < wide, turn(ends, -size - kind * wide, 1), 0.0)
-    return jnp.where(lane >= lanes - wide, turn(ends, -wide - kind * wide, 1), right)
+    return turn(ends, -kind * both_ends - wide, 1)
 
 
 def step_x(main, side, step):
@@ -451,8 +460,9 @@
         edge_here = jnp.where(flag, rows - 1, 0)
         edge_there = jnp.where(flag, 0, tile - 1)
         for part in range(2):
-            place = slots + part * tile
-            sums = got_ends[place : place + tile]
+            sums = got_ends[slots : slots + tile]
+            if part == 1:
+                sums = turn(got_ends[0:tile], -spare_lanes(lanes), 1)
             sums = sums + jnp.where(row_tile == edge_there, there[part], 0.0)
             none = jnp.zeros_like(sums)
             before[part] = before[part] + pick(flag, none, sums)
@@ -525,7 +535,7 @@
                 column = 0.0
                 if x_pairs:
                     kind = crossing(0, step_x_).index(number)
-                    place = (source % slots) * tile + kind
+                    place = (source % slots) * tile + spot(kind)
                     column = turn(halo_x[1 if step_x_ > 0 else 0], edge - place, 1)
                 plane = jnp.where(lane == edge, column, turn(plane, -step_x_, 1))
             if step_y_ != 0:
@@ -689,7 +699,9 @@
         functools.partial(depth_kernel, (x_pairs, y_pairs, z_pairs), levels),
         "add_z_faces",
         [*z_got, *packed],
-        [(rows + slots, lanes)] * x_pairs + [(kinds * slots, lanes)] * y_pairs + [(rows, lanes)],
+        [(rows + y_pairs * slots, lanes)] * x_pairs
+        + [(kinds * slots, lanes)] * y_pairs
+        + [(rows, lanes)],
     )
     x_sent, y_sent, own = (
         filled[:x_pairs],
@@ -704,7 +716,7 @@
         functools.partial(middle_kernel, (x_pairs, y_pairs), levels),
         "add_x_faces",
         [*x_got[::-1], *x_sent, own],
-        [(slots + 2 * tile, lanes)] * y_pairs + [(2, rows, lanes)],
+        [(slots + tile, lanes)] * y_pairs + [(2, rows, lanes)],
     )
     ends_sent, middle = (merged[:y_pairs], merged[y_pairs])
     ends_got = [swap(ends_sent[pairing], "gy", pairing) for pairing in range(y_pairs)]

time: 15.7 us -> 15.6 us (level)
  transfers between devices with their start and end apart: 6 -> 6, of which waited for: 4 -> 4; matrix products, arithmetic and copies ran while one was open for 0% -> 0% of each run, Pallas kernels for 23% -> 22%
where the time goes in v4:
time: 15.6 us; the launch traced here: 15.4 us
  starting transfers between devices  8 us (51%)
  Pallas kernels  5.47 us (35%)
  waiting for transfers between devices  1.12 us (7%)
  between operations  0.72 us (5%)
    ppermute x5, starting transfers between devices, swap(): return lax.ppermute(array, axis, pairs)  7.62 us
    pallas_call x8, Pallas kernels, local_call(): pl.pallas_call(body, out_shape=shapes, in_specs=[far_spec if place in far...  5.47 us
    ppermute x5, waiting for transfers between devices, swap(): return lax.ppermute(array, axis, pairs)  1.11 us
    ppermute x1, starting transfers between devices, swap(): return lax.ppermute(array, (axis, 'depth'), full)  0.38 us
  transfers between devices with their start and end apart: 6, of which 4 were waited for; matrix products, arithmetic and copies ran while one was open for 0% of the time, Pallas kernels for 22%

profile of v4, /device:TPU:0, one launch (start us, length us, event | category | flops | bytes accessed | tf_op | source)
XLA Modules:
  0.0 15.4 jit_solution(7699117807951530937)
XLA Ops:
  0.6 0.0 copy-start
  0.6 0.0 copy-start.2
  0.7 0.0 copy-start.1
  0.7 0.0 copy-start.4
  0.7 0.0 copy-start.3
  0.7 1.0 %depth_faces.1 = f32[5,16,128]{2,1,0:T(8,128)S(1)} custom-call(f32[19,12,16,128]{3,2,1,0:T(8,128)} %adjoint.5), custom_call_target="tpu_custom_call" | custom-call | flops 933888000 | bytes 100000 | tf_op jit(solution)/shard_map/depth_faces/pallas_call | solution.py:660
  1.6 0.5 %collective-permute-start = (f32[5,16,128]{2,1,0:T(8,128)S(1)}, f32[5,16,128]{2,1,0:T(8,128)S(1)}, u32[]{:S(2)}, u32[]{:S(2)}) collective-permute-start(f32[5,16,128]{2,1,0:T(8,128)S(1)} %depth_faces.1), channel_id=1, source_target_pairs={{0,1},{1,0},{2,3},{3,2},{4,5},{5,4},{6,7},{7,6},{8,9},{9,8},{10,11... | collective-permute-start | bytes 122888 | tf_op jit(solution)/shard_map/ppermute | solution.py:78
  2.2 0.0 copy-done
  2.2 0.0 copy-done.2
  2.2 0.0 copy-done.1
  2.2 0.0 copy-done.4
  2.2 0.1 copy-done.3
  2.3 0.5 %pack_faces.1 = (f32[16,128]{1,0:T(8,128)S(1)}, f32[16,128]{1,0:T(8,128)S(1)}, f32[128,128]{1,0:T(8,128)S(1)}, f32[16,128]{1,0:T(8,128)S(1)}, f32[2,3,16,128]{3,2,1,0:T(8,128)S(1)}) custom-call(f32[19,12,16,128]{3,2,1,0:T(8,128)S(1)} %copy-done, f32[3,12,16,128]{3,2,1,0:T(8,128)S(1)} %copy-done.3, f32[16,128]{1,0:T(8,128)S(1)} %copy-done.4, ...), custom_call_target="tpu_custom_call" | custom-call | tf_op jit(solution)/shard_map/pack_faces/pallas_call | solution.py:660
  2.8 0.2 %collective-permute-done.refs_0_.refs_2_ = f32[5,16,128]{2,1,0:T(8,128)S(1)} collective-permute-done((f32[5,16,128]{2,1,0:T(8,128)S(1)}, f32[5,16,128]{2,1,0:T(8,128)S(1)}, u32[]{:S(2)}, u32[]{:S(2)}) %collective-permute-start) | collective-permute-done | bytes 40992 | tf_op jit(solution)/shard_map/ppermute | solution.py:78
  3.0 0.2 %add_z_faces.1 = (f32[32,128]{1,0:T(8,128)S(1)}, f32[32,128]{1,0:T(8,128)S(1)}, f32[128,128]{1,0:T(8,128)S(1)}, f32[16,128]{1,0:T(8,128)S(1)}) custom-call(f32[5,16,128]{2,1,0:T(8,128)S(1)} %collective-permute-done.refs_0_.refs_2_, f32[16,128]{1,0:T(8,128)S(1)} %get-tuple-element.16.refs_1_, f32[16,128]{1,0:T(8,128)S(1)} %get-tuple-element.17.refs_2_, ...), custom_call_target="tpu_custom_call" | custom-call | tf_op jit(solution)/shard_map/add_z_faces/pallas_call | solution.py:660
  3.2 0.4 %collective-permute-start.1 = (f32[32,128]{1,0:T(8,128)S(1)}, f32[32,128]{1,0:T(8,128)S(1)}, u32[]{:S(2)}, u32[]{:S(2)}) collective-permute-start(f32[32,128]{1,0:T(8,128)S(1)} %get-tuple-element.21.refs_3_), channel_id=1, source_target_pairs={{4,8},{5,9},{8,4},{9,5},{12,16},{13,17},{16,12},{17,13},{20,24},{2... | collective-permute-start | bytes 49160 | tf_op jit(solution)/shard_map/ppermute | solution.py:82
  3.6 4.0 %collective-permute-start.2 = (f32[32,128]{1,0:T(8,128)S(1)}, f32[32,128]{1,0:T(8,128)S(1)}, u32[]{:S(2)}, u32[]{:S(2)}) collective-permute-start(f32[32,128]{1,0:T(8,128)S(1)} %get-tuple-element.22.refs_2_), channel_id=1, source_target_pairs={{0,4},{4,0},{8,12},{12,8},{16,20},{20,16},{24,28},{28,24},{1,5},{5... | collective-permute-start | bytes 49160 | tf_op jit(solution)/shard_map/ppermute | solution.py:78
  7.6 1.5 %collective-permute-start.3 = (f32[128,128]{1,0:T(8,128)S(1)}, f32[128,128]{1,0:T(8,128)S(1)}, u32[]{:S(2)}, u32[]{:S(2)}) collective-permute-start(f32[128,128]{1,0:T(8,128)S(1)} %get-tuple-element.25.refs_1_), channel_id=1, source_target_pairs={{0,2},{2,0},{1,3},{3,1},{4,6},{6,4},{5,7},{7,5},{8,10},{10,8},{9,1... | collective-permute-start | bytes 196616 | tf_op jit(solution)/shard_map/ppermute | solution.py:78
  9.1 0.0 collective-permute-done.1.refs_0_
  9.1 0.2 %collective-permute-done.2.refs_1_ = f32[32,128]{1,0:T(8,128)S(1)} collective-permute-done((f32[32,128]{1,0:T(8,128)S(1)}, f32[32,128]{1,0:T(8,128)S(1)}, u32[]{:S(2)}, u32[]{:S(2)}) %collective-permute-start.2) | collective-permute-done | bytes 16416 | tf_op jit(solution)/shard_map/ppermute | solution.py:78
  9.3 0.3 %add_x_faces.1 = (f32[24,128]{1,0:T(8,128)S(1)}, f32[2,16,128]{2,1,0:T(8,128)S(1)}) custom-call(f32[32,128]{1,0:T(8,128)S(1)} %collective-permute-done.1.refs_0_, f32[32,128]{1,0:T(8,128)S(1)} %collective-permute-done.2.refs_1_, f32[32,128]{1,0:T(8,128)S(1)} %get-tuple-element.22.refs_2_, f32[32,128]{1,0:T(8,128)S(1)} %get-tuple-element.21.refs_3_, ...), custom_call_target="tpu_custom_call" | custom-call | tf_op jit(solution)/shard_map/add_x_faces/pallas_call | solution.py:660
  9.6 1.5 %collective-permute-start.4 = (f32[24,128]{1,0:T(8,128)S(1)}, f32[24,128]{1,0:T(8,128)S(1)}, u32[]{:S(2)}, u32[]{:S(2)}) collective-permute-start(f32[24,128]{1,0:T(8,128)S(1)} %get-tuple-element.27.refs_3_), channel_id=1, source_target_pairs={{0,2},{2,0},{1,3},{3,1},{4,6},{6,4},{5,7},{7,5},{8,10},{10,8},{9,1... | collective-permute-start | bytes 36872 | tf_op jit(solution)/shard_map/ppermute | solution.py:78
  11.1 1.8 %collide.1 = (f32[19,12,16,128]{3,2,1,0:T(8,128)}, f32[1,19,12,128]{3,2,1,0:T(8,128)S(1)}, f32[16,128]{1,0:T(8,128)S(1)}) custom-call(f32[19,12,16,128]{3,2,1,0:T(8,128)S(1)} %copy-done, f32[16,128]{1,0:T(8,128)S(1)} %copy-done.4, s32[12,16,128]{2,1,0:T(8,128)S(1)} %copy-done.1, s32[12,16,128]{2,1,0:T(8,128)S(1)} %copy-done.2, ...), custom_call_target="tpu_custom_call" | custom-call | flops 3735552000 | bytes 4000000 | tf_op jit(solution)/shard_map/collide/pallas_call | solution.py:660
  12.9 0.4 %collective-permute-done.4.refs_1_.refs_2_ = f32[24,128]{1,0:T(8,128)S(1)} collective-permute-done((f32[24,128]{1,0:T(8,128)S(1)}, f32[24,128]{1,0:T(8,128)S(1)}, u32[]{:S(2)}, u32[]{:S(2)}) %collective-permute-start.4) | collective-permute-done | bytes 12320 | tf_op jit(solution)/shard_map/ppermute | solution.py:78
  13.3 0.0 collective-permute-done.3.refs_0_
  13.3 0.3 %add_y_faces.1.mine = f32[16,128]{1,0:T(8,128)S(1)} custom-call(f32[128,128]{1,0:T(8,128)S(1)} %collective-permute-done.3.refs_0_, f32[128,128]{1,0:T(8,128)S(1)} %get-tuple-element.25.refs_1_, f32[24,128]{1,0:T(8,128)S(1)} %collective-permute-done.4.refs_1_.refs_2_, f32[24,128]{1,0:T(8,128)S(1)} %get-tuple-element.27.refs_3_, ...), custom_call_target="tpu_custom_call" | custom-call | tf_op jit(solution)/shard_map/add_y_faces/pallas_call | solution.py:660
  13.6 0.1 collective-permute-start.5
  13.7 0.9 %add_y_rows.1 = f32[19,12,16,128]{3,2,1,0:T(8,128)} custom-call(f32[19,12,16,128]{3,2,1,0:T(8,128)} %get-tuple-element.23.new, f32[1,19,12,128]{3,2,1,0:T(8,128)S(1)} %get-tuple-element.24.edge_rows, f32[16,128]{1,0:T(8,128)S(1)} %copy-done.4, s32[12,16,128]{2,1,0:T(8,128)S(1)} %copy-done.1, ...), custom_call_target="tpu_custom_call", output_to_operand_aliasing={{}: (0, {})} | custom-call | tf_op jit(solution)/shard_map/add_y_rows/pallas_call | solution.py:660
  14.6 0.2 %collective-permute-done.5.other = f32[16,128]{1,0:T(8,128)S(1)} collective-permute-done((f32[16,128]{1,0:T(8,128)S(1)}, f32[16,128]{1,0:T(8,128)S(1)}, u32[]{:S(2)}, u32[]{:S(2)}) %collective-permute-start.5) | collective-permute-done | bytes 8224 | tf_op jit(solution)/shard_map/ppermute | solution.py:78
  14.8 0.6 %add_depth.1 = f32[16,128]{1,0:T(8,128)} custom-call(f32[16,128]{1,0:T(8,128)S(1)} %add_y_faces.1.mine, f32[16,128]{1,0:T(8,128)S(1)} %collective-permute-done.5.other), custom_call_target="tpu_custom_call" | custom-call | tf_op jit(solution)/shard_map/add_depth/pallas_call | solution.py:660
Async XLA Ops:
  0.6 1.6 %copy-start = (f32[19,12,16,128]{3,2,1,0:T(8,128)S(1)}, f32[19,12,16,128]{3,2,1,0:T(8,128)}, u32[]{:S(2)}) copy-start(f32[19,12,16,128]{3,2,1,0:T(8,128)} %adjoint.5) | copy-start | bytes 5603332
  0.6 1.6 %copy-start.2 = (s32[12,16,128]{2,1,0:T(8,128)S(1)}, s32[12,16,128]{2,1,0:T(8,128)}, u32[]{:S(2)}) copy-start(s32[12,16,128]{2,1,0:T(8,128)} %port.5) | copy-start | bytes 294916
  0.7 1.5 %copy-start.1 = (s32[12,16,128]{2,1,0:T(8,128)S(1)}, s32[12,16,128]{2,1,0:T(8,128)}, u32[]{:S(2)}) copy-start(s32[12,16,128]{2,1,0:T(8,128)} %solid.5) | copy-start | bytes 294916
  0.7 1.5 %copy-start.4 = (f32[16,128]{1,0:T(8,128)S(1)}, f32[16,128]{1,0:T(8,128)}, u32[]{:S(2)}) copy-start(f32[16,128]{1,0:T(8,128)} %design.5) | copy-start | bytes 24580
  0.7 1.6 %copy-start.3 = (f32[3,12,16,128]{3,2,1,0:T(8,128)S(1)}, f32[3,12,16,128]{3,2,1,0:T(8,128)}, u32[]{:S(2)}) copy-start(f32[3,12,16,128]{3,2,1,0:T(8,128)} %momentum.1) | copy-start | bytes 884740
  1.6 1.4 %collective-permute-start = (f32[5,16,128]{2,1,0:T(8,128)S(1)}, f32[5,16,128]{2,1,0:T(8,128)S(1)}, u32[]{:S(2)}, u32[]{:S(2)}) collective-permute-start(f32[5,16,128]{2,1,0:T(8,128)S(1)} %depth_faces.1), channel_id=1, source_target_pairs={{0,1},{1,0},{2,3},{3,2},{4,5},{5,4},{6,7},{7,6},{8,9},{9,8},{10,11... | collective-permute-start | bytes 122888 | tf_op jit(solution)/shard_map/ppermute | solution.py:78
  3.2 5.9 %collective-permute-start.1 = (f32[32,128]{1,0:T(8,128)S(1)}, f32[32,128]{1,0:T(8,128)S(1)}, u32[]{:S(2)}, u32[]{:S(2)}) collective-permute-start(f32[32,128]{1,0:T(8,128)S(1)} %get-tuple-element.21.refs_3_), channel_id=1, source_target_pairs={{4,8},{5,9},{8,4},{9,5},{12,16},{13,17},{16,12},{17,13},{20,24},{2... | collective-permute-start | bytes 49160 | tf_op jit(solution)/shard_map/ppermute | solution.py:82
  3.6 5.7 %collective-permute-start.2 = (f32[32,128]{1,0:T(8,128)S(1)}, f32[32,128]{1,0:T(8,128)S(1)}, u32[]{:S(2)}, u32[]{:S(2)}) collective-permute-start(f32[32,128]{1,0:T(8,128)S(1)} %get-tuple-element.22.refs_2_), channel_id=1, source_target_pairs={{0,4},{4,0},{8,12},{12,8},{16,20},{20,16},{24,28},{28,24},{1,5},{5... | collective-permute-start | bytes 49160 | tf_op jit(solution)/shard_map/ppermute | solution.py:78
  7.6 5.7 %collective-permute-start.3 = (f32[128,128]{1,0:T(8,128)S(1)}, f32[128,128]{1,0:T(8,128)S(1)}, u32[]{:S(2)}, u32[]{:S(2)}) collective-permute-start(f32[128,128]{1,0:T(8,128)S(1)} %get-tuple-element.25.refs_1_), channel_id=1, source_target_pairs={{0,2},{2,0},{1,3},{3,1},{4,6},{6,4},{5,7},{7,5},{8,10},{10,8},{9,1... | collective-permute-start | bytes 196616 | tf_op jit(solution)/shard_map/ppermute | solution.py:78
  9.6 3.7 %collective-permute-start.4 = (f32[24,128]{1,0:T(8,128)S(1)}, f32[24,128]{1,0:T(8,128)S(1)}, u32[]{:S(2)}, u32[]{:S(2)}) collective-permute-start(f32[24,128]{1,0:T(8,128)S(1)} %get-tuple-element.27.refs_3_), channel_id=1, source_target_pairs={{0,2},{2,0},{1,3},{3,1},{4,6},{6,4},{5,7},{7,5},{8,10},{10,8},{9,1... | collective-permute-start | bytes 36872 | tf_op jit(solution)/shard_map/ppermute | solution.py:78
  13.6 1.2 %collective-permute-start.5 = (f32[16,128]{1,0:T(8,128)S(1)}, f32[16,128]{1,0:T(8,128)S(1)}, u32[]{:S(2)}, u32[]{:S(2)}) collective-permute-start(f32[16,128]{1,0:T(8,128)S(1)} %add_y_faces.1.mine), channel_id=1, source_target_pairs={{0,1},{1,0},{2,3},{3,2},{4,5},{5,4},{6,7},{7,6},{8,9},{9,8},{10,11... | collective-permute-start | bytes 24584 | tf_op jit(solution)/shard_map/ppermute | solution.py:78

commit v5 on v4

--- a/solution.py
+++ b/solution.py
@@ -330,10 +330,10 @@
 
 
 def cross_x(levels, faces, gains, sign):
-    rows, lanes = faces.shape
+    rows = faces.shape[0]
     lane, row = (lanes_of(faces.shape), rows_of(faces.shape))
     gain = [turn(gains, -spot(len(laterals) + part), 1) for part in range(3)]
-    total = jnp.zeros_like(faces)
+    terms = []
     for kind, (step_y, step_z) in enumerate(laterals):
         source = turn(faces, -spot(kind) - tile * step_z, 1)
         pull = sign * gain[0]
@@ -343,9 +343,9 @@
             pull = pull + step_y * gain[1]
         if step_z != 0:
             pull = pull + step_z * gain[2]
-        total = total + lateral_weights[kind] * source * pull
+        terms.append(lateral_weights[kind] * source * pull)
     used = (lane % tile == 0) & (lane < tile * levels)
-    return jnp.sum(jnp.where(used, total, 0.0), axis=1, keepdims=True)
+    return jnp.sum(jnp.where(used, tree_sum(terms), 0.0), axis=1, keepdims=True)
 
 
 def middle_kernel(counts, levels, *refs):
@@ -358,21 +358,26 @@
     slots = lanes // tile
     lane = lanes_of((rows, lanes))
     main = own[...]
-    side = jnp.zeros((rows, lanes), jnp.float32)
+    side, beside = (jnp.zeros((rows, lanes), jnp.float32) for part in range(2))
+    free = spare_lanes(lanes)
     spare = (levels + 1) * tile
-    for pairing in range(x_pairs):
-        after = partner_after("gx", pairing)
-        sign = jnp.where(after, 1.0, -1.0)
-        got = present("gx", pairing, x_got[pairing][0:rows, :])
-        sent = x_sent[pairing][0:rows, :]
-        there = cross_x(levels, sent, got, -sign)
-        here = cross_x(levels, got, sent, sign)
-        beyond = jnp.where(after, 0, lanes - filter_reach)
-        chosen = (lane >= beyond) & (lane < beyond + filter_reach)
-        side = side + jnp.where(chosen, turn(got, -spare - filter_reach, 1), 0.0)
-        side = side + jnp.where(lane == jnp.where(after, 0, lanes - 1), there, 0.0)
-        edge = jnp.where(after, lanes - 1, 0)
-        main = main + jnp.where(lane == edge, here, 0.0)
+    got_left, got_right = halves("gx", [got[0:rows, :] for got in x_got])
+    sent_left, sent_right = halves("gx", [sent[0:rows, :] for sent in x_sent])
+    if x_pairs:
+        there_left = cross_x(levels, sent_left, got_left, 1)
+        there_right = cross_x(levels, sent_right, got_right, -1)
+        here_left = cross_x(levels, got_left, sent_left, -1)
+        here_right = cross_x(levels, got_right, sent_right, 1)
+        main = main + jnp.where(lane == 0, here_left, 0.0)
+        main = main + jnp.where(lane == lanes - 1, here_right, 0.0)
+        sums = jnp.where(lane // filter_reach == spare // filter_reach, got_left, got_right)
+        side = jnp.where(lane == 0, there_right, jnp.where(lane == lanes - 1, there_left, 0.0))
+        chosen = (lane < filter_reach) | (lane >= lanes - filter_reach)
+        side = side + jnp.where(chosen, turn(sums, -spare - filter_reach, 1), 0.0)
+        beside = jnp.where(lane == free, there_right, 0.0)
+        beside = beside + jnp.where(lane == free - 1, there_left, 0.0)
+        chosen = (lane >= free - filter_reach) & (lane < free + filter_reach)
+        beside = beside + jnp.where(chosen, turn(sums, free - spare - filter_reach, 1), 0.0)
     middle[0] = main
     middle[1] = side
     lane = lanes_of((slots, lanes))
@@ -384,43 +389,44 @@
             base = rows + pairing * slots
             left, right = halves("gx", [got[base : base + slots, :] for got in x_got])
             ends = jnp.where(lane % both_ends < wide, left, right)
-        beside = turn(pick(after, side[rows - tile :], side[0:tile]), spare_lanes(lanes), 1)
-        used = lane < kinds * both_ends
-        out[0:slots, :] = jnp.where(used, ends, 0.0)
-        out[0:tile, :] = jnp.where(used[0:tile], ends[0:tile], beside)
+        ends = jnp.where(lane < kinds * both_ends, ends, 0.0)
+        out[0:tile, :] = ends[0:tile] + pick(after, beside[rows - tile :], beside[0:tile])
+        out[tile:slots, :] = ends[tile:]
         out[slots : slots + tile, :] = pick(after, main[rows - tile :], main[0:tile])
 
 
 def spare_lanes(lanes):
-    assert kinds * both_ends + 2 * filter_reach <= lanes
-    return kinds * both_ends + filter_reach
-
-
-def spread_ends(ends, kind, lanes):
-    return turn(ends, -kind * both_ends - wide, 1)
-
-
-def step_x(main, side, step):
+    assert kinds * both_ends + 2 * tile <= lanes and lanes & (lanes - 1) == 0
+    return kinds * both_ends + tile
+
+
+def step_x(line, ends, kind, step):
+    lanes = line.shape[-1]
+    main = turn(line, -step, 1)
+    side = turn(ends, -kind * both_ends - wide - step, 1)
     if step == 0:
         return (main, side)
-    lane = lanes_of(main.shape)
-    edge = lane == (main.shape[-1] - 1 if step > 0 else 0)
-    main, side = (turn(main, -step, 1), turn(side, -step, 1))
+    edge = lanes_of(line.shape) == (lanes - 1 if step > 0 else 0)
     return (jnp.where(edge, side, main), jnp.where(edge, main, side))
 
 
 def cross_y(faces, gains, sign):
+    (lines, ends), (gain_lines, gain_ends) = (faces, gains)
+    gain = [
+        step_x(gain_lines[len(laterals) + part], gain_ends, len(laterals) + part, 0)
+        for part in range(3)
+    ]
     total_main, total_side = (0.0, 0.0)
     for kind, (lateral_x, lateral_z) in enumerate(laterals):
-        main, side = step_x(*faces[kind], lateral_x)
+        main, side = step_x(lines[kind], ends, kind, lateral_x)
         main, side = (turn(main, -lateral_z, 0), turn(side, -lateral_z, 0))
-        pull_main, pull_side = (sign * gains[1][0], sign * gains[1][1])
+        pull_main, pull_side = (sign * gain[1][0], sign * gain[1][1])
         if lateral_x != 0:
-            pull_main = pull_main + lateral_x * gains[0][0]
-            pull_side = pull_side + lateral_x * gains[0][1]
+            pull_main = pull_main + lateral_x * gain[0][0]
+            pull_side = pull_side + lateral_x * gain[0][1]
         if lateral_z != 0:
-            pull_main = pull_main + lateral_z * gains[2][0]
-            pull_side = pull_side + lateral_z * gains[2][1]
+            pull_main = pull_main + lateral_z * gain[2][0]
+            pull_side = pull_side + lateral_z * gain[2][1]
         total_main = total_main + lateral_weights[kind] * main * pull_main
         total_side = total_side + lateral_weights[kind] * side * pull_side
     return (
@@ -429,11 +435,11 @@
     )
 
 
-def face_lines(lines, ends, slots, lanes):
-    return [
-        (lines[kind * slots : (kind + 1) * slots], spread_ends(ends[0:slots], kind, lanes))
-        for kind in range(kinds)
-    ]
+def face_lines(lines, ends, slots):
+    return (
+        [lines[kind * slots : (kind + 1) * slots] for kind in range(kinds)],
+        ends[0:slots],
+    )
 
 
 def extend_kernel(y_pairs, *refs):
@@ -453,10 +459,10 @@
         sign = jnp.where(flag, 1.0, -1.0)
         got_lines = present("gy", pairing, y_got[pairing][...])
         got_ends = present("gy", pairing, ends_got[pairing][...])
-        got = face_lines(got_lines, got_ends, slots, lanes)
-        sent = face_lines(y_sent[pairing][...], ends_sent[pairing][...], slots, lanes)
-        there = cross_y(sent[:5], got[5:], -sign)
-        here = cross_y(got[:5], sent[5:], sign)
+        got = face_lines(got_lines, got_ends, slots)
+        sent = face_lines(y_sent[pairing][...], ends_sent[pairing][...], slots)
+        there = cross_y(sent, got, -sign)
+        here = cross_y(got, sent, sign)
         edge_here = jnp.where(flag, rows - 1, 0)
         edge_there = jnp.where(flag, 0, tile - 1)
         for part in range(2):
@@ -482,16 +488,19 @@
         up = jnp.where(lane < lanes - offset, turn(main, -offset, 1), turn(side, -offset, 1))
         down = jnp.where(lane >= offset, turn(main, offset, 1), turn(side, offset, 1))
         pairs.append(up + down)
-    total = jnp.zeros((rows, lanes), jnp.float32)
+    terms = []
     for offset in range(filter_reach + 1):
-        weighted = jnp.zeros_like(main)
-        for distance, pair in enumerate(pairs):
-            weight = cone(offset, distance)
-            if weight > 0.0:
-                weighted = weighted + weight * pair
+        weights = [cone(offset, distance) for distance in range(filter_reach + 1)]
+        weighted = tree_sum([weight * pair for weight, pair in zip(weights, pairs) if weight > 0.0])
         for step in sorted({offset, -offset}):
-            total = total + turn(weighted, -step, 0)[tile : tile + rows]
-    return total
+            terms.append(turn(weighted, -step, 0)[tile : tile + rows])
+    return tree_sum(terms)
+
+
+def tree_sum(terms):
+    while len(terms) > 1:
+        terms = [sum(terms[place + 1 : place + 2], terms[place]) for place in range(0, len(terms), 2)]
+    return terms[0]
 
 
 def filter_kernel(mine, other, out):
@@ -613,7 +622,7 @@
         for kind, (lateral_x, lateral_z) in enumerate(laterals):
             line = got[kind * slots : (kind + 1) * slots]
             if lateral_x != 0:
-                line = step_x(line, spread_ends(ends, kind, lanes), lateral_x)[0]
+                line = step_x(line, ends, kind, lateral_x)[0]
             line = turn(line, -lateral_z, 0)[0:levels]
             none = jnp.zeros_like(line)
             extra[crossing(1, 1)[kind]] = pick(after, line, none)

time: 15.6 us -> 15.6 us (level)
  Pallas kernels: 5.47 us -> 5.31 us
    pallas_call x8, Pallas kernels: 5.47 us -> 5.31 us  [local_call(): pl.pallas_call(body, out_shape=shapes, in_specs=[far_spec if place in far...]
where the time goes in v5:
time: 15.6 us; the launch traced here: 15.4 us
  starting transfers between devices  8.05 us (52%)
  Pallas kernels  5.31 us (34%)
  waiting for transfers between devices  1.19 us (8%)
  between operations  0.73 us (5%)
    ppermute x5, starting transfers between devices, swap(): return lax.ppermute(array, axis, pairs)  7.67 us
    pallas_call x8, Pallas kernels, local_call(): pl.pallas_call(body, out_shape=shapes, in_specs=[far_spec if place in far...  5.31 us
    ppermute x5, waiting for transfers between devices, swap(): return lax.ppermute(array, axis, pairs)  1.19 us
    ppermute x1, starting transfers between devices, swap(): return lax.ppermute(array, (axis, 'depth'), full)  0.38 us
  transfers between devices with their start and end apart: 6, of which 4 were waited for; matrix products, arithmetic and copies ran while one was open for 0% of the time, Pallas kernels for 22%

profile of v5, /device:TPU:0, one launch (start us, length us, event | category | flops | bytes accessed | tf_op | source)
XLA Modules:
  0.0 15.4 jit_solution(14763731542683989482)
XLA Ops:
  0.6 0.0 copy-start
  0.6 0.0 copy-start.2
  0.7 0.0 copy-start.1
  0.7 0.0 copy-start.4
  0.7 0.0 copy-start.3
  0.7 1.0 %depth_faces.1 = f32[5,16,128]{2,1,0:T(8,128)S(1)} custom-call(f32[19,12,16,128]{3,2,1,0:T(8,128)} %adjoint.5), custom_call_target="tpu_custom_call" | custom-call | flops 933888000 | bytes 100000 | tf_op jit(solution)/shard_map/depth_faces/pallas_call | solution.py:669
  1.6 0.5 %collective-permute-start = (f32[5,16,128]{2,1,0:T(8,128)S(1)}, f32[5,16,128]{2,1,0:T(8,128)S(1)}, u32[]{:S(2)}, u32[]{:S(2)}) collective-permute-start(f32[5,16,128]{2,1,0:T(8,128)S(1)} %depth_faces.1), channel_id=1, source_target_pairs={{0,1},{1,0},{2,3},{3,2},{4,5},{5,4},{6,7},{7,6},{8,9},{9,8},{10,11... | collective-permute-start | bytes 122888 | tf_op jit(solution)/shard_map/ppermute | solution.py:78
  2.2 0.0 copy-done
  2.2 0.0 copy-done.2
  2.2 0.0 copy-done.1
  2.2 0.0 copy-done.4
  2.2 0.1 copy-done.3
  2.3 0.5 %pack_faces.1 = (f32[16,128]{1,0:T(8,128)S(1)}, f32[16,128]{1,0:T(8,128)S(1)}, f32[128,128]{1,0:T(8,128)S(1)}, f32[16,128]{1,0:T(8,128)S(1)}, f32[2,3,16,128]{3,2,1,0:T(8,128)S(1)}) custom-call(f32[19,12,16,128]{3,2,1,0:T(8,128)S(1)} %copy-done, f32[3,12,16,128]{3,2,1,0:T(8,128)S(1)} %copy-done.3, f32[16,128]{1,0:T(8,128)S(1)} %copy-done.4, ...), custom_call_target="tpu_custom_call" | custom-call | tf_op jit(solution)/shard_map/pack_faces/pallas_call | solution.py:669
  2.8 0.2 %collective-permute-done.refs_0_.refs_2_ = f32[5,16,128]{2,1,0:T(8,128)S(1)} collective-permute-done((f32[5,16,128]{2,1,0:T(8,128)S(1)}, f32[5,16,128]{2,1,0:T(8,128)S(1)}, u32[]{:S(2)}, u32[]{:S(2)}) %collective-permute-start) | collective-permute-done | bytes 40992 | tf_op jit(solution)/shard_map/ppermute | solution.py:78
  3.0 0.2 %add_z_faces.1 = (f32[32,128]{1,0:T(8,128)S(1)}, f32[32,128]{1,0:T(8,128)S(1)}, f32[128,128]{1,0:T(8,128)S(1)}, f32[16,128]{1,0:T(8,128)S(1)}) custom-call(f32[5,16,128]{2,1,0:T(8,128)S(1)} %collective-permute-done.refs_0_.refs_2_, f32[16,128]{1,0:T(8,128)S(1)} %get-tuple-element.16.refs_1_, f32[16,128]{1,0:T(8,128)S(1)} %get-tuple-element.17.refs_2_, ...), custom_call_target="tpu_custom_call" | custom-call | tf_op jit(solution)/shard_map/add_z_faces/pallas_call | solution.py:669
  3.2 0.4 %collective-permute-start.1 = (f32[32,128]{1,0:T(8,128)S(1)}, f32[32,128]{1,0:T(8,128)S(1)}, u32[]{:S(2)}, u32[]{:S(2)}) collective-permute-start(f32[32,128]{1,0:T(8,128)S(1)} %get-tuple-element.21.refs_3_), channel_id=1, source_target_pairs={{4,8},{5,9},{8,4},{9,5},{12,16},{13,17},{16,12},{17,13},{20,24},{2... | collective-permute-start | bytes 49160 | tf_op jit(solution)/shard_map/ppermute | solution.py:82
  3.6 4.0 %collective-permute-start.2 = (f32[32,128]{1,0:T(8,128)S(1)}, f32[32,128]{1,0:T(8,128)S(1)}, u32[]{:S(2)}, u32[]{:S(2)}) collective-permute-start(f32[32,128]{1,0:T(8,128)S(1)} %get-tuple-element.22.refs_2_), channel_id=1, source_target_pairs={{0,4},{4,0},{8,12},{12,8},{16,20},{20,16},{24,28},{28,24},{1,5},{5... | collective-permute-start | bytes 49160 | tf_op jit(solution)/shard_map/ppermute | solution.py:78
  7.6 1.5 %collective-permute-start.3 = (f32[128,128]{1,0:T(8,128)S(1)}, f32[128,128]{1,0:T(8,128)S(1)}, u32[]{:S(2)}, u32[]{:S(2)}) collective-permute-start(f32[128,128]{1,0:T(8,128)S(1)} %get-tuple-element.25.refs_1_), channel_id=1, source_target_pairs={{0,2},{2,0},{1,3},{3,1},{4,6},{6,4},{5,7},{7,5},{8,10},{10,8},{9,1... | collective-permute-start | bytes 196616 | tf_op jit(solution)/shard_map/ppermute | solution.py:78
  9.1 0.0 collective-permute-done.1.refs_0_
  9.1 0.2 %collective-permute-done.2.refs_1_ = f32[32,128]{1,0:T(8,128)S(1)} collective-permute-done((f32[32,128]{1,0:T(8,128)S(1)}, f32[32,128]{1,0:T(8,128)S(1)}, u32[]{:S(2)}, u32[]{:S(2)}) %collective-permute-start.2) | collective-permute-done | bytes 16416 | tf_op jit(solution)/shard_map/ppermute | solution.py:78
  9.3 0.2 %add_x_faces.1 = (f32[24,128]{1,0:T(8,128)S(1)}, f32[2,16,128]{2,1,0:T(8,128)S(1)}) custom-call(f32[32,128]{1,0:T(8,128)S(1)} %collective-permute-done.1.refs_0_, f32[32,128]{1,0:T(8,128)S(1)} %collective-permute-done.2.refs_1_, f32[32,128]{1,0:T(8,128)S(1)} %get-tuple-element.22.refs_2_, f32[32,128]{1,0:T(8,128)S(1)} %get-tuple-element.21.refs_3_, ...), custom_call_target="tpu_custom_call" | custom-call | tf_op jit(solution)/shard_map/add_x_faces/pallas_call | solution.py:669
  9.5 1.6 %collective-permute-start.4 = (f32[24,128]{1,0:T(8,128)S(1)}, f32[24,128]{1,0:T(8,128)S(1)}, u32[]{:S(2)}, u32[]{:S(2)}) collective-permute-start(f32[24,128]{1,0:T(8,128)S(1)} %get-tuple-element.27.refs_3_), channel_id=1, source_target_pairs={{0,2},{2,0},{1,3},{3,1},{4,6},{6,4},{5,7},{7,5},{8,10},{10,8},{9,1... | collective-permute-start | bytes 36872 | tf_op jit(solution)/shard_map/ppermute | solution.py:78
  11.1 1.8 %collide.1 = (f32[19,12,16,128]{3,2,1,0:T(8,128)}, f32[1,19,12,128]{3,2,1,0:T(8,128)S(1)}, f32[16,128]{1,0:T(8,128)S(1)}) custom-call(f32[19,12,16,128]{3,2,1,0:T(8,128)S(1)} %copy-done, f32[16,128]{1,0:T(8,128)S(1)} %copy-done.4, s32[12,16,128]{2,1,0:T(8,128)S(1)} %copy-done.1, s32[12,16,128]{2,1,0:T(8,128)S(1)} %copy-done.2, ...), custom_call_target="tpu_custom_call" | custom-call | flops 3735552000 | bytes 4000000 | tf_op jit(solution)/shard_map/collide/pallas_call | solution.py:669
  12.9 0.4 %collective-permute-done.4.refs_1_.refs_2_ = f32[24,128]{1,0:T(8,128)S(1)} collective-permute-done((f32[24,128]{1,0:T(8,128)S(1)}, f32[24,128]{1,0:T(8,128)S(1)}, u32[]{:S(2)}, u32[]{:S(2)}) %collective-permute-start.4) | collective-permute-done | bytes 12320 | tf_op jit(solution)/shard_map/ppermute | solution.py:78
  13.3 0.0 collective-permute-done.3.refs_0_
  13.3 0.2 %add_y_faces.1.mine = f32[16,128]{1,0:T(8,128)S(1)} custom-call(f32[128,128]{1,0:T(8,128)S(1)} %collective-permute-done.3.refs_0_, f32[128,128]{1,0:T(8,128)S(1)} %get-tuple-element.25.refs_1_, f32[24,128]{1,0:T(8,128)S(1)} %collective-permute-done.4.refs_1_.refs_2_, f32[24,128]{1,0:T(8,128)S(1)} %get-tuple-element.27.refs_3_, ...), custom_call_target="tpu_custom_call" | custom-call | tf_op jit(solution)/shard_map/add_y_faces/pallas_call | solution.py:669
  13.6 0.1 collective-permute-start.5
  13.6 0.8 %add_y_rows.1 = f32[19,12,16,128]{3,2,1,0:T(8,128)} custom-call(f32[19,12,16,128]{3,2,1,0:T(8,128)} %get-tuple-element.23.new, f32[1,19,12,128]{3,2,1,0:T(8,128)S(1)} %get-tuple-element.24.edge_rows, f32[16,128]{1,0:T(8,128)S(1)} %copy-done.4, s32[12,16,128]{2,1,0:T(8,128)S(1)} %copy-done.1, ...), custom_call_target="tpu_custom_call", output_to_operand_aliasing={{}: (0, {})} | custom-call | tf_op jit(solution)/shard_map/add_y_rows/pallas_call | solution.py:669
  14.5 0.3 %collective-permute-done.5.other = f32[16,128]{1,0:T(8,128)S(1)} collective-permute-done((f32[16,128]{1,0:T(8,128)S(1)}, f32[16,128]{1,0:T(8,128)S(1)}, u32[]{:S(2)}, u32[]{:S(2)}) %collective-permute-start.5) | collective-permute-done | bytes 8224 | tf_op jit(solution)/shard_map/ppermute | solution.py:78
  14.8 0.6 %add_depth.1 = f32[16,128]{1,0:T(8,128)} custom-call(f32[16,128]{1,0:T(8,128)S(1)} %add_y_faces.1.mine, f32[16,128]{1,0:T(8,128)S(1)} %collective-permute-done.5.other), custom_call_target="tpu_custom_call" | custom-call | tf_op jit(solution)/shard_map/add_depth/pallas_call | solution.py:669
Async XLA Ops:
  0.6 1.6 %copy-start = (f32[19,12,16,128]{3,2,1,0:T(8,128)S(1)}, f32[19,12,16,128]{3,2,1,0:T(8,128)}, u32[]{:S(2)}) copy-start(f32[19,12,16,128]{3,2,1,0:T(8,128)} %adjoint.5) | copy-start | bytes 5603332
  0.6 1.6 %copy-start.2 = (s32[12,16,128]{2,1,0:T(8,128)S(1)}, s32[12,16,128]{2,1,0:T(8,128)}, u32[]{:S(2)}) copy-start(s32[12,16,128]{2,1,0:T(8,128)} %port.5) | copy-start | bytes 294916
  0.7 1.5 %copy-start.1 = (s32[12,16,128]{2,1,0:T(8,128)S(1)}, s32[12,16,128]{2,1,0:T(8,128)}, u32[]{:S(2)}) copy-start(s32[12,16,128]{2,1,0:T(8,128)} %solid.5) | copy-start | bytes 294916
  0.7 1.5 %copy-start.4 = (f32[16,128]{1,0:T(8,128)S(1)}, f32[16,128]{1,0:T(8,128)}, u32[]{:S(2)}) copy-start(f32[16,128]{1,0:T(8,128)} %design.5) | copy-start | bytes 24580
  0.7 1.6 %copy-start.3 = (f32[3,12,16,128]{3,2,1,0:T(8,128)S(1)}, f32[3,12,16,128]{3,2,1,0:T(8,128)}, u32[]{:S(2)}) copy-start(f32[3,12,16,128]{3,2,1,0:T(8,128)} %momentum.1) | copy-start | bytes 884740
  1.6 1.4 %collective-permute-start = (f32[5,16,128]{2,1,0:T(8,128)S(1)}, f32[5,16,128]{2,1,0:T(8,128)S(1)}, u32[]{:S(2)}, u32[]{:S(2)}) collective-permute-start(f32[5,16,128]{2,1,0:T(8,128)S(1)} %depth_faces.1), channel_id=1, source_target_pairs={{0,1},{1,0},{2,3},{3,2},{4,5},{5,4},{6,7},{7,6},{8,9},{9,8},{10,11... | collective-permute-start | bytes 122888 | tf_op jit(solution)/shard_map/ppermute | solution.py:78
  3.2 5.9 %collective-permute-start.1 = (f32[32,128]{1,0:T(8,128)S(1)}, f32[32,128]{1,0:T(8,128)S(1)}, u32[]{:S(2)}, u32[]{:S(2)}) collective-permute-start(f32[32,128]{1,0:T(8,128)S(1)} %get-tuple-element.21.refs_3_), channel_id=1, source_target_pairs={{4,8},{5,9},{8,4},{9,5},{12,16},{13,17},{16,12},{17,13},{20,24},{2... | collective-permute-start | bytes 49160 | tf_op jit(solution)/shard_map/ppermute | solution.py:82
  3.6 5.7 %collective-permute-start.2 = (f32[32,128]{1,0:T(8,128)S(1)}, f32[32,128]{1,0:T(8,128)S(1)}, u32[]{:S(2)}, u32[]{:S(2)}) collective-permute-start(f32[32,128]{1,0:T(8,128)S(1)} %get-tuple-element.22.refs_2_), channel_id=1, source_target_pairs={{0,4},{4,0},{8,12},{12,8},{16,20},{20,16},{24,28},{28,24},{1,5},{5... | collective-permute-start | bytes 49160 | tf_op jit(solution)/shard_map/ppermute | solution.py:78
  7.6 5.7 %collective-permute-start.3 = (f32[128,128]{1,0:T(8,128)S(1)}, f32[128,128]{1,0:T(8,128)S(1)}, u32[]{:S(2)}, u32[]{:S(2)}) collective-permute-start(f32[128,128]{1,0:T(8,128)S(1)} %get-tuple-element.25.refs_1_), channel_id=1, source_target_pairs={{0,2},{2,0},{1,3},{3,1},{4,6},{6,4},{5,7},{7,5},{8,10},{10,8},{9,1... | collective-permute-start | bytes 196616 | tf_op jit(solution)/shard_map/ppermute | solution.py:78
  9.5 3.8 %collective-permute-start.4 = (f32[24,128]{1,0:T(8,128)S(1)}, f32[24,128]{1,0:T(8,128)S(1)}, u32[]{:S(2)}, u32[]{:S(2)}) collective-permute-start(f32[24,128]{1,0:T(8,128)S(1)} %get-tuple-element.27.refs_3_), channel_id=1, source_target_pairs={{0,2},{2,0},{1,3},{3,1},{4,6},{6,4},{5,7},{7,5},{8,10},{10,8},{9,1... | collective-permute-start | bytes 36872 | tf_op jit(solution)/shard_map/ppermute | solution.py:78
  13.6 1.2 %collective-permute-start.5 = (f32[16,128]{1,0:T(8,128)S(1)}, f32[16,128]{1,0:T(8,128)S(1)}, u32[]{:S(2)}, u32[]{:S(2)}) collective-permute-start(f32[16,128]{1,0:T(8,128)S(1)} %add_y_faces.1.mine), channel_id=1, source_target_pairs={{0,1},{1,0},{2,3},{3,2},{4,5},{5,4},{6,7},{7,6},{8,9},{9,8},{10,11... | collective-permute-start | bytes 24584 | tf_op jit(solution)/shard_map/ppermute | solution.py:78

commit v6 on v5

--- a/solution.py
+++ b/solution.py
@@ -48,6 +48,10 @@
     return 2 * kind + 1 if kind < kinds // 2 else 2 * kind - kinds
 
 
+def x_lane(level, kind):
+    return (level + 1) * tile + tile // 2 + spot(kind)
+
+
 def crossing(axis, sign):
     others = [other for other in range(3) if other != axis]
     return [
@@ -208,7 +212,7 @@
     own_out, edge_gain = refs
     levels, rows, lanes = adjoint.shape[1:]
     slots = lanes // tile
-    assert levels + 3 <= slots
+    assert levels + 3 <= slots and 2 * filter_reach <= tile
     scale = 6.0 * damp_top / ((1.0 + design[...]) * (1.0 + design[...]))
     lane = lanes_of((rows, lanes))
     for pairing in range(y_pairs):
@@ -241,7 +245,7 @@
                 plane = jnp.where(lane == lanes - 1, last, first)
             else:
                 plane = gain[kind - len(laterals)]
-            half, place = (kind // (kinds // 2), level * tile + 2 * (kind % (kinds // 2)))
+            half, place = (kind // (kinds // 2), x_lane(level, kind) // 2 * 2)
             chosen = lane // 2 == place // 2
             joint[half] = jnp.where(chosen, turn(plane, place + 1, 1), joint[half])
     for pairing in range(y_pairs):
@@ -300,9 +304,8 @@
                 y_out[pairing][place : place + 1, :] = pick(
                     after, last[rows - 1 : rows], first[0:1]
                 )
-    spare = (levels + 1) * tile
-    chosen = (lane >= spare) & (lane < spare + 2 * filter_reach)
-    sums = jnp.where(chosen, turn(total, spare + filter_reach, 1), 0.0)
+    chosen = (lane < filter_reach) | (lane >= lanes - filter_reach)
+    sums = jnp.where(chosen, total, 0.0)
     packs = []
     for edge_shift, sign in ((0, 1), (1, -1)):
         pack = sums
@@ -310,7 +313,7 @@
             for kind, level, side in beyond:
                 planes = crossing(2, 1 if side else -1)
                 plane = halo[side][planes.index(crossing(0, sign)[kind])]
-                place = (level % slots) * tile + spot(kind)
+                place = x_lane(level, kind)
                 pack = jnp.where(lane == place, turn(plane, place + edge_shift, 1), pack)
         packs.append(pack)
     for pairing in range(x_pairs):
@@ -332,6 +335,7 @@
 def cross_x(levels, faces, gains, sign):
     rows = faces.shape[0]
     lane, row = (lanes_of(faces.shape), rows_of(faces.shape))
+    first = x_lane(0, 0) - spot(0)
     gain = [turn(gains, -spot(len(laterals) + part), 1) for part in range(3)]
     terms = []
     for kind, (step_y, step_z) in enumerate(laterals):
@@ -344,7 +348,7 @@
         if step_z != 0:
             pull = pull + step_z * gain[2]
         terms.append(lateral_weights[kind] * source * pull)
-    used = (lane % tile == 0) & (lane < tile * levels)
+    used = (lane % tile == first % tile) & (lane >= first) & (lane < first + tile * levels)
     return jnp.sum(jnp.where(used, tree_sum(terms), 0.0), axis=1, keepdims=True)
 
 
@@ -360,7 +364,6 @@
     main = own[...]
     side, beside = (jnp.zeros((rows, lanes), jnp.float32) for part in range(2))
     free = spare_lanes(lanes)
-    spare = (levels + 1) * tile
     got_left, got_right = halves("gx", [got[0:rows, :] for got in x_got])
     sent_left, sent_right = halves("gx", [sent[0:rows, :] for sent in x_sent])
     if x_pairs:
@@ -370,14 +373,14 @@
         here_right = cross_x(levels, got_right, sent_right, 1)
         main = main + jnp.where(lane == 0, here_left, 0.0)
         main = main + jnp.where(lane == lanes - 1, here_right, 0.0)
-        sums = jnp.where(lane // filter_reach == spare // filter_reach, got_left, got_right)
+        sums = jnp.where(lane < filter_reach, got_right, got_left)
         side = jnp.where(lane == 0, there_right, jnp.where(lane == lanes - 1, there_left, 0.0))
         chosen = (lane < filter_reach) | (lane >= lanes - filter_reach)
-        side = side + jnp.where(chosen, turn(sums, -spare - filter_reach, 1), 0.0)
+        side = side + jnp.where(chosen, sums, 0.0)
         beside = jnp.where(lane == free, there_right, 0.0)
         beside = beside + jnp.where(lane == free - 1, there_left, 0.0)
         chosen = (lane >= free - filter_reach) & (lane < free + filter_reach)
-        beside = beside + jnp.where(chosen, turn(sums, free - spare - filter_reach, 1), 0.0)
+        beside = beside + jnp.where(chosen, turn(sums, free, 1), 0.0)
     middle[0] = main
     middle[1] = side
     lane = lanes_of((slots, lanes))
@@ -544,8 +547,8 @@
                 column = 0.0
                 if x_pairs:
                     kind = crossing(0, step_x_).index(number)
-                    place = (source % slots) * tile + spot(kind)
-                    column = turn(halo_x[1 if step_x_ > 0 else 0], edge - place, 1)
+                    side = halo_x[1 if step_x_ > 0 else 0]
+                    column = turn(side, edge - x_lane(source, kind), 1)
                 plane = jnp.where(lane == edge, column, turn(plane, -step_x_, 1))
             if step_y_ != 0:
                 plane = along_y(plane, step_y_)

time: 15.6 us -> 15.5 us (level)
  no operation moved by 1% of the time
where the time goes in v6:
time: 15.5 us; the launch traced here: 15.4 us
  starting transfers between devices  8.08 us (52%)
  Pallas kernels  5.25 us (34%)
  waiting for transfers between devices  1.19 us (8%)
  between operations  0.73 us (5%)
    ppermute x5, starting transfers between devices, swap(): return lax.ppermute(array, axis, pairs)  7.67 us
    pallas_call x8, Pallas kernels, local_call(): pl.pallas_call(body, out_shape=shapes, in_specs=[far_spec if place in far...  5.25 us
    ppermute x5, waiting for transfers between devices, swap(): return lax.ppermute(array, axis, pairs)  1.19 us
    ppermute x1, starting transfers between devices, swap(): return lax.ppermute(array, (axis, 'depth'), full)  0.41 us
  transfers between devices with their start and end apart: 6, of which 4 were waited for; matrix products, arithmetic and copies ran while one was open for 0% of the time, Pallas kernels for 22%

profile of v6, /device:TPU:0, one launch (start us, length us, event | category | flops | bytes accessed | tf_op | source)
XLA Modules:
  0.0 15.4 jit_solution(2926886122978755953)
XLA Ops:
  0.6 0.0 copy-start
  0.6 0.0 copy-start.2
  0.7 0.0 copy-start.1
  0.7 0.0 copy-start.4
  0.7 0.0 copy-start.3
  0.7 1.0 %depth_faces.1 = f32[5,16,128]{2,1,0:T(8,128)S(1)} custom-call(f32[19,12,16,128]{3,2,1,0:T(8,128)} %adjoint.5), custom_call_target="tpu_custom_call" | custom-call | flops 933888000 | bytes 100000 | tf_op jit(solution)/shard_map/depth_faces/pallas_call | solution.py:672
  1.6 0.5 %collective-permute-start = (f32[5,16,128]{2,1,0:T(8,128)S(1)}, f32[5,16,128]{2,1,0:T(8,128)S(1)}, u32[]{:S(2)}, u32[]{:S(2)}) collective-permute-start(f32[5,16,128]{2,1,0:T(8,128)S(1)} %depth_faces.1), channel_id=1, source_target_pairs={{0,1},{1,0},{2,3},{3,2},{4,5},{5,4},{6,7},{7,6},{8,9},{9,8},{10,11... | collective-permute-start | bytes 122888 | tf_op jit(solution)/shard_map/ppermute | solution.py:82
  2.2 0.0 copy-done
  2.2 0.0 copy-done.2
  2.2 0.0 copy-done.1
  2.2 0.0 copy-done.4
  2.2 0.1 copy-done.3
  2.3 0.5 %pack_faces.1 = (f32[16,128]{1,0:T(8,128)S(1)}, f32[16,128]{1,0:T(8,128)S(1)}, f32[128,128]{1,0:T(8,128)S(1)}, f32[16,128]{1,0:T(8,128)S(1)}, f32[2,3,16,128]{3,2,1,0:T(8,128)S(1)}) custom-call(f32[19,12,16,128]{3,2,1,0:T(8,128)S(1)} %copy-done, f32[3,12,16,128]{3,2,1,0:T(8,128)S(1)} %copy-done.3, f32[16,128]{1,0:T(8,128)S(1)} %copy-done.4, ...), custom_call_target="tpu_custom_call" | custom-call | tf_op jit(solution)/shard_map/pack_faces/pallas_call | solution.py:672
  2.8 0.2 %collective-permute-done.refs_0_.refs_2_ = f32[5,16,128]{2,1,0:T(8,128)S(1)} collective-permute-done((f32[5,16,128]{2,1,0:T(8,128)S(1)}, f32[5,16,128]{2,1,0:T(8,128)S(1)}, u32[]{:S(2)}, u32[]{:S(2)}) %collective-permute-start) | collective-permute-done | bytes 40992 | tf_op jit(solution)/shard_map/ppermute | solution.py:82
  3.0 0.1 add_z_faces.1
  3.1 0.4 %collective-permute-start.1 = (f32[32,128]{1,0:T(8,128)S(1)}, f32[32,128]{1,0:T(8,128)S(1)}, u32[]{:S(2)}, u32[]{:S(2)}) collective-permute-start(f32[32,128]{1,0:T(8,128)S(1)} %get-tuple-element.21.refs_3_), channel_id=1, source_target_pairs={{4,8},{5,9},{8,4},{9,5},{12,16},{13,17},{16,12},{17,13},{20,24},{2... | collective-permute-start | bytes 49160 | tf_op jit(solution)/shard_map/ppermute | solution.py:86
  3.6 4.0 %collective-permute-start.2 = (f32[32,128]{1,0:T(8,128)S(1)}, f32[32,128]{1,0:T(8,128)S(1)}, u32[]{:S(2)}, u32[]{:S(2)}) collective-permute-start(f32[32,128]{1,0:T(8,128)S(1)} %get-tuple-element.22.refs_2_), channel_id=1, source_target_pairs={{0,4},{4,0},{8,12},{12,8},{16,20},{20,16},{24,28},{28,24},{1,5},{5... | collective-permute-start | bytes 49160 | tf_op jit(solution)/shard_map/ppermute | solution.py:82
  7.6 1.5 %collective-permute-start.3 = (f32[128,128]{1,0:T(8,128)S(1)}, f32[128,128]{1,0:T(8,128)S(1)}, u32[]{:S(2)}, u32[]{:S(2)}) collective-permute-start(f32[128,128]{1,0:T(8,128)S(1)} %get-tuple-element.25.refs_1_), channel_id=1, source_target_pairs={{0,2},{2,0},{1,3},{3,1},{4,6},{6,4},{5,7},{7,5},{8,10},{10,8},{9,1... | collective-permute-start | bytes 196616 | tf_op jit(solution)/shard_map/ppermute | solution.py:82
  9.1 0.0 collective-permute-done.1.refs_0_
  9.1 0.2 %collective-permute-done.2.refs_1_ = f32[32,128]{1,0:T(8,128)S(1)} collective-permute-done((f32[32,128]{1,0:T(8,128)S(1)}, f32[32,128]{1,0:T(8,128)S(1)}, u32[]{:S(2)}, u32[]{:S(2)}) %collective-permute-start.2) | collective-permute-done | bytes 16416 | tf_op jit(solution)/shard_map/ppermute | solution.py:82
  9.3 0.2 %add_x_faces.1 = (f32[24,128]{1,0:T(8,128)S(1)}, f32[2,16,128]{2,1,0:T(8,128)S(1)}) custom-call(f32[32,128]{1,0:T(8,128)S(1)} %collective-permute-done.1.refs_0_, f32[32,128]{1,0:T(8,128)S(1)} %collective-permute-done.2.refs_1_, f32[32,128]{1,0:T(8,128)S(1)} %get-tuple-element.22.refs_2_, f32[32,128]{1,0:T(8,128)S(1)} %get-tuple-element.21.refs_3_, ...), custom_call_target="tpu_custom_call" | custom-call | tf_op jit(solution)/shard_map/add_x_faces/pallas_call | solution.py:672
  9.5 1.6 %collective-permute-start.4 = (f32[24,128]{1,0:T(8,128)S(1)}, f32[24,128]{1,0:T(8,128)S(1)}, u32[]{:S(2)}, u32[]{:S(2)}) collective-permute-start(f32[24,128]{1,0:T(8,128)S(1)} %get-tuple-element.27.refs_3_), channel_id=1, source_target_pairs={{0,2},{2,0},{1,3},{3,1},{4,6},{6,4},{5,7},{7,5},{8,10},{10,8},{9,1... | collective-permute-start | bytes 36872 | tf_op jit(solution)/shard_map/ppermute | solution.py:82
  11.1 1.8 %collide.1 = (f32[19,12,16,128]{3,2,1,0:T(8,128)}, f32[1,19,12,128]{3,2,1,0:T(8,128)S(1)}, f32[16,128]{1,0:T(8,128)S(1)}) custom-call(f32[19,12,16,128]{3,2,1,0:T(8,128)S(1)} %copy-done, f32[16,128]{1,0:T(8,128)S(1)} %copy-done.4, s32[12,16,128]{2,1,0:T(8,128)S(1)} %copy-done.1, s32[12,16,128]{2,1,0:T(8,128)S(1)} %copy-done.2, ...), custom_call_target="tpu_custom_call" | custom-call | flops 3735552000 | bytes 4000000 | tf_op jit(solution)/shard_map/collide/pallas_call | solution.py:672
  12.9 0.4 %collective-permute-done.4.refs_1_.refs_2_ = f32[24,128]{1,0:T(8,128)S(1)} collective-permute-done((f32[24,128]{1,0:T(8,128)S(1)}, f32[24,128]{1,0:T(8,128)S(1)}, u32[]{:S(2)}, u32[]{:S(2)}) %collective-permute-start.4) | collective-permute-done | bytes 12320 | tf_op jit(solution)/shard_map/ppermute | solution.py:82
  13.3 0.0 collective-permute-done.3.refs_0_
  13.3 0.2 %add_y_faces.1.mine = f32[16,128]{1,0:T(8,128)S(1)} custom-call(f32[128,128]{1,0:T(8,128)S(1)} %collective-permute-done.3.refs_0_, f32[128,128]{1,0:T(8,128)S(1)} %get-tuple-element.25.refs_1_, f32[24,128]{1,0:T(8,128)S(1)} %collective-permute-done.4.refs_1_.refs_2_, f32[24,128]{1,0:T(8,128)S(1)} %get-tuple-element.27.refs_3_, ...), custom_call_target="tpu_custom_call" | custom-call | tf_op jit(solution)/shard_map/add_y_faces/pallas_call | solution.py:672
  13.5 0.1 collective-permute-start.5
  13.6 0.8 %add_y_rows.1 = f32[19,12,16,128]{3,2,1,0:T(8,128)} custom-call(f32[19,12,16,128]{3,2,1,0:T(8,128)} %get-tuple-element.23.new, f32[1,19,12,128]{3,2,1,0:T(8,128)S(1)} %get-tuple-element.24.edge_rows, f32[16,128]{1,0:T(8,128)S(1)} %copy-done.4, s32[12,16,128]{2,1,0:T(8,128)S(1)} %copy-done.1, ...), custom_call_target="tpu_custom_call", output_to_operand_aliasing={{}: (0, {})} | custom-call | tf_op jit(solution)/shard_map/add_y_rows/pallas_call | solution.py:672
  14.5 0.3 %collective-permute-done.5.other = f32[16,128]{1,0:T(8,128)S(1)} collective-permute-done((f32[16,128]{1,0:T(8,128)S(1)}, f32[16,128]{1,0:T(8,128)S(1)}, u32[]{:S(2)}, u32[]{:S(2)}) %collective-permute-start.5) | collective-permute-done | bytes 8224 | tf_op jit(solution)/shard_map/ppermute | solution.py:82
  14.8 0.6 %add_depth.1 = f32[16,128]{1,0:T(8,128)} custom-call(f32[16,128]{1,0:T(8,128)S(1)} %add_y_faces.1.mine, f32[16,128]{1,0:T(8,128)S(1)} %collective-permute-done.5.other), custom_call_target="tpu_custom_call" | custom-call | tf_op jit(solution)/shard_map/add_depth/pallas_call | solution.py:672
Async XLA Ops:
  0.6 1.6 %copy-start = (f32[19,12,16,128]{3,2,1,0:T(8,128)S(1)}, f32[19,12,16,128]{3,2,1,0:T(8,128)}, u32[]{:S(2)}) copy-start(f32[19,12,16,128]{3,2,1,0:T(8,128)} %adjoint.5) | copy-start | bytes 5603332
  0.6 1.6 %copy-start.2 = (s32[12,16,128]{2,1,0:T(8,128)S(1)}, s32[12,16,128]{2,1,0:T(8,128)}, u32[]{:S(2)}) copy-start(s32[12,16,128]{2,1,0:T(8,128)} %port.5) | copy-start | bytes 294916
  0.7 1.5 %copy-start.1 = (s32[12,16,128]{2,1,0:T(8,128)S(1)}, s32[12,16,128]{2,1,0:T(8,128)}, u32[]{:S(2)}) copy-start(s32[12,16,128]{2,1,0:T(8,128)} %solid.5) | copy-start | bytes 294916
  0.7 1.5 %copy-start.4 = (f32[16,128]{1,0:T(8,128)S(1)}, f32[16,128]{1,0:T(8,128)}, u32[]{:S(2)}) copy-start(f32[16,128]{1,0:T(8,128)} %design.5) | copy-start | bytes 24580
  0.7 1.6 %copy-start.3 = (f32[3,12,16,128]{3,2,1,0:T(8,128)S(1)}, f32[3,12,16,128]{3,2,1,0:T(8,128)}, u32[]{:S(2)}) copy-start(f32[3,12,16,128]{3,2,1,0:T(8,128)} %momentum.1) | copy-start | bytes 884740
  1.6 1.4 %collective-permute-start = (f32[5,16,128]{2,1,0:T(8,128)S(1)}, f32[5,16,128]{2,1,0:T(8,128)S(1)}, u32[]{:S(2)}, u32[]{:S(2)}) collective-permute-start(f32[5,16,128]{2,1,0:T(8,128)S(1)} %depth_faces.1), channel_id=1, source_target_pairs={{0,1},{1,0},{2,3},{3,2},{4,5},{5,4},{6,7},{7,6},{8,9},{9,8},{10,11... | collective-permute-start | bytes 122888 | tf_op jit(solution)/shard_map/ppermute | solution.py:82
  3.1 5.9 %collective-permute-start.1 = (f32[32,128]{1,0:T(8,128)S(1)}, f32[32,128]{1,0:T(8,128)S(1)}, u32[]{:S(2)}, u32[]{:S(2)}) collective-permute-start(f32[32,128]{1,0:T(8,128)S(1)} %get-tuple-element.21.refs_3_), channel_id=1, source_target_pairs={{4,8},{5,9},{8,4},{9,5},{12,16},{13,17},{16,12},{17,13},{20,24},{2... | collective-permute-start | bytes 49160 | tf_op jit(solution)/shard_map/ppermute | solution.py:86
  3.6 5.7 %collective-permute-start.2 = (f32[32,128]{1,0:T(8,128)S(1)}, f32[32,128]{1,0:T(8,128)S(1)}, u32[]{:S(2)}, u32[]{:S(2)}) collective-permute-start(f32[32,128]{1,0:T(8,128)S(1)} %get-tuple-element.22.refs_2_), channel_id=1, source_target_pairs={{0,4},{4,0},{8,12},{12,8},{16,20},{20,16},{24,28},{28,24},{1,5},{5... | collective-permute-start | bytes 49160 | tf_op jit(solution)/shard_map/ppermute | solution.py:82
  7.6 5.7 %collective-permute-start.3 = (f32[128,128]{1,0:T(8,128)S(1)}, f32[128,128]{1,0:T(8,128)S(1)}, u32[]{:S(2)}, u32[]{:S(2)}) collective-permute-start(f32[128,128]{1,0:T(8,128)S(1)} %get-tuple-element.25.refs_1_), channel_id=1, source_target_pairs={{0,2},{2,0},{1,3},{3,1},{4,6},{6,4},{5,7},{7,5},{8,10},{10,8},{9,1... | collective-permute-start | bytes 196616 | tf_op jit(solution)/shard_map/ppermute | solution.py:82
  9.5 3.8 %collective-permute-start.4 = (f32[24,128]{1,0:T(8,128)S(1)}, f32[24,128]{1,0:T(8,128)S(1)}, u32[]{:S(2)}, u32[]{:S(2)}) collective-permute-start(f32[24,128]{1,0:T(8,128)S(1)} %get-tuple-element.27.refs_3_), channel_id=1, source_target_pairs={{0,2},{2,0},{1,3},{3,1},{4,6},{6,4},{5,7},{7,5},{8,10},{10,8},{9,1... | collective-permute-start | bytes 36872 | tf_op jit(solution)/shard_map/ppermute | solution.py:82
  13.5 1.2 %collective-permute-start.5 = (f32[16,128]{1,0:T(8,128)S(1)}, f32[16,128]{1,0:T(8,128)S(1)}, u32[]{:S(2)}, u32[]{:S(2)}) collective-permute-start(f32[16,128]{1,0:T(8,128)S(1)} %add_y_faces.1.mine), channel_id=1, source_target_pairs={{0,1},{1,0},{2,3},{3,2},{4,5},{5,4},{6,7},{7,6},{8,9},{9,8},{10,11... | collective-permute-start | bytes 24584 | tf_op jit(solution)/shard_map/ppermute | solution.py:82

commit v7 on v6

--- a/solution.py
+++ b/solution.py
@@ -212,7 +212,7 @@
     own_out, edge_gain = refs
     levels, rows, lanes = adjoint.shape[1:]
     slots = lanes // tile
-    assert levels + 3 <= slots and 2 * filter_reach <= tile
+    assert levels + 3 <= slots == 2 * tile and 2 * filter_reach <= tile
     scale = 6.0 * damp_top / ((1.0 + design[...]) * (1.0 + design[...]))
     lane = lanes_of((rows, lanes))
     for pairing in range(y_pairs):
@@ -293,7 +293,8 @@
     beyond = ((3, levels, 1), (4, -1, 0))
     for pairing in range(y_pairs):
         after = partner_after("gy", pairing)
-        y_out[pairing][...] = y_pack[pairing][...]
+        y_out[pairing][0 : kinds * slots, :] = y_pack[pairing][...]
+        y_out[pairing][kinds * slots :, :] = pick(after, total[rows - tile :], total[0:tile])
         if z_pairs:
             for kind, level, side in beyond:
                 planes = crossing(2, 1 if side else -1)
@@ -319,17 +320,22 @@
     for pairing in range(x_pairs):
         after = partner_after("gx", pairing)
         x_out[pairing][0:rows, :] = x_pack[pairing][...] + pick(after, packs[1], packs[0])
-    lane = lanes_of((slots, lanes))
+    lane = lanes_of((tile, lanes))
     for y_pairing in range(y_pairs):
-        ends = jnp.zeros((slots, lanes), jnp.float32)
+        first, last = (jnp.zeros((tile, lanes), jnp.float32) for side in range(2))
         for kind in range(kinds):
             line = y_out[y_pairing][kind * slots : (kind + 1) * slots, :]
+            upper, lower = (line[0:tile], line[tile:])
             place = kind * both_ends
-            chosen = (lane >= place) & (lane < place + both_ends)
-            ends = jnp.where(chosen, turn(line, place + wide, 1), ends)
+            low = (lane >= place) & (lane < place + wide)
+            high = (lane >= place + wide) & (lane < place + both_ends)
+            upper = turn(upper, place + wide, 1)
+            last = jnp.where(low, upper, jnp.where(high, turn(lower, place + both_ends, 1), last))
+            first = jnp.where(high, upper, jnp.where(low, turn(lower, place, 1), first))
+        base = rows + y_pairing * tile
         for pairing in range(x_pairs):
-            base = rows + y_pairing * slots
-            x_out[pairing][base : base + slots, :] = ends
+            after = partner_after("gx", pairing)
+            x_out[pairing][base : base + tile, :] = pick(after, last, first)
 
 
 def cross_x(levels, faces, gains, sign):
@@ -364,6 +370,7 @@
     main = own[...]
     side, beside = (jnp.zeros((rows, lanes), jnp.float32) for part in range(2))
     free = spare_lanes(lanes)
+    within = free + 2 * tile
     got_left, got_right = halves("gx", [got[0:rows, :] for got in x_got])
     sent_left, sent_right = halves("gx", [sent[0:rows, :] for sent in x_sent])
     if x_pairs:
@@ -379,6 +386,8 @@
         side = side + jnp.where(chosen, sums, 0.0)
         beside = jnp.where(lane == free, there_right, 0.0)
         beside = beside + jnp.where(lane == free - 1, there_left, 0.0)
+        beside = beside + jnp.where(lane == within, here_left, 0.0)
+        beside = beside + jnp.where(lane == within - 1, here_right, 0.0)
         chosen = (lane >= free - filter_reach) & (lane < free + filter_reach)
         beside = beside + jnp.where(chosen, turn(sums, free, 1), 0.0)
     middle[0] = main
@@ -389,17 +398,19 @@
         out = y_out[pairing]
         ends = jnp.zeros((slots, lanes), jnp.float32)
         if x_pairs:
-            base = rows + pairing * slots
-            left, right = halves("gx", [got[base : base + slots, :] for got in x_got])
-            ends = jnp.where(lane % both_ends < wide, left, right)
+            base = rows + pairing * tile
+            left, right = halves("gx", [got[base : base + tile, :] for got in x_got])
+            low = lane[0:tile] % both_ends < wide
+            upper = jnp.where(low, left, right)
+            lower = jnp.where(low, turn(left, -wide, 1), turn(right, wide, 1))
+            ends = jnp.concatenate([upper, lower], axis=0)
         ends = jnp.where(lane < kinds * both_ends, ends, 0.0)
         out[0:tile, :] = ends[0:tile] + pick(after, beside[rows - tile :], beside[0:tile])
         out[tile:slots, :] = ends[tile:]
-        out[slots : slots + tile, :] = pick(after, main[rows - tile :], main[0:tile])
 
 
 def spare_lanes(lanes):
-    assert kinds * both_ends + 2 * tile <= lanes and lanes & (lanes - 1) == 0
+    assert kinds * both_ends + 4 * tile <= lanes and lanes & (lanes - 1) == 0
     return kinds * both_ends + tile
 
 
@@ -453,7 +464,11 @@
     middle, norm, out = refs
     rows, lanes = middle.shape[1:]
     slots = lanes // tile
-    row, row_tile = (rows_of((rows, lanes)), rows_of((tile, lanes)))
+    row, row_tile, lane_tile = (
+        rows_of((rows, lanes)),
+        rows_of((tile, lanes)),
+        lanes_of((tile, lanes)),
+    )
     own = [middle[0], middle[1]]
     before = [jnp.zeros((tile, lanes), jnp.float32) for part in range(2)]
     after = [jnp.zeros((tile, lanes), jnp.float32) for part in range(2)]
@@ -469,8 +484,11 @@
         edge_here = jnp.where(flag, rows - 1, 0)
         edge_there = jnp.where(flag, 0, tile - 1)
         for part in range(2):
-            sums = got_ends[slots : slots + tile]
-            if part == 1:
+            if part == 0:
+                within = turn(got_ends[0:tile], -spare_lanes(lanes) - 2 * tile, 1)
+                edge = (lane_tile == 0) | (lane_tile == lanes - 1)
+                sums = got_lines[kinds * slots :] + jnp.where(edge, within, 0.0)
+            else:
                 sums = turn(got_ends[0:tile], -spare_lanes(lanes), 1)
             sums = sums + jnp.where(row_tile == edge_there, there[part], 0.0)
             none = jnp.zeros_like(sums)
@@ -711,8 +729,8 @@
         functools.partial(depth_kernel, (x_pairs, y_pairs, z_pairs), levels),
         "add_z_faces",
         [*z_got, *packed],
-        [(rows + y_pairs * slots, lanes)] * x_pairs
-        + [(kinds * slots, lanes)] * y_pairs
+        [(rows + y_pairs * tile, lanes)] * x_pairs
+        + [(kinds * slots + tile, lanes)] * y_pairs
         + [(rows, lanes)],
     )
     x_sent, y_sent, own = (
@@ -728,7 +746,7 @@
         functools.partial(middle_kernel, (x_pairs, y_pairs), levels),
         "add_x_faces",
         [*x_got[::-1], *x_sent, own],
-        [(slots + tile, lanes)] * y_pairs + [(2, rows, lanes)],
+        [(slots, lanes)] * y_pairs + [(2, rows, lanes)],
     )
     ends_sent, middle = (merged[:y_pairs], merged[y_pairs])
     ends_got = [swap(ends_sent[pairing], "gy", pairing) for pairing in range(y_pairs)]

time: 15.5 us -> 15.5 us (level)
  no operation moved by 1% of the time
where the time goes in v7:
time: 15.5 us; the launch traced here: 15.3 us
  starting transfers between devices  8.09 us (52%)
  Pallas kernels  5.27 us (34%)
  waiting for transfers between devices  1.1 us (7%)
  between operations  0.73 us (5%)
    ppermute x5, starting transfers between devices, swap(): return lax.ppermute(array, axis, pairs)  7.67 us
    pallas_call x8, Pallas kernels, local_call(): pl.pallas_call(body, out_shape=shapes, in_specs=[far_spec if place in far...  5.27 us
    ppermute x5, waiting for transfers between devices, swap(): return lax.ppermute(array, axis, pairs)  1.1 us
    ppermute x1, starting transfers between devices, swap(): return lax.ppermute(array, (axis, 'depth'), full)  0.42 us
  transfers between devices with their start and end apart: 6, of which 4 were waited for; matrix products, arithmetic and copies ran while one was open for 0% of the time, Pallas kernels for 22%

profile of v7, /device:TPU:0, one launch (start us, length us, event | category | flops | bytes accessed | tf_op | source)
XLA Modules:
  0.0 15.3 jit_solution(13833449367141288899)
XLA Ops:
  0.6 0.0 copy-start
  0.6 0.0 copy-start.2
  0.7 0.0 copy-start.1
  0.7 0.0 copy-start.4
  0.7 0.0 copy-start.3
  0.7 1.0 %depth_faces.1 = f32[5,16,128]{2,1,0:T(8,128)S(1)} custom-call(f32[19,12,16,128]{3,2,1,0:T(8,128)} %adjoint.5), custom_call_target="tpu_custom_call" | custom-call | flops 933888000 | bytes 100000 | tf_op jit(solution)/shard_map/depth_faces/pallas_call | solution.py:690
  1.6 0.5 %collective-permute-start = (f32[5,16,128]{2,1,0:T(8,128)S(1)}, f32[5,16,128]{2,1,0:T(8,128)S(1)}, u32[]{:S(2)}, u32[]{:S(2)}) collective-permute-start(f32[5,16,128]{2,1,0:T(8,128)S(1)} %depth_faces.1), channel_id=1, source_target_pairs={{0,1},{1,0},{2,3},{3,2},{4,5},{5,4},{6,7},{7,6},{8,9},{9,8},{10,11... | collective-permute-start | bytes 122888 | tf_op jit(solution)/shard_map/ppermute | solution.py:82
  2.2 0.0 copy-done
  2.2 0.0 copy-done.2
  2.2 0.0 copy-done.1
  2.2 0.0 copy-done.4
  2.2 0.1 copy-done.3
  2.3 0.5 %pack_faces.1 = (f32[16,128]{1,0:T(8,128)S(1)}, f32[16,128]{1,0:T(8,128)S(1)}, f32[128,128]{1,0:T(8,128)S(1)}, f32[16,128]{1,0:T(8,128)S(1)}, f32[2,3,16,128]{3,2,1,0:T(8,128)S(1)}) custom-call(f32[19,12,16,128]{3,2,1,0:T(8,128)S(1)} %copy-done, f32[3,12,16,128]{3,2,1,0:T(8,128)S(1)} %copy-done.3, f32[16,128]{1,0:T(8,128)S(1)} %copy-done.4, ...), custom_call_target="tpu_custom_call" | custom-call | tf_op jit(solution)/shard_map/pack_faces/pallas_call | solution.py:690
  2.8 0.2 %collective-permute-done.refs_0_.refs_2_ = f32[5,16,128]{2,1,0:T(8,128)S(1)} collective-permute-done((f32[5,16,128]{2,1,0:T(8,128)S(1)}, f32[5,16,128]{2,1,0:T(8,128)S(1)}, u32[]{:S(2)}, u32[]{:S(2)}) %collective-permute-start) | collective-permute-done | bytes 40992 | tf_op jit(solution)/shard_map/ppermute | solution.py:82
  3.0 0.1 add_z_faces.1
  3.1 0.4 %collective-permute-start.1 = (f32[24,128]{1,0:T(8,128)S(1)}, f32[24,128]{1,0:T(8,128)S(1)}, u32[]{:S(2)}, u32[]{:S(2)}) collective-permute-start(f32[24,128]{1,0:T(8,128)S(1)} %get-tuple-element.21.refs_3_), channel_id=1, source_target_pairs={{4,8},{5,9},{8,4},{9,5},{12,16},{13,17},{16,12},{17,13},{20,24},{2... | collective-permute-start | bytes 36872 | tf_op jit(solution)/shard_map/ppermute | solution.py:86
  3.6 4.0 %collective-permute-start.2 = (f32[24,128]{1,0:T(8,128)S(1)}, f32[24,128]{1,0:T(8,128)S(1)}, u32[]{:S(2)}, u32[]{:S(2)}) collective-permute-start(f32[24,128]{1,0:T(8,128)S(1)} %get-tuple-element.22.refs_2_), channel_id=1, source_target_pairs={{0,4},{4,0},{8,12},{12,8},{16,20},{20,16},{24,28},{28,24},{1,5},{5... | collective-permute-start | bytes 36872 | tf_op jit(solution)/shard_map/ppermute | solution.py:82
  7.6 1.5 %collective-permute-start.3 = (f32[136,128]{1,0:T(8,128)S(1)}, f32[136,128]{1,0:T(8,128)S(1)}, u32[]{:S(2)}, u32[]{:S(2)}) collective-permute-start(f32[136,128]{1,0:T(8,128)S(1)} %get-tuple-element.25.refs_1_), channel_id=1, source_target_pairs={{0,2},{2,0},{1,3},{3,1},{4,6},{6,4},{5,7},{7,5},{8,10},{10,8},{9,1... | collective-permute-start | bytes 208904 | tf_op jit(solution)/shard_map/ppermute | solution.py:82
  9.1 0.0 collective-permute-done.1.refs_0_
  9.1 0.2 %collective-permute-done.2.refs_1_ = f32[24,128]{1,0:T(8,128)S(1)} collective-permute-done((f32[24,128]{1,0:T(8,128)S(1)}, f32[24,128]{1,0:T(8,128)S(1)}, u32[]{:S(2)}, u32[]{:S(2)}) %collective-permute-start.2) | collective-permute-done | bytes 12320 | tf_op jit(solution)/shard_map/ppermute | solution.py:82
  9.3 0.2 %add_x_faces.1 = (f32[16,128]{1,0:T(8,128)S(1)}, f32[2,16,128]{2,1,0:T(8,128)S(1)}) custom-call(f32[24,128]{1,0:T(8,128)S(1)} %collective-permute-done.1.refs_0_, f32[24,128]{1,0:T(8,128)S(1)} %collective-permute-done.2.refs_1_, f32[24,128]{1,0:T(8,128)S(1)} %get-tuple-element.22.refs_2_, f32[24,128]{1,0:T(8,128)S(1)} %get-tuple-element.21.refs_3_, ...), custom_call_target="tpu_custom_call" | custom-call | tf_op jit(solution)/shard_map/add_x_faces/pallas_call | solution.py:690
  9.5 1.6 %collective-permute-start.4 = (f32[16,128]{1,0:T(8,128)S(1)}, f32[16,128]{1,0:T(8,128)S(1)}, u32[]{:S(2)}, u32[]{:S(2)}) collective-permute-start(f32[16,128]{1,0:T(8,128)S(1)} %get-tuple-element.27.refs_3_), channel_id=1, source_target_pairs={{0,2},{2,0},{1,3},{3,1},{4,6},{6,4},{5,7},{7,5},{8,10},{10,8},{9,1... | collective-permute-start | bytes 24584 | tf_op jit(solution)/shard_map/ppermute | solution.py:82
  11.0 1.8 %collide.1 = (f32[19,12,16,128]{3,2,1,0:T(8,128)}, f32[1,19,12,128]{3,2,1,0:T(8,128)S(1)}, f32[16,128]{1,0:T(8,128)S(1)}) custom-call(f32[19,12,16,128]{3,2,1,0:T(8,128)S(1)} %copy-done, f32[16,128]{1,0:T(8,128)S(1)} %copy-done.4, s32[12,16,128]{2,1,0:T(8,128)S(1)} %copy-done.1, s32[12,16,128]{2,1,0:T(8,128)S(1)} %copy-done.2, ...), custom_call_target="tpu_custom_call" | custom-call | flops 3735552000 | bytes 4000000 | tf_op jit(solution)/shard_map/collide/pallas_call | solution.py:690
  12.8 0.4 %collective-permute-done.4.refs_1_.refs_2_ = f32[16,128]{1,0:T(8,128)S(1)} collective-permute-done((f32[16,128]{1,0:T(8,128)S(1)}, f32[16,128]{1,0:T(8,128)S(1)}, u32[]{:S(2)}, u32[]{:S(2)}) %collective-permute-start.4) | collective-permute-done | bytes 8224 | tf_op jit(solution)/shard_map/ppermute | solution.py:82
  13.2 0.0 collective-permute-done.3.refs_0_
  13.2 0.3 %add_y_faces.1.mine = f32[16,128]{1,0:T(8,128)S(1)} custom-call(f32[136,128]{1,0:T(8,128)S(1)} %collective-permute-done.3.refs_0_, f32[136,128]{1,0:T(8,128)S(1)} %get-tuple-element.25.refs_1_, f32[16,128]{1,0:T(8,128)S(1)} %collective-permute-done.4.refs_1_.refs_2_, f32[16,128]{1,0:T(8,128)S(1)} %get-tuple-element.27.refs_3_, ...), custom_call_target="tpu_custom_call" | custom-call | tf_op jit(solution)/shard_map/add_y_faces/pallas_call | solution.py:690
  13.5 0.1 collective-permute-start.5
  13.6 0.8 %add_y_rows.1 = f32[19,12,16,128]{3,2,1,0:T(8,128)} custom-call(f32[19,12,16,128]{3,2,1,0:T(8,128)} %get-tuple-element.23.new, f32[1,19,12,128]{3,2,1,0:T(8,128)S(1)} %get-tuple-element.24.edge_rows, f32[16,128]{1,0:T(8,128)S(1)} %copy-done.4, s32[12,16,128]{2,1,0:T(8,128)S(1)} %copy-done.1, ...), custom_call_target="tpu_custom_call", output_to_operand_aliasing={{}: (0, {})} | custom-call | tf_op jit(solution)/shard_map/add_y_rows/pallas_call | solution.py:690
  14.4 0.3 %collective-permute-done.5.other = f32[16,128]{1,0:T(8,128)S(1)} collective-permute-done((f32[16,128]{1,0:T(8,128)S(1)}, f32[16,128]{1,0:T(8,128)S(1)}, u32[]{:S(2)}, u32[]{:S(2)}) %collective-permute-start.5) | collective-permute-done | bytes 8224 | tf_op jit(solution)/shard_map/ppermute | solution.py:82
  14.7 0.6 %add_depth.1 = f32[16,128]{1,0:T(8,128)} custom-call(f32[16,128]{1,0:T(8,128)S(1)} %add_y_faces.1.mine, f32[16,128]{1,0:T(8,128)S(1)} %collective-permute-done.5.other), custom_call_target="tpu_custom_call" | custom-call | tf_op jit(solution)/shard_map/add_depth/pallas_call | solution.py:690
Async XLA Ops:
  0.6 1.6 %copy-start = (f32[19,12,16,128]{3,2,1,0:T(8,128)S(1)}, f32[19,12,16,128]{3,2,1,0:T(8,128)}, u32[]{:S(2)}) copy-start(f32[19,12,16,128]{3,2,1,0:T(8,128)} %adjoint.5) | copy-start | bytes 5603332
  0.6 1.6 %copy-start.2 = (s32[12,16,128]{2,1,0:T(8,128)S(1)}, s32[12,16,128]{2,1,0:T(8,128)}, u32[]{:S(2)}) copy-start(s32[12,16,128]{2,1,0:T(8,128)} %port.5) | copy-start | bytes 294916
  0.7 1.5 %copy-start.1 = (s32[12,16,128]{2,1,0:T(8,128)S(1)}, s32[12,16,128]{2,1,0:T(8,128)}, u32[]{:S(2)}) copy-start(s32[12,16,128]{2,1,0:T(8,128)} %solid.5) | copy-start | bytes 294916
  0.7 1.5 %copy-start.4 = (f32[16,128]{1,0:T(8,128)S(1)}, f32[16,128]{1,0:T(8,128)}, u32[]{:S(2)}) copy-start(f32[16,128]{1,0:T(8,128)} %design.5) | copy-start | bytes 24580
  0.7 1.6 %copy-start.3 = (f32[3,12,16,128]{3,2,1,0:T(8,128)S(1)}, f32[3,12,16,128]{3,2,1,0:T(8,128)}, u32[]{:S(2)}) copy-start(f32[3,12,16,128]{3,2,1,0:T(8,128)} %momentum.1) | copy-start | bytes 884740
  1.6 1.4 %collective-permute-start = (f32[5,16,128]{2,1,0:T(8,128)S(1)}, f32[5,16,128]{2,1,0:T(8,128)S(1)}, u32[]{:S(2)}, u32[]{:S(2)}) collective-permute-start(f32[5,16,128]{2,1,0:T(8,128)S(1)} %depth_faces.1), channel_id=1, source_target_pairs={{0,1},{1,0},{2,3},{3,2},{4,5},{5,4},{6,7},{7,6},{8,9},{9,8},{10,11... | collective-permute-start | bytes 122888 | tf_op jit(solution)/shard_map/ppermute | solution.py:82
  3.1 5.9 %collective-permute-start.1 = (f32[24,128]{1,0:T(8,128)S(1)}, f32[24,128]{1,0:T(8,128)S(1)}, u32[]{:S(2)}, u32[]{:S(2)}) collective-permute-start(f32[24,128]{1,0:T(8,128)S(1)} %get-tuple-element.21.refs_3_), channel_id=1, source_target_pairs={{4,8},{5,9},{8,4},{9,5},{12,16},{13,17},{16,12},{17,13},{20,24},{2... | collective-permute-start | bytes 36872 | tf_op jit(solution)/shard_map/ppermute | solution.py:86
  3.6 5.7 %collective-permute-start.2 = (f32[24,128]{1,0:T(8,128)S(1)}, f32[24,128]{1,0:T(8,128)S(1)}, u32[]{:S(2)}, u32[]{:S(2)}) collective-permute-start(f32[24,128]{1,0:T(8,128)S(1)} %get-tuple-element.22.refs_2_), channel_id=1, source_target_pairs={{0,4},{4,0},{8,12},{12,8},{16,20},{20,16},{24,28},{28,24},{1,5},{5... | collective-permute-start | bytes 36872 | tf_op jit(solution)/shard_map/ppermute | solution.py:82
  7.6 5.6 %collective-permute-start.3 = (f32[136,128]{1,0:T(8,128)S(1)}, f32[136,128]{1,0:T(8,128)S(1)}, u32[]{:S(2)}, u32[]{:S(2)}) collective-permute-start(f32[136,128]{1,0:T(8,128)S(1)} %get-tuple-element.25.refs_1_), channel_id=1, source_target_pairs={{0,2},{2,0},{1,3},{3,1},{4,6},{6,4},{5,7},{7,5},{8,10},{10,8},{9,1... | collective-permute-start | bytes 208904 | tf_op jit(solution)/shard_map/ppermute | solution.py:82
  9.5 3.7 %collective-permute-start.4 = (f32[16,128]{1,0:T(8,128)S(1)}, f32[16,128]{1,0:T(8,128)S(1)}, u32[]{:S(2)}, u32[]{:S(2)}) collective-permute-start(f32[16,128]{1,0:T(8,128)S(1)} %get-tuple-element.27.refs_3_), channel_id=1, source_target_pairs={{0,2},{2,0},{1,3},{3,1},{4,6},{6,4},{5,7},{7,5},{8,10},{10,8},{9,1... | collective-permute-start | bytes 24584 | tf_op jit(solution)/shard_map/ppermute | solution.py:82
  13.5 1.2 %collective-permute-start.5 = (f32[16,128]{1,0:T(8,128)S(1)}, f32[16,128]{1,0:T(8,128)S(1)}, u32[]{:S(2)}, u32[]{:S(2)}) collective-permute-start(f32[16,128]{1,0:T(8,128)S(1)} %add_y_faces.1.mine), channel_id=1, source_target_pairs={{0,1},{1,0},{2,3},{3,2},{4,5},{5,4},{6,7},{7,6},{8,9},{9,8},{10,11... | collective-permute-start | bytes 24584 | tf_op jit(solution)/shard_map/ppermute | solution.py:82

commit v8 on v7

--- a/solution.py
+++ b/solution.py
@@ -252,8 +252,11 @@
         after = partner_after("gy", pairing)
         for kind in range(len(laterals)):
             last, first = (crossing(1, -1)[kind], crossing(1, 1)[kind])
-            y_out[pairing][kind * slots : kind * slots + levels, :] = pick(
-                after, adjoint[last, :, rows - 1, :], adjoint[first, :, 0, :]
+            step = laterals[kind][1]
+            low, high = (max(step, 0), levels + min(step, 0))
+            base = kind * slots - step
+            y_out[pairing][base + low : base + high, :] = pick(
+                after, adjoint[last, low:high, rows - 1, :], adjoint[first, low:high, 0, :]
             )
     own_out[...] = total
     odd = lane % 2 == 1
@@ -301,7 +304,7 @@
                 last, first = (
                     halo[side][planes.index(crossing(1, sign)[kind])] for sign in (-1, 1)
                 )
-                place = kind * slots + level % slots
+                place = kind * slots + level - laterals[kind][1]
                 y_out[pairing][place : place + 1, :] = pick(
                     after, last[rows - 1 : rows], first[0:1]
                 )
@@ -433,7 +436,6 @@
     total_main, total_side = (0.0, 0.0)
     for kind, (lateral_x, lateral_z) in enumerate(laterals):
         main, side = step_x(lines[kind], ends, kind, lateral_x)
-        main, side = (turn(main, -lateral_z, 0), turn(side, -lateral_z, 0))
         pull_main, pull_side = (sign * gain[1][0], sign * gain[1][1])
         if lateral_x != 0:
             pull_main = pull_main + lateral_x * gain[0][0]
@@ -644,7 +646,7 @@
             line = got[kind * slots : (kind + 1) * slots]
             if lateral_x != 0:
                 line = step_x(line, ends, kind, lateral_x)[0]
-            line = turn(line, -lateral_z, 0)[0:levels]
+            line = line[0:levels]
             none = jnp.zeros_like(line)
             extra[crossing(1, 1)[kind]] = pick(after, line, none)
             extra[crossing(1, -1)[kind]] = pick(after, none, line)

time: 15.5 us -> 15.5 us (level)
  no operation moved by 1% of the time
where the time goes in v8:
time: 15.5 us; the launch traced here: 15.3 us
  starting transfers between devices  8.09 us (52%)
  Pallas kernels  5.27 us (34%)
  waiting for transfers between devices  1.1 us (7%)
  between operations  0.73 us (5%)
    ppermute x5, starting transfers between devices, swap(): return lax.ppermute(array, axis, pairs)  7.67 us
    pallas_call x8, Pallas kernels, local_call(): pl.pallas_call(body, out_shape=shapes, in_specs=[far_spec if place in far...  5.27 us
    ppermute x5, waiting for transfers between devices, swap(): return lax.ppermute(array, axis, pairs)  1.1 us
    ppermute x1, starting transfers between devices, swap(): return lax.ppermute(array, (axis, 'depth'), full)  0.42 us
  transfers between devices with their start and end apart: 6, of which 4 were waited for; matrix products, arithmetic and copies ran while one was open for 0% of the time, Pallas kernels for 22%

profile of v8, /device:TPU:0, one launch (start us, length us, event | category | flops | bytes accessed | tf_op | source)
XLA Modules:
  0.0 15.3 jit_solution(7922201259708195701)
XLA Ops:
  0.6 0.0 copy-start
  0.6 0.0 copy-start.2
  0.7 0.0 copy-start.1
  0.7 0.0 copy-start.4
  0.7 0.0 copy-start.3
  0.7 1.0 %depth_faces.1 = f32[5,16,128]{2,1,0:T(8,128)S(1)} custom-call(f32[19,12,16,128]{3,2,1,0:T(8,128)} %adjoint.5), custom_call_target="tpu_custom_call" | custom-call | flops 933888000 | bytes 100000 | tf_op jit(solution)/shard_map/depth_faces/pallas_call | solution.py:692
  1.6 0.5 %collective-permute-start = (f32[5,16,128]{2,1,0:T(8,128)S(1)}, f32[5,16,128]{2,1,0:T(8,128)S(1)}, u32[]{:S(2)}, u32[]{:S(2)}) collective-permute-start(f32[5,16,128]{2,1,0:T(8,128)S(1)} %depth_faces.1), channel_id=1, source_target_pairs={{0,1},{1,0},{2,3},{3,2},{4,5},{5,4},{6,7},{7,6},{8,9},{9,8},{10,11... | collective-permute-start | bytes 122888 | tf_op jit(solution)/shard_map/ppermute | solution.py:82
  2.2 0.0 copy-done
  2.2 0.0 copy-done.2
  2.2 0.0 copy-done.1
  2.2 0.0 copy-done.4
  2.2 0.1 copy-done.3
  2.3 0.5 %pack_faces.1 = (f32[16,128]{1,0:T(8,128)S(1)}, f32[16,128]{1,0:T(8,128)S(1)}, f32[128,128]{1,0:T(8,128)S(1)}, f32[16,128]{1,0:T(8,128)S(1)}, f32[2,3,16,128]{3,2,1,0:T(8,128)S(1)}) custom-call(f32[19,12,16,128]{3,2,1,0:T(8,128)S(1)} %copy-done, f32[3,12,16,128]{3,2,1,0:T(8,128)S(1)} %copy-done.3, f32[16,128]{1,0:T(8,128)S(1)} %copy-done.4, ...), custom_call_target="tpu_custom_call" | custom-call | tf_op jit(solution)/shard_map/pack_faces/pallas_call | solution.py:692
  2.8 0.2 %collective-permute-done.refs_0_.refs_2_ = f32[5,16,128]{2,1,0:T(8,128)S(1)} collective-permute-done((f32[5,16,128]{2,1,0:T(8,128)S(1)}, f32[5,16,128]{2,1,0:T(8,128)S(1)}, u32[]{:S(2)}, u32[]{:S(2)}) %collective-permute-start) | collective-permute-done | bytes 40992 | tf_op jit(solution)/shard_map/ppermute | solution.py:82
  3.0 0.1 add_z_faces.1
  3.1 0.4 %collective-permute-start.1 = (f32[24,128]{1,0:T(8,128)S(1)}, f32[24,128]{1,0:T(8,128)S(1)}, u32[]{:S(2)}, u32[]{:S(2)}) collective-permute-start(f32[24,128]{1,0:T(8,128)S(1)} %get-tuple-element.21.refs_3_), channel_id=1, source_target_pairs={{4,8},{5,9},{8,4},{9,5},{12,16},{13,17},{16,12},{17,13},{20,24},{2... | collective-permute-start | bytes 36872 | tf_op jit(solution)/shard_map/ppermute | solution.py:86
  3.6 4.0 %collective-permute-start.2 = (f32[24,128]{1,0:T(8,128)S(1)}, f32[24,128]{1,0:T(8,128)S(1)}, u32[]{:S(2)}, u32[]{:S(2)}) collective-permute-start(f32[24,128]{1,0:T(8,128)S(1)} %get-tuple-element.22.refs_2_), channel_id=1, source_target_pairs={{0,4},{4,0},{8,12},{12,8},{16,20},{20,16},{24,28},{28,24},{1,5},{5... | collective-permute-start | bytes 36872 | tf_op jit(solution)/shard_map/ppermute | solution.py:82
  7.6 1.5 %collective-permute-start.3 = (f32[136,128]{1,0:T(8,128)S(1)}, f32[136,128]{1,0:T(8,128)S(1)}, u32[]{:S(2)}, u32[]{:S(2)}) collective-permute-start(f32[136,128]{1,0:T(8,128)S(1)} %get-tuple-element.25.refs_1_), channel_id=1, source_target_pairs={{0,2},{2,0},{1,3},{3,1},{4,6},{6,4},{5,7},{7,5},{8,10},{10,8},{9,1... | collective-permute-start | bytes 208904 | tf_op jit(solution)/shard_map/ppermute | solution.py:82
  9.1 0.0 collective-permute-done.1.refs_0_
  9.1 0.2 %collective-permute-done.2.refs_1_ = f32[24,128]{1,0:T(8,128)S(1)} collective-permute-done((f32[24,128]{1,0:T(8,128)S(1)}, f32[24,128]{1,0:T(8,128)S(1)}, u32[]{:S(2)}, u32[]{:S(2)}) %collective-permute-start.2) | collective-permute-done | bytes 12320 | tf_op jit(solution)/shard_map/ppermute | solution.py:82
  9.3 0.2 %add_x_faces.1 = (f32[16,128]{1,0:T(8,128)S(1)}, f32[2,16,128]{2,1,0:T(8,128)S(1)}) custom-call(f32[24,128]{1,0:T(8,128)S(1)} %collective-permute-done.1.refs_0_, f32[24,128]{1,0:T(8,128)S(1)} %collective-permute-done.2.refs_1_, f32[24,128]{1,0:T(8,128)S(1)} %get-tuple-element.22.refs_2_, f32[24,128]{1,0:T(8,128)S(1)} %get-tuple-element.21.refs_3_, ...), custom_call_target="tpu_custom_call" | custom-call | tf_op jit(solution)/shard_map/add_x_faces/pallas_call | solution.py:692
  9.5 1.6 %collective-permute-start.4 = (f32[16,128]{1,0:T(8,128)S(1)}, f32[16,128]{1,0:T(8,128)S(1)}, u32[]{:S(2)}, u32[]{:S(2)}) collective-permute-start(f32[16,128]{1,0:T(8,128)S(1)} %get-tuple-element.27.refs_3_), channel_id=1, source_target_pairs={{0,2},{2,0},{1,3},{3,1},{4,6},{6,4},{5,7},{7,5},{8,10},{10,8},{9,1... | collective-permute-start | bytes 24584 | tf_op jit(solution)/shard_map/ppermute | solution.py:82
  11.0 1.8 %collide.1 = (f32[19,12,16,128]{3,2,1,0:T(8,128)}, f32[1,19,12,128]{3,2,1,0:T(8,128)S(1)}, f32[16,128]{1,0:T(8,128)S(1)}) custom-call(f32[19,12,16,128]{3,2,1,0:T(8,128)S(1)} %copy-done, f32[16,128]{1,0:T(8,128)S(1)} %copy-done.4, s32[12,16,128]{2,1,0:T(8,128)S(1)} %copy-done.1, s32[12,16,128]{2,1,0:T(8,128)S(1)} %copy-done.2, ...), custom_call_target="tpu_custom_call" | custom-call | flops 3735552000 | bytes 4000000 | tf_op jit(solution)/shard_map/collide/pallas_call | solution.py:692
  12.8 0.4 %collective-permute-done.4.refs_1_.refs_2_ = f32[16,128]{1,0:T(8,128)S(1)} collective-permute-done((f32[16,128]{1,0:T(8,128)S(1)}, f32[16,128]{1,0:T(8,128)S(1)}, u32[]{:S(2)}, u32[]{:S(2)}) %collective-permute-start.4) | collective-permute-done | bytes 8224 | tf_op jit(solution)/shard_map/ppermute | solution.py:82
  13.2 0.0 collective-permute-done.3.refs_0_
  13.2 0.3 %add_y_faces.1.mine = f32[16,128]{1,0:T(8,128)S(1)} custom-call(f32[136,128]{1,0:T(8,128)S(1)} %collective-permute-done.3.refs_0_, f32[136,128]{1,0:T(8,128)S(1)} %get-tuple-element.25.refs_1_, f32[16,128]{1,0:T(8,128)S(1)} %collective-permute-done.4.refs_1_.refs_2_, f32[16,128]{1,0:T(8,128)S(1)} %get-tuple-element.27.refs_3_, ...), custom_call_target="tpu_custom_call" | custom-call | tf_op jit(solution)/shard_map/add_y_faces/pallas_call | solution.py:692
  13.5 0.1 collective-permute-start.5
  13.6 0.8 %add_y_rows.1 = f32[19,12,16,128]{3,2,1,0:T(8,128)} custom-call(f32[19,12,16,128]{3,2,1,0:T(8,128)} %get-tuple-element.23.new, f32[1,19,12,128]{3,2,1,0:T(8,128)S(1)} %get-tuple-element.24.edge_rows, f32[16,128]{1,0:T(8,128)S(1)} %copy-done.4, s32[12,16,128]{2,1,0:T(8,128)S(1)} %copy-done.1, ...), custom_call_target="tpu_custom_call", output_to_operand_aliasing={{}: (0, {})} | custom-call | tf_op jit(solution)/shard_map/add_y_rows/pallas_call | solution.py:692
  14.4 0.3 %collective-permute-done.5.other = f32[16,128]{1,0:T(8,128)S(1)} collective-permute-done((f32[16,128]{1,0:T(8,128)S(1)}, f32[16,128]{1,0:T(8,128)S(1)}, u32[]{:S(2)}, u32[]{:S(2)}) %collective-permute-start.5) | collective-permute-done | bytes 8224 | tf_op jit(solution)/shard_map/ppermute | solution.py:82
  14.7 0.6 %add_depth.1 = f32[16,128]{1,0:T(8,128)} custom-call(f32[16,128]{1,0:T(8,128)S(1)} %add_y_faces.1.mine, f32[16,128]{1,0:T(8,128)S(1)} %collective-permute-done.5.other), custom_call_target="tpu_custom_call" | custom-call | tf_op jit(solution)/shard_map/add_depth/pallas_call | solution.py:692
Async XLA Ops:
  0.6 1.6 %copy-start = (f32[19,12,16,128]{3,2,1,0:T(8,128)S(1)}, f32[19,12,16,128]{3,2,1,0:T(8,128)}, u32[]{:S(2)}) copy-start(f32[19,12,16,128]{3,2,1,0:T(8,128)} %adjoint.5) | copy-start | bytes 5603332
  0.6 1.6 %copy-start.2 = (s32[12,16,128]{2,1,0:T(8,128)S(1)}, s32[12,16,128]{2,1,0:T(8,128)}, u32[]{:S(2)}) copy-start(s32[12,16,128]{2,1,0:T(8,128)} %port.5) | copy-start | bytes 294916
  0.7 1.5 %copy-start.1 = (s32[12,16,128]{2,1,0:T(8,128)S(1)}, s32[12,16,128]{2,1,0:T(8,128)}, u32[]{:S(2)}) copy-start(s32[12,16,128]{2,1,0:T(8,128)} %solid.5) | copy-start | bytes 294916
  0.7 1.5 %copy-start.4 = (f32[16,128]{1,0:T(8,128)S(1)}, f32[16,128]{1,0:T(8,128)}, u32[]{:S(2)}) copy-start(f32[16,128]{1,0:T(8,128)} %design.5) | copy-start | bytes 24580
  0.7 1.6 %copy-start.3 = (f32[3,12,16,128]{3,2,1,0:T(8,128)S(1)}, f32[3,12,16,128]{3,2,1,0:T(8,128)}, u32[]{:S(2)}) copy-start(f32[3,12,16,128]{3,2,1,0:T(8,128)} %momentum.1) | copy-start | bytes 884740
  1.6 1.4 %collective-permute-start = (f32[5,16,128]{2,1,0:T(8,128)S(1)}, f32[5,16,128]{2,1,0:T(8,128)S(1)}, u32[]{:S(2)}, u32[]{:S(2)}) collective-permute-start(f32[5,16,128]{2,1,0:T(8,128)S(1)} %depth_faces.1), channel_id=1, source_target_pairs={{0,1},{1,0},{2,3},{3,2},{4,5},{5,4},{6,7},{7,6},{8,9},{9,8},{10,11... | collective-permute-start | bytes 122888 | tf_op jit(solution)/shard_map/ppermute | solution.py:82
  3.1 5.9 %collective-permute-start.1 = (f32[24,128]{1,0:T(8,128)S(1)}, f32[24,128]{1,0:T(8,128)S(1)}, u32[]{:S(2)}, u32[]{:S(2)}) collective-permute-start(f32[24,128]{1,0:T(8,128)S(1)} %get-tuple-element.21.refs_3_), channel_id=1, source_target_pairs={{4,8},{5,9},{8,4},{9,5},{12,16},{13,17},{16,12},{17,13},{20,24},{2... | collective-permute-start | bytes 36872 | tf_op jit(solution)/shard_map/ppermute | solution.py:86
  3.6 5.7 %collective-permute-start.2 = (f32[24,128]{1,0:T(8,128)S(1)}, f32[24,128]{1,0:T(8,128)S(1)}, u32[]{:S(2)}, u32[]{:S(2)}) collective-permute-start(f32[24,128]{1,0:T(8,128)S(1)} %get-tuple-element.22.refs_2_), channel_id=1, source_target_pairs={{0,4},{4,0},{8,12},{12,8},{16,20},{20,16},{24,28},{28,24},{1,5},{5... | collective-permute-start | bytes 36872 | tf_op jit(solution)/shard_map/ppermute | solution.py:82
  7.6 5.6 %collective-permute-start.3 = (f32[136,128]{1,0:T(8,128)S(1)}, f32[136,128]{1,0:T(8,128)S(1)}, u32[]{:S(2)}, u32[]{:S(2)}) collective-permute-start(f32[136,128]{1,0:T(8,128)S(1)} %get-tuple-element.25.refs_1_), channel_id=1, source_target_pairs={{0,2},{2,0},{1,3},{3,1},{4,6},{6,4},{5,7},{7,5},{8,10},{10,8},{9,1... | collective-permute-start | bytes 208904 | tf_op jit(solution)/shard_map/ppermute | solution.py:82
  9.5 3.7 %collective-permute-start.4 = (f32[16,128]{1,0:T(8,128)S(1)}, f32[16,128]{1,0:T(8,128)S(1)}, u32[]{:S(2)}, u32[]{:S(2)}) collective-permute-start(f32[16,128]{1,0:T(8,128)S(1)} %get-tuple-element.27.refs_3_), channel_id=1, source_target_pairs={{0,2},{2,0},{1,3},{3,1},{4,6},{6,4},{5,7},{7,5},{8,10},{10,8},{9,1... | collective-permute-start | bytes 24584 | tf_op jit(solution)/shard_map/ppermute | solution.py:82
  13.5 1.2 %collective-permute-start.5 = (f32[16,128]{1,0:T(8,128)S(1)}, f32[16,128]{1,0:T(8,128)S(1)}, u32[]{:S(2)}, u32[]{:S(2)}) collective-permute-start(f32[16,128]{1,0:T(8,128)S(1)} %add_y_faces.1.mine), channel_id=1, source_target_pairs={{0,1},{1,0},{2,3},{3,2},{4,5},{5,4},{6,7},{7,6},{8,9},{9,8},{10,11... | collective-permute-start | bytes 24584 | tf_op jit(solution)/shard_map/ppermute | solution.py:82

commit v9 on v8

--- a/solution.py
+++ b/solution.py
@@ -159,22 +159,22 @@
 
 
 def own_moment(take):
-    heavy, light = (1.0 / 18.0, 1.0 / 36.0)
+    heavy = lattice_weights[1] / lattice_weights[7]
     p = {
         number: take(number, vector[2]) for number, vector in enumerate(velocities) if number != 0
     }
     for number in (7, 8, 9, 10):
         p[number] = along_y(p[number], velocities[number][1])
-    right_x = along_x(heavy * p[1] + light * ((p[7] + p[9]) + (p[11] + p[13])), 1)
-    left_x = along_x(heavy * p[2] + light * ((p[8] + p[10]) + (p[12] + p[14])), -1)
-    right_y = along_x(light * (p[7] - p[9]), 1)
-    left_y = along_x(light * (p[10] - p[8]), -1)
-    right_z = along_x(light * (p[11] - p[13]), 1)
-    left_z = along_x(light * (p[14] - p[12]), -1)
-    lower_y = along_y(heavy * p[3] + light * (p[15] + p[17]), 1)
-    upper_y = along_y(heavy * p[4] + light * (p[16] + p[18]), -1)
-    lower_z = along_y(light * (p[15] - p[17]), 1)
-    upper_z = along_y(light * (p[18] - p[16]), -1)
+    right_x = along_x(heavy * p[1] + ((p[7] + p[9]) + (p[11] + p[13])), 1)
+    left_x = along_x(heavy * p[2] + ((p[8] + p[10]) + (p[12] + p[14])), -1)
+    right_y = along_x((p[7] - p[9]), 1)
+    left_y = along_x((p[10] - p[8]), -1)
+    right_z = along_x((p[11] - p[13]), 1)
+    left_z = along_x((p[14] - p[12]), -1)
+    lower_y = along_y(heavy * p[3] + (p[15] + p[17]), 1)
+    upper_y = along_y(heavy * p[4] + (p[16] + p[18]), -1)
+    lower_z = along_y((p[15] - p[17]), 1)
+    upper_z = along_y((p[18] - p[16]), -1)
     moment_x = right_x - left_x
     moment_y = (lower_y - upper_y) + (right_y + left_y)
     moment_z = heavy * (p[5] - p[6]) + ((right_z + left_z) + (lower_z + upper_z))
@@ -258,7 +258,7 @@
             y_out[pairing][base + low : base + high, :] = pick(
                 after, adjoint[last, low:high, rows - 1, :], adjoint[first, low:high, 0, :]
             )
-    own_out[...] = total
+    own_out[...] = lattice_weights[7] * total
     odd = lane % 2 == 1
     first_pack = jnp.where(odd, joint[0], turn(joint[1], -1, 1))
     last_pack = jnp.where(odd, turn(joint[0], 1, 1), joint[1])

time: 15.5 us -> 15.5 us (level)
  no operation moved by 1% of the time
where the time goes in v9:
time: 15.5 us; the launch traced here: 15.3 us
  starting transfers between devices  8.09 us (52%)
  Pallas kernels  5.26 us (34%)
  waiting for transfers between devices  1.11 us (7%)
  between operations  0.73 us (5%)
    ppermute x5, starting transfers between devices, swap(): return lax.ppermute(array, axis, pairs)  7.67 us
    pallas_call x8, Pallas kernels, local_call(): pl.pallas_call(body, out_shape=shapes, in_specs=[far_spec if place in far...  5.26 us
    ppermute x5, waiting for transfers between devices, swap(): return lax.ppermute(array, axis, pairs)  1.1 us
    ppermute x1, starting transfers between devices, swap(): return lax.ppermute(array, (axis, 'depth'), full)  0.42 us
  transfers between devices with their start and end apart: 6, of which 4 were waited for; matrix products, arithmetic and copies ran while one was open for 0% of the time, Pallas kernels for 22%

profile of v9, /device:TPU:0, one launch (start us, length us, event | category | flops | bytes accessed | tf_op | source)
XLA Modules:
  0.0 15.3 jit_solution(16094216227926514572)
XLA Ops:
  0.6 0.0 copy-start
  0.6 0.0 copy-start.2
  0.7 0.0 copy-start.1
  0.7 0.0 copy-start.4
  0.7 0.0 copy-start.3
  0.7 1.0 %depth_faces.1 = f32[5,16,128]{2,1,0:T(8,128)S(1)} custom-call(f32[19,12,16,128]{3,2,1,0:T(8,128)} %adjoint.5), custom_call_target="tpu_custom_call" | custom-call | flops 933888000 | bytes 100000 | tf_op jit(solution)/shard_map/depth_faces/pallas_call | solution.py:692
  1.6 0.5 %collective-permute-start = (f32[5,16,128]{2,1,0:T(8,128)S(1)}, f32[5,16,128]{2,1,0:T(8,128)S(1)}, u32[]{:S(2)}, u32[]{:S(2)}) collective-permute-start(f32[5,16,128]{2,1,0:T(8,128)S(1)} %depth_faces.1), channel_id=1, source_target_pairs={{0,1},{1,0},{2,3},{3,2},{4,5},{5,4},{6,7},{7,6},{8,9},{9,8},{10,11... | collective-permute-start | bytes 122888 | tf_op jit(solution)/shard_map/ppermute | solution.py:82
  2.2 0.0 copy-done
  2.2 0.0 copy-done.2
  2.2 0.0 copy-done.1
  2.2 0.0 copy-done.4
  2.2 0.1 copy-done.3
  2.3 0.5 %pack_faces.1 = (f32[16,128]{1,0:T(8,128)S(1)}, f32[16,128]{1,0:T(8,128)S(1)}, f32[128,128]{1,0:T(8,128)S(1)}, f32[16,128]{1,0:T(8,128)S(1)}, f32[2,3,16,128]{3,2,1,0:T(8,128)S(1)}) custom-call(f32[19,12,16,128]{3,2,1,0:T(8,128)S(1)} %copy-done, f32[3,12,16,128]{3,2,1,0:T(8,128)S(1)} %copy-done.3, f32[16,128]{1,0:T(8,128)S(1)} %copy-done.4, ...), custom_call_target="tpu_custom_call" | custom-call | tf_op jit(solution)/shard_map/pack_faces/pallas_call | solution.py:692
  2.8 0.2 %collective-permute-done.refs_0_.refs_2_ = f32[5,16,128]{2,1,0:T(8,128)S(1)} collective-permute-done((f32[5,16,128]{2,1,0:T(8,128)S(1)}, f32[5,16,128]{2,1,0:T(8,128)S(1)}, u32[]{:S(2)}, u32[]{:S(2)}) %collective-permute-start) | collective-permute-done | bytes 40992 | tf_op jit(solution)/shard_map/ppermute | solution.py:82
  3.0 0.1 add_z_faces.1
  3.1 0.4 %collective-permute-start.1 = (f32[24,128]{1,0:T(8,128)S(1)}, f32[24,128]{1,0:T(8,128)S(1)}, u32[]{:S(2)}, u32[]{:S(2)}) collective-permute-start(f32[24,128]{1,0:T(8,128)S(1)} %get-tuple-element.21.refs_3_), channel_id=1, source_target_pairs={{4,8},{5,9},{8,4},{9,5},{12,16},{13,17},{16,12},{17,13},{20,24},{2... | collective-permute-start | bytes 36872 | tf_op jit(solution)/shard_map/ppermute | solution.py:86
  3.6 4.0 %collective-permute-start.2 = (f32[24,128]{1,0:T(8,128)S(1)}, f32[24,128]{1,0:T(8,128)S(1)}, u32[]{:S(2)}, u32[]{:S(2)}) collective-permute-start(f32[24,128]{1,0:T(8,128)S(1)} %get-tuple-element.22.refs_2_), channel_id=1, source_target_pairs={{0,4},{4,0},{8,12},{12,8},{16,20},{20,16},{24,28},{28,24},{1,5},{5... | collective-permute-start | bytes 36872 | tf_op jit(solution)/shard_map/ppermute | solution.py:82
  7.6 1.5 %collective-permute-start.3 = (f32[136,128]{1,0:T(8,128)S(1)}, f32[136,128]{1,0:T(8,128)S(1)}, u32[]{:S(2)}, u32[]{:S(2)}) collective-permute-start(f32[136,128]{1,0:T(8,128)S(1)} %get-tuple-element.25.refs_1_), channel_id=1, source_target_pairs={{0,2},{2,0},{1,3},{3,1},{4,6},{6,4},{5,7},{7,5},{8,10},{10,8},{9,1... | collective-permute-start | bytes 208904 | tf_op jit(solution)/shard_map/ppermute | solution.py:82
  9.1 0.0 collective-permute-done.1.refs_0_
  9.1 0.2 %collective-permute-done.2.refs_1_ = f32[24,128]{1,0:T(8,128)S(1)} collective-permute-done((f32[24,128]{1,0:T(8,128)S(1)}, f32[24,128]{1,0:T(8,128)S(1)}, u32[]{:S(2)}, u32[]{:S(2)}) %collective-permute-start.2) | collective-permute-done | bytes 12320 | tf_op jit(solution)/shard_map/ppermute | solution.py:82
  9.3 0.2 %add_x_faces.1 = (f32[16,128]{1,0:T(8,128)S(1)}, f32[2,16,128]{2,1,0:T(8,128)S(1)}) custom-call(f32[24,128]{1,0:T(8,128)S(1)} %collective-permute-done.1.refs_0_, f32[24,128]{1,0:T(8,128)S(1)} %collective-permute-done.2.refs_1_, f32[24,128]{1,0:T(8,128)S(1)} %get-tuple-element.22.refs_2_, f32[24,128]{1,0:T(8,128)S(1)} %get-tuple-element.21.refs_3_, ...), custom_call_target="tpu_custom_call" | custom-call | tf_op jit(solution)/shard_map/add_x_faces/pallas_call | solution.py:692
  9.5 1.6 %collective-permute-start.4 = (f32[16,128]{1,0:T(8,128)S(1)}, f32[16,128]{1,0:T(8,128)S(1)}, u32[]{:S(2)}, u32[]{:S(2)}) collective-permute-start(f32[16,128]{1,0:T(8,128)S(1)} %get-tuple-element.27.refs_3_), channel_id=1, source_target_pairs={{0,2},{2,0},{1,3},{3,1},{4,6},{6,4},{5,7},{7,5},{8,10},{10,8},{9,1... | collective-permute-start | bytes 24584 | tf_op jit(solution)/shard_map/ppermute | solution.py:82
  11.0 1.8 %collide.1 = (f32[19,12,16,128]{3,2,1,0:T(8,128)}, f32[1,19,12,128]{3,2,1,0:T(8,128)S(1)}, f32[16,128]{1,0:T(8,128)S(1)}) custom-call(f32[19,12,16,128]{3,2,1,0:T(8,128)S(1)} %copy-done, f32[16,128]{1,0:T(8,128)S(1)} %copy-done.4, s32[12,16,128]{2,1,0:T(8,128)S(1)} %copy-done.1, s32[12,16,128]{2,1,0:T(8,128)S(1)} %copy-done.2, ...), custom_call_target="tpu_custom_call" | custom-call | flops 3735552000 | bytes 4000000 | tf_op jit(solution)/shard_map/collide/pallas_call | solution.py:692
  12.8 0.4 %collective-permute-done.4.refs_1_.refs_2_ = f32[16,128]{1,0:T(8,128)S(1)} collective-permute-done((f32[16,128]{1,0:T(8,128)S(1)}, f32[16,128]{1,0:T(8,128)S(1)}, u32[]{:S(2)}, u32[]{:S(2)}) %collective-permute-start.4) | collective-permute-done | bytes 8224 | tf_op jit(solution)/shard_map/ppermute | solution.py:82
  13.2 0.0 collective-permute-done.3.refs_0_
  13.2 0.3 %add_y_faces.1.mine = f32[16,128]{1,0:T(8,128)S(1)} custom-call(f32[136,128]{1,0:T(8,128)S(1)} %collective-permute-done.3.refs_0_, f32[136,128]{1,0:T(8,128)S(1)} %get-tuple-element.25.refs_1_, f32[16,128]{1,0:T(8,128)S(1)} %collective-permute-done.4.refs_1_.refs_2_, f32[16,128]{1,0:T(8,128)S(1)} %get-tuple-element.27.refs_3_, ...), custom_call_target="tpu_custom_call" | custom-call | tf_op jit(solution)/shard_map/add_y_faces/pallas_call | solution.py:692
  13.5 0.1 collective-permute-start.5
  13.6 0.8 %add_y_rows.1 = f32[19,12,16,128]{3,2,1,0:T(8,128)} custom-call(f32[19,12,16,128]{3,2,1,0:T(8,128)} %get-tuple-element.23.new, f32[1,19,12,128]{3,2,1,0:T(8,128)S(1)} %get-tuple-element.24.edge_rows, f32[16,128]{1,0:T(8,128)S(1)} %copy-done.4, s32[12,16,128]{2,1,0:T(8,128)S(1)} %copy-done.1, ...), custom_call_target="tpu_custom_call", output_to_operand_aliasing={{}: (0, {})} | custom-call | tf_op jit(solution)/shard_map/add_y_rows/pallas_call | solution.py:692
  14.4 0.3 %collective-permute-done.5.other = f32[16,128]{1,0:T(8,128)S(1)} collective-permute-done((f32[16,128]{1,0:T(8,128)S(1)}, f32[16,128]{1,0:T(8,128)S(1)}, u32[]{:S(2)}, u32[]{:S(2)}) %collective-permute-start.5) | collective-permute-done | bytes 8224 | tf_op jit(solution)/shard_map/ppermute | solution.py:82
  14.7 0.6 %add_depth.1 = f32[16,128]{1,0:T(8,128)} custom-call(f32[16,128]{1,0:T(8,128)S(1)} %add_y_faces.1.mine, f32[16,128]{1,0:T(8,128)S(1)} %collective-permute-done.5.other), custom_call_target="tpu_custom_call" | custom-call | tf_op jit(solution)/shard_map/add_depth/pallas_call | solution.py:692
Async XLA Ops:
  0.6 1.6 %copy-start = (f32[19,12,16,128]{3,2,1,0:T(8,128)S(1)}, f32[19,12,16,128]{3,2,1,0:T(8,128)}, u32[]{:S(2)}) copy-start(f32[19,12,16,128]{3,2,1,0:T(8,128)} %adjoint.5) | copy-start | bytes 5603332
  0.6 1.6 %copy-start.2 = (s32[12,16,128]{2,1,0:T(8,128)S(1)}, s32[12,16,128]{2,1,0:T(8,128)}, u32[]{:S(2)}) copy-start(s32[12,16,128]{2,1,0:T(8,128)} %port.5) | copy-start | bytes 294916
  0.7 1.5 %copy-start.1 = (s32[12,16,128]{2,1,0:T(8,128)S(1)}, s32[12,16,128]{2,1,0:T(8,128)}, u32[]{:S(2)}) copy-start(s32[12,16,128]{2,1,0:T(8,128)} %solid.5) | copy-start | bytes 294916
  0.7 1.5 %copy-start.4 = (f32[16,128]{1,0:T(8,128)S(1)}, f32[16,128]{1,0:T(8,128)}, u32[]{:S(2)}) copy-start(f32[16,128]{1,0:T(8,128)} %design.5) | copy-start | bytes 24580
  0.7 1.6 %copy-start.3 = (f32[3,12,16,128]{3,2,1,0:T(8,128)S(1)}, f32[3,12,16,128]{3,2,1,0:T(8,128)}, u32[]{:S(2)}) copy-start(f32[3,12,16,128]{3,2,1,0:T(8,128)} %momentum.1) | copy-start | bytes 884740
  1.6 1.4 %collective-permute-start = (f32[5,16,128]{2,1,0:T(8,128)S(1)}, f32[5,16,128]{2,1,0:T(8,128)S(1)}, u32[]{:S(2)}, u32[]{:S(2)}) collective-permute-start(f32[5,16,128]{2,1,0:T(8,128)S(1)} %depth_faces.1), channel_id=1, source_target_pairs={{0,1},{1,0},{2,3},{3,2},{4,5},{5,4},{6,7},{7,6},{8,9},{9,8},{10,11... | collective-permute-start | bytes 122888 | tf_op jit(solution)/shard_map/ppermute | solution.py:82
  3.1 5.9 %collective-permute-start.1 = (f32[24,128]{1,0:T(8,128)S(1)}, f32[24,128]{1,0:T(8,128)S(1)}, u32[]{:S(2)}, u32[]{:S(2)}) collective-permute-start(f32[24,128]{1,0:T(8,128)S(1)} %get-tuple-element.21.refs_3_), channel_id=1, source_target_pairs={{4,8},{5,9},{8,4},{9,5},{12,16},{13,17},{16,12},{17,13},{20,24},{2... | collective-permute-start | bytes 36872 | tf_op jit(solution)/shard_map/ppermute | solution.py:86
  3.6 5.7 %collective-permute-start.2 = (f32[24,128]{1,0:T(8,128)S(1)}, f32[24,128]{1,0:T(8,128)S(1)}, u32[]{:S(2)}, u32[]{:S(2)}) collective-permute-start(f32[24,128]{1,0:T(8,128)S(1)} %get-tuple-element.22.refs_2_), channel_id=1, source_target_pairs={{0,4},{4,0},{8,12},{12,8},{16,20},{20,16},{24,28},{28,24},{1,5},{5... | collective-permute-start | bytes 36872 | tf_op jit(solution)/shard_map/ppermute | solution.py:82
  7.6 5.6 %collective-permute-start.3 = (f32[136,128]{1,0:T(8,128)S(1)}, f32[136,128]{1,0:T(8,128)S(1)}, u32[]{:S(2)}, u32[]{:S(2)}) collective-permute-start(f32[136,128]{1,0:T(8,128)S(1)} %get-tuple-element.25.refs_1_), channel_id=1, source_target_pairs={{0,2},{2,0},{1,3},{3,1},{4,6},{6,4},{5,7},{7,5},{8,10},{10,8},{9,1... | collective-permute-start | bytes 208904 | tf_op jit(solution)/shard_map/ppermute | solution.py:82
  9.5 3.7 %collective-permute-start.4 = (f32[16,128]{1,0:T(8,128)S(1)}, f32[16,128]{1,0:T(8,128)S(1)}, u32[]{:S(2)}, u32[]{:S(2)}) collective-permute-start(f32[16,128]{1,0:T(8,128)S(1)} %get-tuple-element.27.refs_3_), channel_id=1, source_target_pairs={{0,2},{2,0},{1,3},{3,1},{4,6},{6,4},{5,7},{7,5},{8,10},{10,8},{9,1... | collective-permute-start | bytes 24584 | tf_op jit(solution)/shard_map/ppermute | solution.py:82
  13.5 1.2 %collective-permute-start.5 = (f32[16,128]{1,0:T(8,128)S(1)}, f32[16,128]{1,0:T(8,128)S(1)}, u32[]{:S(2)}, u32[]{:S(2)}) collective-permute-start(f32[16,128]{1,0:T(8,128)S(1)} %add_y_faces.1.mine), channel_id=1, source_target_pairs={{0,1},{1,0},{2,3},{3,2},{4,5},{5,4},{6,7},{7,6},{8,9},{9,8},{10,11... | collective-permute-start | bytes 24584 | tf_op jit(solution)/shard_map/ppermute | solution.py:82
